TPU v7x, 512 devices: a whole 4x4x16 slice. The times are simulated.
512 devices in a mesh: dp: 4 (over x), own: 128 (over z, y, core).
Axes of the slice: x: 4, y: 4, z: 16, core: 2. Of those that a mesh axis runs over, the one named last changes fastest.
Arguments:
- partial_grads: bfloat16 [4, 128, 512, 512], P('dp', None, 'own'), may hold values from -6 to 6
- owner_list: int32 [128], replicated, may hold values from 0 to 127, as said below
- left_stat: float32 [256, 512, 512], P('own', 'dp'), may hold values from -6 to 6
- right_stat: float32 [256, 512, 512], P('own', 'dp'), may hold values from -6 to 6
- left_root: bfloat16 [256, 512, 512], P('own', 'dp'), as said below
- right_root: bfloat16 [256, 512, 512], P('own', 'dp'), as said below
Outputs:
- new_left: float32 [256, 512, 512], P('own', 'dp')
- new_right: float32 [256, 512, 512], P('own', 'dp')
- update: bfloat16 [128, 512, 512], P(None, 'own', 'dp')
Inputs may be any that keep to these rules, and one draw needn't show every extreme that they name: `owner_list`: each owner is named by at most 2 blocks; a quarter of the owners are named by exactly 2 blocks, half by one, a quarter by none. `left_root`: each matrix is symmetric and positive definite. `right_root`: each matrix is symmetric and positive definite.
All inputs are finite; a program needn't handle non-finite values.
Results may differ from a plain program's by a relative error of at most 0.015.
Values may be sent and summed in bfloat16 or wider, within the bound.
No kernel may reach another device: no remote copies, remote signals or barrier semaphores. Data moves between devices by JAX's collectives and lax.ppermute only.
A program may use at most 64 MiB of HBM per device.

v0:
```python
import jax
import jax.numpy as jnp
from jax import lax
from jax.sharding import PartitionSpec as P

decay_rate = 0.95
epsilon = 1e-06


def body(partial_grads, owner_list, left_stat, right_stat, left_root, right_root):
    owners = lax.axis_size("own")
    capacity = left_stat.shape[0]
    quarter = left_stat.shape[1]
    block_width = left_stat.shape[2]
    blocks = owner_list.shape[0]
    owner_hits = (owner_list[:, None] == jnp.arange(owners, dtype=jnp.int32)[None, :]).astype(
        jnp.int32
    )
    before = jnp.cumsum(owner_hits, axis=0) - owner_hits
    slot_index = jnp.sum(before * owner_hits, axis=1)
    slot_hits = (slot_index[:, None] == jnp.arange(capacity, dtype=jnp.int32)[None, :]).astype(
        jnp.int32
    )
    slot_match = slot_hits[:, :, None] * owner_hits[:, None, :]
    source_block = jnp.sum(slot_match * jnp.arange(blocks, dtype=jnp.int32)[:, None, None], axis=0)
    filled_flag = jnp.sum(slot_match, axis=0).astype(jnp.bfloat16)
    local_terms = partial_grads[0].astype(jnp.float32)
    shared = lax.psum(local_terms.astype(jnp.bfloat16), "dp")
    outgoing = jnp.take(shared, source_block, axis=0) * filled_flag[:, :, None, None]
    arrived = lax.all_to_all(outgoing, "own", split_axis=1, concat_axis=1, tiled=True)
    grad_part = arrived.reshape(capacity, block_width, arrived.shape[3])
    dp_lane = lax.axis_index("dp")
    own_index = lax.axis_index("own")
    owner_load = jnp.sum((owner_list == own_index).astype(jnp.int32))
    slot_used = (jnp.arange(capacity, dtype=jnp.int32) < owner_load)[:, None, None]
    row_start = dp_lane * quarter
    grad_rows = lax.dynamic_slice_in_dim(grad_part, row_start, quarter, 1)
    grad_colq = lax.dynamic_slice_in_dim(grad_part, row_start, quarter, 2)
    left_gram = jnp.einsum("cqk,cnk->cqn", grad_rows, grad_part, preferred_element_type=jnp.float32)
    right_gram = jnp.einsum(
        "ckq,ckn->cqn", grad_colq, grad_part, preferred_element_type=jnp.float32
    )
    new_left = jnp.where(slot_used, decay_rate * left_stat + left_gram / block_width, left_stat)
    new_right = jnp.where(slot_used, decay_rate * right_stat + right_gram / block_width, right_stat)
    half_done = jnp.einsum(
        "ckn,cqn->ckq", grad_part, right_root, preferred_element_type=jnp.float32
    ).astype(jnp.bfloat16)
    product = jnp.einsum(
        "cpn,cpq->cnq",
        lax.all_gather(left_root, "dp", axis=1, tiled=True),
        half_done,
        preferred_element_type=jnp.float32,
    )
    grad_sq = jnp.sum(jnp.square(grad_part.astype(jnp.float32)), axis=(1, 2))
    prod_sq = lax.psum(jnp.sum(product * product, axis=(1, 2)), "dp")
    cell_count = float(block_width * block_width)
    graft_ratio = jnp.sqrt(grad_sq / cell_count) / jnp.sqrt(prod_sq / cell_count + epsilon)
    scaled = (product * graft_ratio[:, None, None]).astype(jnp.bfloat16)
    returned = lax.all_to_all(
        scaled.reshape(capacity, owners, block_width // owners, quarter),
        "own",
        split_axis=1,
        concat_axis=1,
        tiled=True,
    )
    gathered_back = returned.reshape(capacity * owners, block_width // owners, quarter)
    update = jnp.take(gathered_back, slot_index * owners + owner_list, axis=0)
    return (new_left, new_right, update)


def solution(mesh):
    in_specs = (
        P("dp", None, "own", None),
        P(),
        P("own", "dp", None),
        P("own", "dp", None),
        P("own", "dp", None),
        P("own", "dp", None),
    )
    out_specs = (P("own", "dp", None), P("own", "dp", None), P(None, "own", "dp"))
    return jax.shard_map(body, mesh=mesh, in_specs=in_specs, out_specs=out_specs, check_vma=False)
```

profile of v0, /device:TPU:1, one launch (start us, length us, event | category | flops | bytes accessed | tf_op | source)
XLA Modules:
  0.0 200.8 jit_solution(6066571486796467803)
XLA Ops:
  7.2 0.0 all-reduce.2.cloned.1.call-start
  7.2 0.7 all-reduce.2.cloned.1.call-update
  7.9 0.7 fusion.9
  8.7 0.2 reduce_window_sum.11
  8.8 0.8 select_reduce_fusion
  9.7 0.1 multiply_reduce_fusion.2
  9.8 62.1 %all-reduce.2.cloned.1.call-done = bf16[128,4,512]{2,1,0:T(4,128)(2,1)} async-done(((bf16[128,4,512]{2,1,0:T(4,128)(2,1)}), bf16[128,4,512]{2,1,0:T(4,128)(2,1)}) %all-reduce.2.cloned.1.call-update) | async-done | bytes 524304 | tf_op jit(solution)/shard_map/psum | solution.py:28
  71.9 2.6 %gather_fusion = bf16[256,4,512]{2,1,0:T(4,128)(2,1)S(1)} fusion(bf16[128,4,512]{2,1,0:T(4,128)(2,1)} %all-reduce.2.cloned.1.call-done, s32[1024]{0:T(1024)S(1)} %pad_clamp_fusion.1), kind=kCustom, calls=%fused_computation | custom fusion | bytes 2098176 | tf_op jit(solution)/shard_map/jit(_take)/gather | solution.py:29
  74.5 0.2 copy.38
  74.7 0.2 select_multiply_fusion
  74.9 1.8 copy.39
  76.7 18.8 %all-to-all-start = ((bf16[2,128,4,512]{3,2,0,1:T(4,128)(2,1)}), bf16[2,128,4,512]{3,2,0,1:T(4,128)(2,1)S(1)}, u32[]{:S(2)}, u32[]{:S(2)}) async-start(bf16[2,128,4,512]{3,2,0,1:T(4,128)(2,1)} %copy.39), calls=%async_computation | async-start | bytes 2097152 | tf_op jit(solution)/shard_map/all_to_all | solution.py:30
  95.5 0.0 all-gather.2.cloned.1.call-start
  95.6 0.7 all-gather.2.cloned.1.call-update
  96.3 51.1 %all-to-all-done = bf16[2,128,4,512]{3,2,0,1:T(4,128)(2,1)S(1)} async-done(((bf16[2,128,4,512]{3,2,0,1:T(4,128)(2,1)}), bf16[2,128,4,512]{3,2,0,1:T(4,128)(2,1)S(1)}, u32[]{:S(2)}, u32[]{:S(2)}) %all-to-all-start) | async-done | bytes 1048608 | tf_op jit(solution)/shard_map/all_to_all | solution.py:30
  147.4 0.4 copy.40
  147.7 0.3 reshape.85
  148.1 2.1 %multiply_reduce_fusion.1 = (f32[2]{0:T(128)S(1)}, f32[2,128,512]{2,1,0:T(8,128)S(1)}) fusion(bf16[2,512,512]{2,1,0:T(8,128)(2,1)} %all-gather.2.cloned.1.call-done, bf16[2,512,512]{2,1,0:T(8,128)(2,1)S(1)} %reshape.85, bf16[2,128,512]{2,1,0:T(8,128)(2,1)S(1)} %copy-done), kind=kOutput, calls=%fused_computation.13 | convolution fusion | flops 268828672 | bytes 2883592 | tf_op jit(solution)/shard_map/cpn,cpq->cnq/dot_general | solution.py:48
  150.2 7.4 %psum.15 = f32[2]{0:T(128)S(1)} all-reduce(f32[2]{0:T(128)S(1)} %get-tuple-element.7), channel_id=1, replica_groups=mesh['dp'=4,'own'=128] {'dp'}, use_global_device_ids=true, to_apply=%region_8.9 | all-reduce | flops 2 | bytes 16 | tf_op jit(solution)/shard_map/psum | solution.py:55
  157.6 0.7 multiply_reduce_fusion
  158.3 0.1 fusion.5
  158.4 0.2 copy.43
  158.6 0.8 copy.44
  159.4 12.2 %all-to-all-start.1 = ((bf16[2,128,4,128]{3,2,0,1:T(4,128)(2,1)}), bf16[2,128,4,128]{3,2,0,1:T(4,128)(2,1)S(1)}, u32[]{:S(2)}, u32[]{:S(2)}) async-start(bf16[2,128,4,128]{3,2,0,1:T(4,128)(2,1)} %copy.44), calls=%async_computation.1 | async-start | bytes 524288 | tf_op jit(solution)/shard_map/all_to_all | solution.py:59
  171.6 0.6 fusion.11
  172.2 0.6 iota_compare_fusion.1
  172.9 1.3 fusion.1
  174.2 1.1 fusion.3
  175.4 16.7 %all-to-all-done.1 = bf16[2,128,4,128]{3,2,0,1:T(4,128)(2,1)S(1)} async-done(((bf16[2,128,4,128]{3,2,0,1:T(4,128)(2,1)}), bf16[2,128,4,128]{3,2,0,1:T(4,128)(2,1)S(1)}, u32[]{:S(2)}, u32[]{:S(2)}) %all-to-all-start.1) | async-done | bytes 262176 | tf_op jit(solution)/shard_map/all_to_all | solution.py:59
  192.1 0.2 copy.46
  192.3 0.7 gather_fusion.1
  193.1 0.9 broadcast_select_fusion
  (18 shorter events, 0.1 us)
Async XLA Ops:
  7.2 140.9 %copy-start = (bf16[2,128,512]{2,1,0:T(8,128)(2,1)S(1)}, bf16[2,128,512]{2,1,0:T(8,128)(2,1)}, u32[]{:S(2)}) copy-start(bf16[2,128,512]{2,1,0:T(8,128)(2,1)} %param.11) | copy-start | bytes 786436
  7.2 64.7 %all-reduce.2.cloned.1.call-start = ((), (), s32[]{:S(2)}) async-start(), calls=%async_computation.2 | async-start | bytes 1048576 | tf_op jit(solution)/shard_map/psum | solution.py:28
  76.7 70.6 %all-to-all-start = ((bf16[2,128,4,512]{3,2,0,1:T(4,128)(2,1)}), bf16[2,128,4,512]{3,2,0,1:T(4,128)(2,1)S(1)}, u32[]{:S(2)}, u32[]{:S(2)}) async-start(bf16[2,128,4,512]{3,2,0,1:T(4,128)(2,1)} %copy.39), calls=%async_computation | async-start | bytes 2097152 | tf_op jit(solution)/shard_map/all_to_all | solution.py:30
  95.5 52.5 %all-gather.2.cloned.1.call-start = ((), (), s32[]{:S(2)}) async-start(), calls=%async_computation.3 | async-start | bytes 1310720 | tf_op jit(solution)/shard_map/all_gather | solution.py:50
  158.3 13.3 %copy-start.3 = (s32[128]{0:T(128)S(1)}, s32[128]{0:T(128)}, u32[]{:S(2)}) copy-start(s32[128]{0:T(128)} %param.7) | copy-start | bytes 1540
  158.3 14.6 %copy-start.1 = (f32[2,128,512]{2,1,0:T(8,128)S(1)}, f32[2,128,512]{2,1,0:T(8,128)}, u32[]{:S(2)}) copy-start(f32[2,128,512]{2,1,0:T(8,128)} %param.8) | copy-start | bytes 1572868
  159.4 32.7 %all-to-all-start.1 = ((bf16[2,128,4,128]{3,2,0,1:T(4,128)(2,1)}), bf16[2,128,4,128]{3,2,0,1:T(4,128)(2,1)S(1)}, u32[]{:S(2)}, u32[]{:S(2)}) async-start(bf16[2,128,4,128]{3,2,0,1:T(4,128)(2,1)} %copy.44), calls=%async_computation.1 | async-start | bytes 524288 | tf_op jit(solution)/shard_map/all_to_all | solution.py:59
  172.9 1.3 copy-start.2
Sparse Core Ops, SparseCore 0:
  10.4 61.5 all-reduce.1
  98.5 30.8 all-gather.1
where the time goes:
time: 202 us; the launch traced here: 201 us
  waiting for transfers between devices  131 us (65%)
  starting transfers between devices  31.1 us (15%)
  between operations  14.2 us (7%)
  blocking collectives  7.43 us (4%)
  local copies, waits for them, and re-layouts  7.25 us (4%)
  other arithmetic  5.02 us (2%)
  matrix products  4.51 us (2%)
    psum x1, waiting for transfers between devices, body(): shared = lax.psum(local_terms.astype(jnp.bfloat16), 'dp')  62.1 us
    all_to_all x1, waiting for transfers between devices, body(): lax.all_to_all(outgoing, 'own', split_axis=1, concat_axis=1, tiled=True)  51.1 us
    all_to_all x1, starting transfers between devices, body(): lax.all_to_all(outgoing, 'own', split_axis=1, concat_axis=1, tiled=True)  18.8 us
    all_to_all x1, waiting for transfers between devices, body(): lax.all_to_all(scaled.reshape(capacity, owners, block_width // owners, qu...  16.7 us
    all_to_all x1, starting transfers between devices, body(): lax.all_to_all(scaled.reshape(capacity, owners, block_width // owners, qu...  12.2 us
    psum x1, blocking collectives, body(): prod_sq = lax.psum(jnp.sum(product * product, axis=(1, 2)), 'dp')  7.43 us
  transfers between devices with their start and end apart: 4, of which 3 were waited for; matrix products, arithmetic and copies ran while one was open for 3% of the time, Pallas kernels for 0%

commit v1 on v0

v1 whole, which is shorter than its diff:
```python
import jax
import jax.numpy as jnp
from jax import lax
from jax.sharding import PartitionSpec as P

decay_rate = 0.95
epsilon = 1e-06


def spread(piece, lanes):
    copies = jnp.broadcast_to(piece[None], (lanes,) + piece.shape)
    return lax.all_to_all(copies, "dp", split_axis=0, concat_axis=0, tiled=True)


def body(partial_grads, owner_list, left_stat, right_stat, left_root, right_root):
    owners = lax.axis_size("own")
    lanes = lax.axis_size("dp")
    capacity, quarter, width = left_stat.shape
    blocks = owner_list.shape[0]
    rows = width // owners
    block_ids = jnp.arange(blocks, dtype=jnp.int32)

    terms = partial_grads[0].reshape(blocks, rows, lanes, quarter).transpose(2, 0, 1, 3)
    terms = lax.all_to_all(terms, "dp", split_axis=0, concat_axis=0, tiled=True)
    summed = jnp.sum(terms.astype(jnp.float32), axis=0).astype(jnp.bfloat16)

    same = (owner_list[:, None] == owner_list[None, :]) & (block_ids[None, :] < block_ids[:, None])
    slot_index = jnp.sum(same.astype(jnp.int32), axis=1)
    where_to = owner_list * capacity + slot_index
    cells = jnp.arange(owners * capacity, dtype=jnp.int32)
    match = where_to[None, :] == cells[:, None]
    source = jnp.sum(jnp.where(match, block_ids[None, :], 0), axis=1)
    filled = jnp.any(match, axis=1)

    picked = summed.at[source].get(mode="promise_in_bounds")
    outgoing = jnp.where(filled[:, None, None], picked, jnp.zeros_like(picked))
    outgoing = outgoing.reshape(owners, capacity, rows, quarter)
    arrived = lax.all_to_all(outgoing, "own", split_axis=0, concat_axis=0, tiled=True)
    mine = arrived.transpose(1, 0, 2, 3).reshape(capacity, width, quarter)

    left_all = spread(left_root, lanes)
    grads = spread(mine, lanes)
    grads = grads.transpose(1, 2, 0, 3).reshape(capacity, width, width)

    lane = lax.axis_index("dp")
    used = jnp.sum((owner_list == lax.axis_index("own")).astype(jnp.int32))
    slot_used = (jnp.arange(capacity, dtype=jnp.int32) < used)[:, None, None]

    half = jnp.einsum(
        "ckn,cqn->ckq", grads, right_root, preferred_element_type=jnp.float32
    ).astype(jnp.bfloat16)
    left_full = left_all.transpose(1, 0, 2, 3).reshape(capacity, width, width)
    product = jnp.einsum("cpn,cpq->cnq", left_full, half, preferred_element_type=jnp.float32)
    prod_part = jnp.sum(product * product, axis=(1, 2))
    prod_sq = jnp.sum(spread(prod_part, lanes), axis=0)

    grad_rows = lax.dynamic_slice_in_dim(grads, lane * quarter, quarter, 1)
    left_gram = jnp.einsum("cqk,cnk->cqn", grad_rows, grads, preferred_element_type=jnp.float32)
    right_gram = jnp.einsum("ckq,ckn->cqn", mine, grads, preferred_element_type=jnp.float32)
    new_left = jnp.where(slot_used, decay_rate * left_stat + left_gram / width, left_stat)
    new_right = jnp.where(slot_used, decay_rate * right_stat + right_gram / width, right_stat)

    grad_sq = jnp.sum(jnp.square(grads.astype(jnp.float32)), axis=(1, 2))
    cell_count = float(width * width)
    ratio = jnp.sqrt(grad_sq / cell_count) / jnp.sqrt(prod_sq / cell_count + epsilon)
    scaled = (product * ratio[:, None, None]).astype(jnp.bfloat16)
    scaled = scaled.reshape(capacity, owners, rows, quarter).transpose(1, 0, 2, 3)
    returned = lax.all_to_all(scaled, "own", split_axis=0, concat_axis=0, tiled=True)
    returned = returned.reshape(owners * capacity, rows, quarter)
    update = returned.at[where_to].get(mode="promise_in_bounds")
    return (new_left, new_right, update)


def solution(mesh):
    in_specs = (
        P("dp", None, "own", None),
        P(),
        P("own", "dp", None),
        P("own", "dp", None),
        P("own", "dp", None),
        P("own", "dp", None),
    )
    out_specs = (P("own", "dp", None), P("own", "dp", None), P(None, "own", "dp"))
    return jax.shard_map(body, mesh=mesh, in_specs=in_specs, out_specs=out_specs, check_vma=False)
```

time: 202 us -> 143 us (0.71)
  waiting for transfers between devices: 131 us -> 52.7 us
  blocking collectives: 7.43 us -> 42.8 us
  between operations: 14.2 us -> 0.81 us
  starting transfers between devices: 31.1 us -> 26.7 us
  local copies, waits for them, and re-layouts: 7.25 us -> 11.3 us
  other arithmetic: 5.02 us -> 2.88 us
    psum x1 -> x0, waiting for transfers between devices: 62.1 us -> none  [body(): shared = lax.psum(local_terms.astype(jnp.bfloat16), 'dp')]
    all_to_all x0 -> x1, blocking collectives: none -> 42.8 us  [body(): lax.all_to_all(outgoing, 'own', split_axis=0, concat_axis=0, tiled=True)]
    all_to_all x2 -> x5, waiting for transfers between devices: 67.8 us -> 52.7 us  [the longest x3 30.7 us: spread(): return lax.all_to_all(copies, 'dp', split_axis=0, concat_axis=0, tiled=True)]
    psum x1 -> x0, blocking collectives: 7.43 us -> none  [body(): prod_sq = lax.psum(jnp.sum(product * product, axis=(1, 2)), 'dp')]
    all_to_all x2 -> x5, starting transfers between devices: 31 us -> 26.7 us  [the longest x1 11.6 us: body(): lax.all_to_all(scaled, 'own', split_axis=0, concat_axis=0, tiled=True)]
    transpose x0 -> x4, local copies, waits for them, and re-layouts: none -> 3.07 us  [the longest x1 1.15 us: body(): left_full = left_all.transpose(1, 0, 2, 3).reshape(capacity, width, width)]
    broadcast_in_dim x0 -> x4, local copies, waits for them, and re-layouts: none -> 2.95 us  [the longest x3 2.79 us: spread(): copies = jnp.broadcast_to(piece[None], (lanes,) + piece.shape)]
    unnamed x8 -> x11, local copies, waits for them, and re-layouts: 0.03 us -> 2.44 us
  transfers between devices with their start and end apart: 4 -> 5, of which waited for: 3 -> 5; matrix products, arithmetic and copies ran while one was open for 3% -> 4% of each run, Pallas kernels for 0% -> 0%
where the time goes in v1:
time: 143 us; the launch traced here: 142 us
  waiting for transfers between devices  52.7 us (37%)
  blocking collectives  42.8 us (30%)
  starting transfers between devices  26.7 us (19%)
  local copies, waits for them, and re-layouts  11.3 us (8%)
  matrix products  4.5 us (3%)
  other arithmetic  2.88 us (2%)
    all_to_all x1, blocking collectives, body(): lax.all_to_all(outgoing, 'own', split_axis=0, concat_axis=0, tiled=True)  42.8 us
    all_to_all x3, waiting for transfers between devices, spread(): return lax.all_to_all(copies, 'dp', split_axis=0, concat_axis=0, tiled=True)  30.7 us
    all_to_all x1, waiting for transfers between devices, body(): lax.all_to_all(scaled, 'own', split_axis=0, concat_axis=0, tiled=True)  16.3 us
    all_to_all x1, starting transfers between devices, body(): lax.all_to_all(scaled, 'own', split_axis=0, concat_axis=0, tiled=True)  11.6 us
    all_to_all x3, starting transfers between devices, spread(): return lax.all_to_all(copies, 'dp', split_axis=0, concat_axis=0, tiled=True)  10.3 us
    all_to_all x1, waiting for transfers between devices, body(): terms = lax.all_to_all(terms, 'dp', split_axis=0, concat_axis=0, tiled=True)  5.69 us
    all_to_all x1, starting transfers between devices, body(): terms = lax.all_to_all(terms, 'dp', split_axis=0, concat_axis=0, tiled=True)  4.84 us
  transfers between devices with their start and end apart: 5, of which 5 were waited for; matrix products, arithmetic and copies ran while one was open for 4% of the time, Pallas kernels for 0%

profile of v1, /device:TPU:1, one launch (start us, length us, event | category | flops | bytes accessed | tf_op | source)
XLA Modules:
  0.0 141.8 jit_solution(552757476281664973)
XLA Ops:
  0.6 1.5 %copy.59 = bf16[1,128,4,512]{1,3,2,0:T(8,128)(2,1)S(1)} copy(bf16[1,128,4,512]{3,2,1,0:T(4,128)(2,1)} %param.6) | data formatting | bytes 1048576 | tf_op args[0]
  2.2 1.1 copy.60
  3.2 4.8 %all-to-all-start = ((bf16[4,128,4,128]{3,2,1,0:T(4,128)(2,1)}), bf16[4,128,4,128]{3,2,1,0:T(4,128)(2,1)S(1)}, u32[]{:S(2)}, u32[]{:S(2)}) async-start(bf16[4,128,4,128]{3,2,1,0:T(4,128)(2,1)} %copy.60), calls=%async_computation | async-start | bytes 1048576 | tf_op jit(solution)/shard_map/all_to_all | solution.py:24
  8.1 0.2 convert_reduce_fusion
  8.2 0.6 compare_select_fusion.1
  9.3 5.7 %all-to-all-done = bf16[4,128,4,128]{3,2,1,0:T(4,128)(2,1)S(1)} async-done(((bf16[4,128,4,128]{3,2,1,0:T(4,128)(2,1)}), bf16[4,128,4,128]{3,2,1,0:T(4,128)(2,1)S(1)}, u32[]{:S(2)}, u32[]{:S(2)}) %all-to-all-start) | async-done | bytes 524320 | tf_op jit(solution)/shard_map/all_to_all | solution.py:24
  15.0 0.3 reduce_sum.70
  15.3 1.0 gather_fusion
  16.4 0.3 broadcast_select_fusion
  16.7 0.2 copy.62
  16.9 42.8 %all_to_all.31 = bf16[128,2,4,128]{3,1,2,0:T(2,128)(2,1)S(1)} all-to-all(bf16[128,2,4,128]{3,1,2,0:T(2,128)(2,1)S(1)} %copy.62), channel_id=1, replica_groups=mesh['dp'=4,'own'=128] {'own'}, dimensions={0} | all-to-all | bytes 524288 | tf_op jit(solution)/shard_map/all_to_all | solution.py:38
  59.7 1.1 broadcast_in_dim.77
  60.8 3.5 %all-to-all-start.3 = ((bf16[4,2,128,512]{3,2,1,0:T(8,128)(2,1)}), bf16[4,2,128,512]{3,2,1,0:T(8,128)(2,1)S(1)}, u32[]{:S(2)}, u32[]{:S(2)}) async-start(bf16[4,2,128,512]{3,2,1,0:T(8,128)(2,1)} %broadcast_in_dim.77), calls=%async_computation.3 | async-start | bytes 2097152 | tf_op jit(solution)/shard_map/all_to_all | solution.py:12
  64.4 14.5 %all-to-all-done.3 = bf16[4,2,128,512]{3,2,1,0:T(8,128)(2,1)S(1)} async-done(((bf16[4,2,128,512]{3,2,1,0:T(8,128)(2,1)}), bf16[4,2,128,512]{3,2,1,0:T(8,128)(2,1)S(1)}, u32[]{:S(2)}, u32[]{:S(2)}) %all-to-all-start.3) | async-done | bytes 1048608 | tf_op jit(solution)/shard_map/all_to_all | solution.py:12
  78.9 1.1 broadcast_in_dim.76
  80.1 3.5 %all-to-all-start.2 = ((bf16[4,2,512,128]{3,2,1,0:T(8,128)(2,1)}), bf16[4,2,512,128]{3,2,1,0:T(8,128)(2,1)S(1)}, u32[]{:S(2)}, u32[]{:S(2)}) async-start(bf16[4,2,512,128]{3,2,1,0:T(8,128)(2,1)} %broadcast_in_dim.76), calls=%async_computation.2 | async-start | bytes 2097152 | tf_op jit(solution)/shard_map/all_to_all | solution.py:12
  83.6 1.1 copy.66
  84.7 12.5 %all-to-all-done.2 = bf16[4,2,512,128]{3,2,1,0:T(8,128)(2,1)S(1)} async-done(((bf16[4,2,512,128]{3,2,1,0:T(8,128)(2,1)}), bf16[4,2,512,128]{3,2,1,0:T(8,128)(2,1)S(1)}, u32[]{:S(2)}, u32[]{:S(2)}) %all-to-all-start.2) | async-done | bytes 1048608 | tf_op jit(solution)/shard_map/all_to_all | solution.py:12
  97.3 2.1 %multiply_reduce_fusion.1 = (f32[2]{0:T(128)S(1)}, f32[2,128,512]{2,1,0:T(8,128)S(1)}) fusion(bf16[2,512,512]{2,1,0:T(8,128)(2,1)} %bitcast.43, bf16[2,128,512]{2,1,0:T(8,128)(2,1)S(1)} %copy-done, bf16[4,2,512,128]{3,2,1,0:T(8,128)(2,1)S(1)} %all-to-all-done.2), kind=kOutput, calls=%fused_computation.13 | convolution fusion | flops 268828672 | bytes 2883592 | tf_op jit(solution)/shard_map/cpn,cpq->cnq/dot_general | solution.py:53
  99.4 0.6 broadcast_in_dim.78
  100.0 3.2 %all-to-all-start.4 = ((f32[4,1,2]{2,1,0:T(1,128)}), f32[4,1,2]{2,1,0:T(1,128)S(1)}, u32[]{:S(2)}, u32[]{:S(2)}) async-start(f32[4,1,2]{2,1,0:T(1,128)} %broadcast_in_dim.78), calls=%async_computation.4 | async-start | bytes 4096 | tf_op jit(solution)/shard_map/all_to_all | solution.py:12
  103.2 0.4 multiply_reduce_fusion
  103.6 3.6 %all-to-all-done.4 = f32[4,1,2]{2,1,0:T(1,128)S(1)} async-done(((f32[4,1,2]{2,1,0:T(1,128)}), f32[4,1,2]{2,1,0:T(1,128)S(1)}, u32[]{:S(2)}, u32[]{:S(2)}) %all-to-all-start.4) | async-done | bytes 64 | tf_op jit(solution)/shard_map/all_to_all | solution.py:12
  107.3 0.2 copy.69
  107.5 0.8 copy.70
  108.3 11.6 %all-to-all-start.5 = ((bf16[128,2,4,128]{3,2,1,0:T(4,128)(2,1)}), bf16[128,2,4,128]{3,2,1,0:T(4,128)(2,1)S(1)}, u32[]{:S(2)}, u32[]{:S(2)}) async-start(bf16[128,2,4,128]{3,2,1,0:T(4,128)(2,1)} %copy.70), calls=%async_computation.5 | async-start | bytes 524288 | tf_op jit(solution)/shard_map/all_to_all | solution.py:68
  119.9 0.7 iota_compare_fusion.2
  120.7 0.9 copy-done.2
  121.6 1.3 fusion.1
  122.9 1.1 fusion.3
  124.0 16.3 %all-to-all-done.5 = bf16[128,2,4,128]{3,2,1,0:T(4,128)(2,1)S(1)} async-done(((bf16[128,2,4,128]{3,2,1,0:T(4,128)(2,1)}), bf16[128,2,4,128]{3,2,1,0:T(4,128)(2,1)S(1)}, u32[]{:S(2)}, u32[]{:S(2)}) %all-to-all-start.5) | async-done | bytes 262176 | tf_op jit(solution)/shard_map/all_to_all | solution.py:68
  140.4 1.4 gather_fusion.1
  (21 shorter events, 0.8 us)
Async XLA Ops:
  0.6 96.7 %copy-start = (bf16[2,128,512]{2,1,0:T(8,128)(2,1)S(1)}, bf16[2,128,512]{2,1,0:T(8,128)(2,1)}, u32[]{:S(2)}) copy-start(bf16[2,128,512]{2,1,0:T(8,128)(2,1)} %param.11) | copy-start | bytes 786436
  2.1 5.9 %copy-start.4 = (s32[128]{0:T(128)S(1)}, s32[128]{0:T(128)}, u32[]{:S(2)}) copy-start(s32[128]{0:T(128)} %param.7) | copy-start | bytes 1540
  3.2 11.8 %all-to-all-start = ((bf16[4,128,4,128]{3,2,1,0:T(4,128)(2,1)}), bf16[4,128,4,128]{3,2,1,0:T(4,128)(2,1)S(1)}, u32[]{:S(2)}, u32[]{:S(2)}) async-start(bf16[4,128,4,128]{3,2,1,0:T(4,128)(2,1)} %copy.60), calls=%async_computation | async-start | bytes 1048576 | tf_op jit(solution)/shard_map/all_to_all | solution.py:24
  16.3 43.4 %copy-start.3 = (bf16[2,128,512]{2,1,0:T(8,128)(2,1)S(1)}, bf16[2,128,512]{2,1,0:T(8,128)(2,1)}, u32[]{:S(2)}) copy-start(bf16[2,128,512]{2,1,0:T(8,128)(2,1)} %param.10) | copy-start | bytes 786436
  60.8 18.1 %all-to-all-start.3 = ((bf16[4,2,128,512]{3,2,1,0:T(8,128)(2,1)}), bf16[4,2,128,512]{3,2,1,0:T(8,128)(2,1)S(1)}, u32[]{:S(2)}, u32[]{:S(2)}) async-start(bf16[4,2,128,512]{3,2,1,0:T(8,128)(2,1)} %broadcast_in_dim.77), calls=%async_computation.3 | async-start | bytes 2097152 | tf_op jit(solution)/shard_map/all_to_all | solution.py:12
  80.1 17.2 %all-to-all-start.2 = ((bf16[4,2,512,128]{3,2,1,0:T(8,128)(2,1)}), bf16[4,2,512,128]{3,2,1,0:T(8,128)(2,1)S(1)}, u32[]{:S(2)}, u32[]{:S(2)}) async-start(bf16[4,2,512,128]{3,2,1,0:T(8,128)(2,1)} %broadcast_in_dim.76), calls=%async_computation.2 | async-start | bytes 2097152 | tf_op jit(solution)/shard_map/all_to_all | solution.py:12
  100.0 7.2 %all-to-all-start.4 = ((f32[4,1,2]{2,1,0:T(1,128)}), f32[4,1,2]{2,1,0:T(1,128)S(1)}, u32[]{:S(2)}, u32[]{:S(2)}) async-start(f32[4,1,2]{2,1,0:T(1,128)} %broadcast_in_dim.78), calls=%async_computation.4 | async-start | bytes 4096 | tf_op jit(solution)/shard_map/all_to_all | solution.py:12
  108.3 32.1 %all-to-all-start.5 = ((bf16[128,2,4,128]{3,2,1,0:T(4,128)(2,1)}), bf16[128,2,4,128]{3,2,1,0:T(4,128)(2,1)S(1)}, u32[]{:S(2)}, u32[]{:S(2)}) async-start(bf16[128,2,4,128]{3,2,1,0:T(4,128)(2,1)} %copy.70), calls=%async_computation.5 | async-start | bytes 524288 | tf_op jit(solution)/shard_map/all_to_all | solution.py:68
  120.6 1.0 copy-start.2
  121.6 1.3 copy-start.1

commit v2 on v1

v2 whole, which is shorter than its diff:
```python
import jax
import jax.numpy as jnp
from jax import lax
from jax.experimental import pallas as pl
from jax.experimental.pallas import tpu as pltpu
from jax.sharding import PartitionSpec as P

decay_rate = 0.95
epsilon = 1e-06

VMEM = pl.BlockSpec(memory_space=pltpu.VMEM)
SMEM = pl.BlockSpec(memory_space=pltpu.SMEM)
ANY = pl.BlockSpec(memory_space=pl.ANY)
PARAMS = pltpu.CompilerParams(vmem_limit_bytes=40 * 1024 * 1024)

LANE_ORDER = (2, 3, 0, 1)
OWN_SHIFT = 80


def split_columns(x_ref, out_ref):
    quarter = out_ref.shape[3]
    for place in range(out_ref.shape[0]):
        lane = LANE_ORDER[place]
        out_ref[place] = x_ref[:, :, lane * quarter : (lane + 1) * quarter]


def sum_and_place(place_ref, terms_ref, out_ref):
    out_ref[...] = jnp.zeros_like(out_ref)

    def step(block, carry):
        total = terms_ref[0, block].astype(jnp.float32)
        for term in range(1, terms_ref.shape[0]):
            total += terms_ref[term, block].astype(jnp.float32)
        out_ref[place_ref[block]] = total.astype(out_ref.dtype)
        return carry

    lax.fori_loop(0, terms_ref.shape[1], step, 0, unroll=8)


def take_cells(place_ref, cells_ref, out_ref):
    def step(block, carry):
        out_ref[block] = cells_ref[place_ref[block]]
        return carry

    lax.fori_loop(0, out_ref.shape[0], step, 0, unroll=8)


def precondition(
    lane_ref, g0, g1, g2, g3, right_hbm, l0, l1, l2, l3,
    grads_ref, product_ref, squares_ref, part_ref,
    pieces, right, lefts, g_sems, r_sem, l_sems,
):
    lane = lane_ref[0]
    g_copies = [
        pltpu.make_async_copy(src, pieces.at[s], g_sems.at[s]) for s, src in enumerate((g0, g1, g2, g3))
    ]
    r_copy = pltpu.make_async_copy(right_hbm, right, r_sem)
    l_copies = [
        pltpu.make_async_copy(src, lefts.at[s], l_sems.at[s]) for s, src in enumerate((l0, l1, l2, l3))
    ]
    for copy in g_copies + [r_copy] + l_copies:
        copy.start()

    slots, width, _ = grads_ref.shape
    quarter = right.shape[1]
    pairs = pieces.shape[1]
    cut = pairs - OWN_SHIFT // 2
    upper = lax.broadcasted_iota(jnp.int32, (pairs, 8, quarter), 1) < 4
    squares = [jnp.zeros((1, quarter), jnp.float32) for _ in range(slots)]
    for s in range(4):
        g_copies[s].wait()
        first = pieces[s, :, 0].astype(jnp.float32)
        second = pieces[s, :, 1].astype(jnp.float32)
        slot0 = jnp.where(upper, first, pltpu.roll(second, 4, 1))
        slot1 = jnp.where(upper, pltpu.roll(first, 4, 1), second)
        column = pl.multiple_of(lax.rem(lane + (4 - s), 4) * quarter, quarter)
        for c, value in enumerate((slot0, slot1)):
            squares[c] += jnp.sum(value * value, axis=(0, 1))[None]
            flat = value.reshape(width, quarter).astype(jnp.bfloat16)
            grads_ref[c, pl.ds(0, width - cut * 8), pl.ds(column, quarter)] = flat[cut * 8 :]
            grads_ref[c, pl.ds(width - cut * 8, cut * 8), pl.ds(column, quarter)] = flat[: cut * 8]
    r_copy.wait()
    halves = []
    for c in range(slots):
        half = lax.dot_general(
            grads_ref[c], right[c], (((1,), (1,)), ((), ())), preferred_element_type=jnp.float32
        )
        halves.append(half.astype(jnp.bfloat16))
    parts = [jnp.zeros((1, quarter), jnp.float32) for _ in range(slots)]
    for s in range(4):
        l_copies[s].wait()
        row = pl.multiple_of(lax.rem(lane + (4 - s), 4) * quarter, quarter)
        for c in range(slots):
            block = jnp.dot(lefts[s, c], halves[c], preferred_element_type=jnp.float32)
            product_ref[c, pl.ds(row, quarter)] = block
            parts[c] += jnp.sum(block * block, axis=0, keepdims=True)
    squares_ref[...] = jnp.zeros_like(squares_ref)
    part_ref[...] = jnp.zeros_like(part_ref)
    for c in range(slots):
        squares_ref[pl.ds(c, 1)] = jnp.broadcast_to(
            jnp.sum(squares[c], axis=1, keepdims=True), (1, quarter)
        )
        total = jnp.broadcast_to(jnp.sum(parts[c], axis=1, keepdims=True), (1, quarter))
        for place in range(part_ref.shape[0]):
            part_ref[place, pl.ds(c, 1)] = total


def graft(product_ref, squares_ref, parts_ref, out_ref):
    pairs, _, _, quarter = out_ref.shape
    width = product_ref.shape[1]
    cells = float(width * width)
    cut = OWN_SHIFT // 2
    scaled = []
    for c in range(2):
        grad_sq = squares_ref[pl.ds(c, 1)]
        prod_sq = sum(parts_ref[k, pl.ds(c, 1)] for k in range(parts_ref.shape[0]))
        ratio = jnp.sqrt(grad_sq / cells) / jnp.sqrt(prod_sq / cells + epsilon)
        scaled.append((product_ref[c] * ratio).reshape(pairs, 8, quarter))
    upper = lax.broadcasted_iota(jnp.int32, (pairs, 8, quarter), 1) < 4
    first = jnp.where(upper, scaled[0], pltpu.roll(scaled[1], 4, 1)).astype(out_ref.dtype)
    second = jnp.where(upper, pltpu.roll(scaled[0], 4, 1), scaled[1]).astype(out_ref.dtype)
    for member, value in enumerate((first, second)):
        out_ref[pl.ds(0, pairs - cut), member] = value[cut:]
        out_ref[pl.ds(pairs - cut, cut), member] = value[:cut]


def lane_shift(x, step, lanes):
    return lax.ppermute(x, "dp", [(i, (i + step) % lanes) for i in range(lanes)])


def body(partial_grads, owner_list, left_stat, right_stat, left_root, right_root):
    owners = lax.axis_size("own")
    lanes = lax.axis_size("dp")
    capacity, quarter, width = left_stat.shape
    blocks = owner_list.shape[0]
    rows = width // owners
    block_ids = jnp.arange(blocks, dtype=jnp.int32)
    lane = lax.axis_index("dp")
    lane_groups = [list(LANE_ORDER)]
    own_groups = [[(i + OWN_SHIFT) % owners for i in range(owners)]]

    terms = pl.pallas_call(
        split_columns,
        out_shape=jax.ShapeDtypeStruct((lanes, blocks, rows, quarter), jnp.bfloat16),
        in_specs=[VMEM],
        out_specs=VMEM,
        compiler_params=PARAMS,
        name="split_columns",
    )(partial_grads[0])
    terms = lax.all_to_all(
        terms, "dp", split_axis=0, concat_axis=0, tiled=True, axis_index_groups=lane_groups
    )

    same = (owner_list[:, None] == owner_list[None, :]) & (block_ids[None, :] < block_ids[:, None])
    slot_index = jnp.sum(same.astype(jnp.int32), axis=1)
    place = lax.rem(owner_list + (owners - OWN_SHIFT), owners) * capacity + slot_index

    outgoing = pl.pallas_call(
        sum_and_place,
        out_shape=jax.ShapeDtypeStruct((owners * capacity, rows, quarter), jnp.bfloat16),
        in_specs=[SMEM, VMEM],
        out_specs=VMEM,
        compiler_params=PARAMS,
        name="sum_and_place",
    )(place, terms)
    outgoing = outgoing.reshape(owners, capacity * rows, quarter)
    left_mine, outgoing = lax.optimization_barrier((left_root, outgoing))
    arrived = lax.all_to_all(
        outgoing, "own", split_axis=0, concat_axis=0, tiled=True, axis_index_groups=own_groups
    )
    lefts = [left_mine] + [lane_shift(left_mine, s, lanes) for s in range(1, lanes)]

    arrived = arrived.reshape(owners // 2, 2, capacity * rows, quarter)
    pieces = [arrived] + [lane_shift(arrived, s, lanes) for s in range(1, lanes)]
    grads, product, squares, part = pl.pallas_call(
        precondition,
        out_shape=(
            jax.ShapeDtypeStruct((capacity, width, width), jnp.bfloat16),
            jax.ShapeDtypeStruct((capacity, width, quarter), jnp.float32),
            jax.ShapeDtypeStruct((8, quarter), jnp.float32),
            jax.ShapeDtypeStruct((lanes, 8, quarter), jnp.float32),
        ),
        in_specs=[SMEM] + [ANY] * 9,
        out_specs=(VMEM, VMEM, VMEM, VMEM),
        scratch_shapes=[
            pltpu.VMEM((lanes, owners // 2, 2, capacity * rows, quarter), jnp.bfloat16),
            pltpu.VMEM((capacity, quarter, width), jnp.bfloat16),
            pltpu.VMEM((lanes, capacity, quarter, width), jnp.bfloat16),
            pltpu.SemaphoreType.DMA((lanes,)),
            pltpu.SemaphoreType.DMA,
            pltpu.SemaphoreType.DMA((lanes,)),
        ],
        compiler_params=PARAMS,
        name="precondition",
    )(lane.reshape(1), *pieces, right_root, *lefts)
    parts = lax.all_to_all(
        part, "dp", split_axis=0, concat_axis=0, tiled=True, axis_index_groups=lane_groups
    )
    scaled = pl.pallas_call(
        graft,
        out_shape=jax.ShapeDtypeStruct((owners // 2, 2, capacity * rows, quarter), jnp.bfloat16),
        in_specs=[VMEM, VMEM, VMEM],
        out_specs=VMEM,
        compiler_params=PARAMS,
        name="graft",
    )(product, squares, parts)
    scaled = scaled.reshape(owners, capacity * rows, quarter)
    grads, scaled = lax.optimization_barrier((grads, scaled))
    returned = lax.all_to_all(
        scaled, "own", split_axis=0, concat_axis=0, tiled=True, axis_index_groups=own_groups
    )

    used = jnp.sum((owner_list == lax.axis_index("own")).astype(jnp.int32))
    slot_used = (jnp.arange(capacity, dtype=jnp.int32) < used)[:, None, None]
    grad_rows = lax.dynamic_slice_in_dim(grads, lane * quarter, quarter, 1)
    grad_cols = lax.dynamic_slice_in_dim(grads, lane * quarter, quarter, 2)
    left_gram = jnp.einsum("cqk,cnk->cqn", grad_rows, grads, preferred_element_type=jnp.float32)
    right_gram = jnp.einsum("ckq,ckn->cqn", grad_cols, grads, preferred_element_type=jnp.float32)
    new_left = jnp.where(slot_used, decay_rate * left_stat + left_gram / width, left_stat)
    new_right = jnp.where(slot_used, decay_rate * right_stat + right_gram / width, right_stat)

    update = pl.pallas_call(
        take_cells,
        out_shape=jax.ShapeDtypeStruct((blocks, rows, quarter), jnp.bfloat16),
        in_specs=[SMEM, VMEM],
        out_specs=VMEM,
        compiler_params=PARAMS,
        name="take_cells",
    )(place, returned.reshape(owners * capacity, rows, quarter))
    return (new_left, new_right, update)


def solution(mesh):
    in_specs = (
        P("dp", None, "own", None),
        P(),
        P("own", "dp", None),
        P("own", "dp", None),
        P("own", "dp", None),
        P("own", "dp", None),
    )
    out_specs = (P("own", "dp", None), P("own", "dp", None), P(None, "own", "dp"))
    return jax.shard_map(body, mesh=mesh, in_specs=in_specs, out_specs=out_specs, check_vma=False)
```

time: 143 us -> 117 us (0.82)
  starting transfers between devices: 26.7 us -> 66.7 us
  blocking collectives: 42.8 us -> 7.78 us
  waiting for transfers between devices: 52.7 us -> 28.2 us
  local copies, waits for them, and re-layouts: 11.3 us -> 1.71 us
  Pallas kernels: 0 us -> 7.06 us
  matrix products: 4.5 us -> 2.43 us
    all_to_all x1, blocking collectives: 42.8 us -> 7.78 us  [body(): lax.all_to_all(part, 'dp', split_axis=0, concat_axis=0, tiled=True, axis_...]
    all_to_all x5 -> x3, waiting for transfers between devices: 52.7 us -> 20.7 us  [the longest x1 12.7 us: body(): lax.all_to_all(scaled, 'own', split_axis=0, concat_axis=0, tiled=True, ax...]
    ppermute x0 -> x6, starting transfers between devices: none -> 21 us  [lane_shift(): lax.ppermute(x, 'dp', [(i, (i + step) % lanes) for i in range(lanes)])]
    all_to_all x5 -> x3, starting transfers between devices: 26.7 us -> 45.8 us  [the longest x1 24.5 us: body(): lax.all_to_all(outgoing, 'own', split_axis=0, concat_axis=0, tiled=True,...]
    ppermute x0 -> x6, waiting for transfers between devices: none -> 7.54 us  [lane_shift(): lax.ppermute(x, 'dp', [(i, (i + step) % lanes) for i in range(lanes)])]
    pallas_call x0 -> x5, Pallas kernels: none -> 7.06 us  [the longest x1 2.3 us: body(): pl.pallas_call(precondition, out_shape=(jax.ShapeDtypeStruct((capacity, w...]
    transpose x4 -> x0, local copies, waits for them, and re-layouts: 3.07 us -> none  [the longest x1 1.15 us: body(): left_full = left_all.transpose(1, 0, 2, 3).reshape(capacity, width, width)]
    broadcast_in_dim x4 -> x0, local copies, waits for them, and re-layouts: 2.95 us -> none  [the longest x3 2.79 us: spread(): copies = jnp.broadcast_to(piece[None], (lanes,) + piece.shape)]
  transfers between devices with their start and end apart: 5 -> 9, of which waited for: 5 -> 5; matrix products, arithmetic and copies ran while one was open for 4% -> 3% of each run, Pallas kernels for 0% -> 0%
where the time goes in v2:
time: 117 us; the launch traced here: 116 us
  starting transfers between devices  66.7 us (57%)
  waiting for transfers between devices  28.2 us (24%)
  blocking collectives  7.78 us (7%)
  Pallas kernels  7.06 us (6%)
  matrix products  2.43 us (2%)
  local copies, waits for them, and re-layouts  1.71 us (1%)
  other arithmetic  1.46 us (1%)
    all_to_all x1, starting transfers between devices, body(): lax.all_to_all(outgoing, 'own', split_axis=0, concat_axis=0, tiled=True,...  24.5 us
    ppermute x6, starting transfers between devices, lane_shift(): lax.ppermute(x, 'dp', [(i, (i + step) % lanes) for i in range(lanes)])  21 us
    all_to_all x1, starting transfers between devices, body(): lax.all_to_all(scaled, 'own', split_axis=0, concat_axis=0, tiled=True, ax...  14.3 us
    all_to_all x1, waiting for transfers between devices, body(): lax.all_to_all(scaled, 'own', split_axis=0, concat_axis=0, tiled=True, ax...  12.7 us
    all_to_all x1, blocking collectives, body(): lax.all_to_all(part, 'dp', split_axis=0, concat_axis=0, tiled=True, axis_...  7.78 us
    ppermute x6, waiting for transfers between devices, lane_shift(): lax.ppermute(x, 'dp', [(i, (i + step) % lanes) for i in range(lanes)])  7.54 us
    all_to_all x1, starting transfers between devices, body(): lax.all_to_all(terms, 'dp', split_axis=0, concat_axis=0, tiled=True, axis...  7.01 us
    all_to_all x1, waiting for transfers between devices, body(): lax.all_to_all(outgoing, 'own', split_axis=0, concat_axis=0, tiled=True,...  5.25 us
  transfers between devices with their start and end apart: 9, of which 5 were waited for; matrix products, arithmetic and copies ran while one was open for 3% of the time, Pallas kernels for 0%

profile of v2, /device:TPU:1, one launch (start us, length us, event | category | flops | bytes accessed | tf_op | source)
XLA Modules:
  0.0 116.2 jit_solution(1487023173553875151)
XLA Ops:
  0.6 1.0 copy-done
  1.7 1.0 split_columns.1
  2.6 7.0 %all-to-all-start = ((bf16[4,128,4,128]{3,2,1,0:T(4,128)(2,1)}), bf16[4,128,4,128]{3,2,1,0:T(4,128)(2,1)S(1)}, u32[]{:S(2)}, u32[]{:S(2)}) async-start(bf16[4,128,4,128]{3,2,1,0:T(4,128)(2,1)} %split_columns.1), calls=%async_computation | async-start | bytes 1048576 | tf_op jit(solution)/shard_map/all_to_all | solution.py:150
  9.7 0.7 copy-done.5
  10.3 0.2 convert_reduce_fusion
  10.5 0.6 fusion.7
  11.1 2.8 %all-to-all-done.terms_ref = bf16[4,128,4,128]{3,2,1,0:T(4,128)(2,1)S(1)} async-done(((bf16[4,128,4,128]{3,2,1,0:T(4,128)(2,1)}), bf16[4,128,4,128]{3,2,1,0:T(4,128)(2,1)S(1)}, u32[]{:S(2)}, u32[]{:S(2)}) %all-to-all-start) | async-done | bytes 524320 | tf_op jit(solution)/shard_map/all_to_all | solution.py:150
  13.9 1.6 %sum_and_place.1 = bf16[256,4,128]{2,1,0:T(4,128)(2,1)} custom-call(s32[128]{0:T(128)S(1)} %get-tuple-element.20.place_ref, bf16[4,128,4,128]{3,2,1,0:T(4,128)(2,1)S(1)} %all-to-all-done.terms_ref), custom_call_target="tpu_custom_call" | custom-call | tf_op jit(solution)/shard_map/sum_and_place/pallas_call | solution.py:158
  15.5 24.5 %all-to-all-start.1 = ((bf16[128,8,128]{2,1,0:T(8,128)(2,1)}), bf16[128,8,128]{2,1,0:T(8,128)(2,1)S(1)}, u32[]{:S(2)}, u32[]{:S(2)}) async-start(bf16[128,8,128]{2,1,0:T(8,128)(2,1)} %bitcast.2), calls=%async_computation.1 | async-start | bytes 524288 | tf_op jit(solution)/shard_map/all_to_all | solution.py:168
  40.0 2.5 %collective-permute-start.3 = (bf16[2,128,512]{2,1,0:T(8,128)(2,1)S(1)}, bf16[2,128,512]{2,1,0:T(8,128)(2,1)S(1)}, u32[]{:S(2)}, u32[]{:S(2)}) collective-permute-start(bf16[2,128,512]{2,1,0:T(8,128)(2,1)S(1)} %copy-done.2), channel_id=1, source_target_pairs={{0,128},{128,256},{256,384},{384,0},{1,129},{129,257},{257,385},{3... | collective-permute-start | bytes 786440 | tf_op jit(solution)/shard_map/ppermute | solution.py:128
  42.5 4.9 %collective-permute-start.4 = (bf16[2,128,512]{2,1,0:T(8,128)(2,1)S(1)}, bf16[2,128,512]{2,1,0:T(8,128)(2,1)S(1)}, u32[]{:S(2)}, u32[]{:S(2)}) collective-permute-start(bf16[2,128,512]{2,1,0:T(8,128)(2,1)S(1)} %copy-done.2), channel_id=1, source_target_pairs={{0,256},{128,384},{256,0},{384,128},{1,257},{129,385},{257,1},{385... | collective-permute-start | bytes 786440 | tf_op jit(solution)/shard_map/ppermute | solution.py:128
  47.4 3.1 %collective-permute-start.5 = (bf16[2,128,512]{2,1,0:T(8,128)(2,1)S(1)}, bf16[2,128,512]{2,1,0:T(8,128)(2,1)S(1)}, u32[]{:S(2)}, u32[]{:S(2)}) collective-permute-start(bf16[2,128,512]{2,1,0:T(8,128)(2,1)S(1)} %copy-done.2), channel_id=1, source_target_pairs={{0,384},{128,0},{256,128},{384,256},{1,385},{129,1},{257,129},{385... | collective-permute-start | bytes 786440 | tf_op jit(solution)/shard_map/ppermute | solution.py:128
  50.5 5.2 %all-to-all-done.1 = bf16[128,8,128]{2,1,0:T(8,128)(2,1)S(1)} async-done(((bf16[128,8,128]{2,1,0:T(8,128)(2,1)}), bf16[128,8,128]{2,1,0:T(8,128)(2,1)S(1)}, u32[]{:S(2)}, u32[]{:S(2)}) %all-to-all-start.1) | async-done | bytes 262176 | tf_op jit(solution)/shard_map/all_to_all | solution.py:168
  55.7 2.5 %collective-permute-start = (bf16[64,2,8,128]{3,2,1,0:T(8,128)(2,1)S(1)}, bf16[64,2,8,128]{3,2,1,0:T(8,128)(2,1)S(1)}, u32[]{:S(2)}, u32[]{:S(2)}) collective-permute-start(bf16[64,2,8,128]{3,2,1,0:T(8,128)(2,1)S(1)} %bitcast.8), channel_id=1, source_target_pairs={{0,128},{128,256},{256,384},{384,0},{1,129},{129,257},{257,385},{3... | collective-permute-start | bytes 786440 | tf_op jit(solution)/shard_map/ppermute | solution.py:128
  58.2 4.9 %collective-permute-start.1 = (bf16[64,2,8,128]{3,2,1,0:T(8,128)(2,1)S(1)}, bf16[64,2,8,128]{3,2,1,0:T(8,128)(2,1)S(1)}, u32[]{:S(2)}, u32[]{:S(2)}) collective-permute-start(bf16[64,2,8,128]{3,2,1,0:T(8,128)(2,1)S(1)} %bitcast.9), channel_id=1, source_target_pairs={{0,256},{128,384},{256,0},{384,128},{1,257},{129,385},{257,1},{385... | collective-permute-start | bytes 786440 | tf_op jit(solution)/shard_map/ppermute | solution.py:128
  63.1 0.0 collective-permute-done.3.l1
  63.2 3.1 %collective-permute-start.2 = (bf16[64,2,8,128]{3,2,1,0:T(8,128)(2,1)S(1)}, bf16[64,2,8,128]{3,2,1,0:T(8,128)(2,1)S(1)}, u32[]{:S(2)}, u32[]{:S(2)}) collective-permute-start(bf16[64,2,8,128]{3,2,1,0:T(8,128)(2,1)S(1)} %bitcast.10), channel_id=1, source_target_pairs={{0,384},{128,0},{256,128},{384,256},{1,385},{129,1},{257,129},{385... | collective-permute-start | bytes 786440 | tf_op jit(solution)/shard_map/ppermute | solution.py:128
  66.3 0.0 collective-permute-done.4.l2
  66.3 0.0 collective-permute-done.5.l3
  66.3 0.0 collective-permute-done.g1
  66.3 6.3 %collective-permute-done.1.g2 = bf16[64,2,8,128]{3,2,1,0:T(8,128)(2,1)S(1)} collective-permute-done((bf16[64,2,8,128]{3,2,1,0:T(8,128)(2,1)S(1)}, bf16[64,2,8,128]{3,2,1,0:T(8,128)(2,1)S(1)}, u32[]{:S(2)}, u32[]{:S(2)}) %collective-permute-start.1) | collective-permute-done | bytes 262176 | tf_op jit(solution)/shard_map/ppermute | solution.py:128
  72.6 1.3 %collective-permute-done.2.g3 = bf16[64,2,8,128]{3,2,1,0:T(8,128)(2,1)S(1)} collective-permute-done((bf16[64,2,8,128]{3,2,1,0:T(8,128)(2,1)S(1)}, bf16[64,2,8,128]{3,2,1,0:T(8,128)(2,1)S(1)}, u32[]{:S(2)}, u32[]{:S(2)}) %collective-permute-start.2) | collective-permute-done | bytes 262176 | tf_op jit(solution)/shard_map/ppermute | solution.py:128
  73.8 2.3 %precondition.1 = (bf16[2,512,512]{2,1,0:T(8,128)(2,1)S(1)}, f32[2,512,128]{2,1,0:T(8,128)S(1)}, f32[8,128]{1,0:T(8,128)S(1)}, f32[4,8,128]{2,1,0:T(8,128)S(1)}) custom-call(s32[1]{0:T(128)} %bitcast.lane_ref, bf16[64,2,8,128]{3,2,1,0:T(8,128)(2,1)S(1)} %bitcast.11, bf16[64,2,8,128]{3,2,1,0:T(8,128)(2,1)S(1)} %collective-permute-done.g1, ...), custom_call_target="tpu_custom_call" | custom-call | tf_op jit(solution)/shard_map/precondition/pallas_call | solution.py:175
  76.1 7.8 %all_to_all.20.parts_ref = f32[4,8,128]{2,1,0:T(8,128)S(1)} all-to-all(f32[4,8,128]{2,1,0:T(8,128)S(1)} %get-tuple-element.16), channel_id=1, replica_groups={{256,384,0,128},{257,385,1,129},{258,386,2,130},{259,387,3,131},{260,38..., dimensions={0} | all-to-all | bytes 32768 | tf_op jit(solution)/shard_map/all_to_all | solution.py:196
  83.9 0.8 graft.1
  84.7 14.3 %all-to-all-start.3 = ((bf16[128,8,128]{2,1,0:T(8,128)(2,1)}), bf16[128,8,128]{2,1,0:T(8,128)(2,1)S(1)}, u32[]{:S(2)}, u32[]{:S(2)}) async-start(bf16[128,8,128]{2,1,0:T(8,128)(2,1)} %bitcast.4), calls=%async_computation.3 | async-start | bytes 524288 | tf_op jit(solution)/shard_map/all_to_all | solution.py:209
  99.0 0.7 iota_compare_fusion.1
  99.7 0.0 copy-start.4
  99.7 1.2 fusion.3
  100.8 1.3 %fusion.1 = f32[2,128,512]{2,1,0:T(8,128)} fusion(f32[2,128,512]{2,1,0:T(8,128)S(1)} %copy-done.4, bf16[2,512,512]{2,1,0:T(8,128)(2,1)S(1)} %get-tuple-element.17, s32[]{:T(128)S(6)} %select_n.11, pred[2]{0:T(512)(128)(4,1)S(1)} %iota_compare_fusion.1), kind=kOutput, calls=%fused_computation.3 | convolution fusion | flops 134742016 | bytes 2359812 | tf_op jit(solution)/shard_map/cqk,cnk->cqn/dot_general | solution.py:217
  102.1 12.7 %all-to-all-done.3 = bf16[128,8,128]{2,1,0:T(8,128)(2,1)S(1)} async-done(((bf16[128,8,128]{2,1,0:T(8,128)(2,1)}), bf16[128,8,128]{2,1,0:T(8,128)(2,1)S(1)}, u32[]{:S(2)}, u32[]{:S(2)}) %all-to-all-start.3) | async-done | bytes 262176 | tf_op jit(solution)/shard_map/all_to_all | solution.py:209
  114.8 1.4 %take_cells.1 = bf16[128,4,128]{2,1,0:T(4,128)(2,1)} custom-call(s32[128]{0:T(128)S(1)} %get-tuple-element.20.place_ref, bf16[256,4,128]{2,1,0:T(4,128)(2,1)S(1)} %bitcast.12), custom_call_target="tpu_custom_call" | custom-call | tf_op jit(solution)/shard_map/take_cells/pallas_call | solution.py:222
  (9 shorter events, 0.0 us)
Async XLA Ops:
  0.6 1.0 copy-start
  2.6 11.3 %all-to-all-start = ((bf16[4,128,4,128]{3,2,1,0:T(4,128)(2,1)}), bf16[4,128,4,128]{3,2,1,0:T(4,128)(2,1)S(1)}, u32[]{:S(2)}, u32[]{:S(2)}) async-start(bf16[4,128,4,128]{3,2,1,0:T(4,128)(2,1)} %split_columns.1), calls=%async_computation | async-start | bytes 1048576 | tf_op jit(solution)/shard_map/all_to_all | solution.py:150
  9.7 0.7 copy-start.5
  15.5 24.5 %copy-start.2 = (bf16[2,128,512]{2,1,0:T(8,128)(2,1)S(1)}, bf16[2,128,512]{2,1,0:T(8,128)(2,1)}, u32[]{:S(2)}) copy-start(bf16[2,128,512]{2,1,0:T(8,128)(2,1)} %l0) | copy-start | bytes 786436
  15.5 58.3 %copy-start.1 = (bf16[2,128,512]{2,1,0:T(8,128)(2,1)S(1)}, bf16[2,128,512]{2,1,0:T(8,128)(2,1)}, u32[]{:S(2)}) copy-start(bf16[2,128,512]{2,1,0:T(8,128)(2,1)} %right_hbm.1) | copy-start | bytes 786436
  15.5 40.3 %all-to-all-start.1 = ((bf16[128,8,128]{2,1,0:T(8,128)(2,1)}), bf16[128,8,128]{2,1,0:T(8,128)(2,1)S(1)}, u32[]{:S(2)}, u32[]{:S(2)}) async-start(bf16[128,8,128]{2,1,0:T(8,128)(2,1)} %bitcast.2), calls=%async_computation.1 | async-start | bytes 524288 | tf_op jit(solution)/shard_map/all_to_all | solution.py:168
  40.0 23.2 %collective-permute-start.3 = (bf16[2,128,512]{2,1,0:T(8,128)(2,1)S(1)}, bf16[2,128,512]{2,1,0:T(8,128)(2,1)S(1)}, u32[]{:S(2)}, u32[]{:S(2)}) collective-permute-start(bf16[2,128,512]{2,1,0:T(8,128)(2,1)S(1)} %copy-done.2), channel_id=1, source_target_pairs={{0,128},{128,256},{256,384},{384,0},{1,129},{129,257},{257,385},{3... | collective-permute-start | bytes 786440 | tf_op jit(solution)/shard_map/ppermute | solution.py:128
  42.5 23.8 %collective-permute-start.4 = (bf16[2,128,512]{2,1,0:T(8,128)(2,1)S(1)}, bf16[2,128,512]{2,1,0:T(8,128)(2,1)S(1)}, u32[]{:S(2)}, u32[]{:S(2)}) collective-permute-start(bf16[2,128,512]{2,1,0:T(8,128)(2,1)S(1)} %copy-done.2), channel_id=1, source_target_pairs={{0,256},{128,384},{256,0},{384,128},{1,257},{129,385},{257,1},{385... | collective-permute-start | bytes 786440 | tf_op jit(solution)/shard_map/ppermute | solution.py:128
  47.4 18.9 %collective-permute-start.5 = (bf16[2,128,512]{2,1,0:T(8,128)(2,1)S(1)}, bf16[2,128,512]{2,1,0:T(8,128)(2,1)S(1)}, u32[]{:S(2)}, u32[]{:S(2)}) collective-permute-start(bf16[2,128,512]{2,1,0:T(8,128)(2,1)S(1)} %copy-done.2), channel_id=1, source_target_pairs={{0,384},{128,0},{256,128},{384,256},{1,385},{129,1},{257,129},{385... | collective-permute-start | bytes 786440 | tf_op jit(solution)/shard_map/ppermute | solution.py:128
  55.7 10.5 %collective-permute-start = (bf16[64,2,8,128]{3,2,1,0:T(8,128)(2,1)S(1)}, bf16[64,2,8,128]{3,2,1,0:T(8,128)(2,1)S(1)}, u32[]{:S(2)}, u32[]{:S(2)}) collective-permute-start(bf16[64,2,8,128]{3,2,1,0:T(8,128)(2,1)S(1)} %bitcast.8), channel_id=1, source_target_pairs={{0,128},{128,256},{256,384},{384,0},{1,129},{129,257},{257,385},{3... | collective-permute-start | bytes 786440 | tf_op jit(solution)/shard_map/ppermute | solution.py:128
  58.2 14.3 %collective-permute-start.1 = (bf16[64,2,8,128]{3,2,1,0:T(8,128)(2,1)S(1)}, bf16[64,2,8,128]{3,2,1,0:T(8,128)(2,1)S(1)}, u32[]{:S(2)}, u32[]{:S(2)}) collective-permute-start(bf16[64,2,8,128]{3,2,1,0:T(8,128)(2,1)S(1)} %bitcast.9), channel_id=1, source_target_pairs={{0,256},{128,384},{256,0},{384,128},{1,257},{129,385},{257,1},{385... | collective-permute-start | bytes 786440 | tf_op jit(solution)/shard_map/ppermute | solution.py:128
  63.2 10.7 %collective-permute-start.2 = (bf16[64,2,8,128]{3,2,1,0:T(8,128)(2,1)S(1)}, bf16[64,2,8,128]{3,2,1,0:T(8,128)(2,1)S(1)}, u32[]{:S(2)}, u32[]{:S(2)}) collective-permute-start(bf16[64,2,8,128]{3,2,1,0:T(8,128)(2,1)S(1)} %bitcast.10), channel_id=1, source_target_pairs={{0,384},{128,0},{256,128},{384,256},{1,385},{129,1},{257,129},{385... | collective-permute-start | bytes 786440 | tf_op jit(solution)/shard_map/ppermute | solution.py:128
  83.9 15.7 %copy-start.3 = (f32[2,128,512]{2,1,0:T(8,128)S(1)}, f32[2,128,512]{2,1,0:T(8,128)}, u32[]{:S(2)}) copy-start(f32[2,128,512]{2,1,0:T(8,128)} %param.9) | copy-start | bytes 1572868
  84.7 30.0 %all-to-all-start.3 = ((bf16[128,8,128]{2,1,0:T(8,128)(2,1)}), bf16[128,8,128]{2,1,0:T(8,128)(2,1)S(1)}, u32[]{:S(2)}, u32[]{:S(2)}) async-start(bf16[128,8,128]{2,1,0:T(8,128)(2,1)} %bitcast.4), calls=%async_computation.3 | async-start | bytes 524288 | tf_op jit(solution)/shard_map/all_to_all | solution.py:209
  99.7 1.2 %copy-start.4 = (f32[2,128,512]{2,1,0:T(8,128)S(1)}, f32[2,128,512]{2,1,0:T(8,128)}, u32[]{:S(2)}) copy-start(f32[2,128,512]{2,1,0:T(8,128)} %param.8) | copy-start | bytes 1572868

commit v3 on v1

v3 whole, which is shorter than its diff:
```python
import jax
import jax.numpy as jnp
from jax import lax
from jax.experimental import pallas as pl
from jax.experimental.pallas import tpu as pltpu
from jax.sharding import PartitionSpec as P

decay_rate = 0.95
epsilon = 1e-06

VMEM = pl.BlockSpec(memory_space=pltpu.VMEM)
SMEM = pl.BlockSpec(memory_space=pltpu.SMEM)
ANY = pl.BlockSpec(memory_space=pl.ANY)
HBM = pl.BlockSpec(memory_space=pltpu.HBM)
PARAMS = pltpu.CompilerParams(vmem_limit_bytes=40 * 1024 * 1024)

PLANES, COLUMNS, CORES, LANES = 16, 4, 2, 4
LANE_ORDER = (2, 3, 0, 1)
COLUMN_ORDER = (2, 3, 0, 1)
FIRST_PLANE = 10
PLANE_ORDER = tuple((FIRST_PLANE + i) % PLANES for i in range(PLANES))
SEATS = COLUMNS * CORES
SEAT_ORDER = tuple(y * CORES + c for y in COLUMN_ORDER for c in range(CORES))


def split_columns(x_ref, out_ref):
    quarter = out_ref.shape[3]
    for place in range(out_ref.shape[0]):
        lane = LANE_ORDER[place]
        out_ref[place] = x_ref[:, :, lane * quarter : (lane + 1) * quarter]


def sum_and_place(place_ref, terms_ref, out_ref):
    out_ref[...] = jnp.zeros_like(out_ref)

    def step(block, carry):
        total = terms_ref[0, block].astype(jnp.float32)
        for term in range(1, terms_ref.shape[0]):
            total += terms_ref[term, block].astype(jnp.float32)
        out_ref[place_ref[block]] = total.astype(out_ref.dtype)
        return carry

    lax.fori_loop(0, terms_ref.shape[1], step, 0, unroll=8)


def take_cells(place_ref, cells_ref, out_ref):
    def step(block, carry):
        out_ref[block] = cells_ref[place_ref[block]]
        return carry

    lax.fori_loop(0, out_ref.shape[0], step, 0, unroll=8)


def fan_out(x_ref, out_hbm, slots, sems):
    for slot in range(2):
        for i, seat in enumerate(SEAT_ORDER):
            for k, plane in enumerate(PLANE_ORDER):
                slots[slot, i, plane] = x_ref[k, seat, slot]
    copies = [
        pltpu.make_async_copy(slots.at[lane % 2], out_hbm.at[i], sems.at[i])
        for i, lane in enumerate(LANE_ORDER)
    ]
    for copy in copies:
        copy.start()
    for copy in copies:
        copy.wait()


def two_terms(value):
    high = value.astype(jnp.bfloat16).astype(jnp.float32)
    return high, value - high


def paired(first, second):
    upper = lax.broadcasted_iota(jnp.int32, first.shape, first.ndim - 2) < 4
    return (
        jnp.where(upper, first, pltpu.roll(second, 4, first.ndim - 2)),
        jnp.where(upper, pltpu.roll(first, 4, first.ndim - 2), second),
    )


def precondition(
    lane_ref, pieces, left_hbm, right_hbm, beside, across, opposite, grads_ref, out_ref,
    lefts, rights, sems,
):
    lane = lane_ref[0]
    parity = lax.rem(lane, 2)
    width = grads_ref.shape[0]
    quarter = left_hbm.shape[1]

    def rows_of(x):
        return pl.ds(pl.multiple_of(x * quarter, quarter), quarter)

    copies = [
        pltpu.make_async_copy(left_hbm.at[parity], lefts.at[rows_of(parity)], sems.at[0]),
        pltpu.make_async_copy(beside.at[1], lefts.at[rows_of(1 - parity)], sems.at[1]),
        pltpu.make_async_copy(right_hbm.at[parity], rights.at[rows_of(lane)], sems.at[2]),
        pltpu.make_async_copy(beside.at[0], rights.at[rows_of(lane ^ 1)], sems.at[3]),
        pltpu.make_async_copy(across, rights.at[rows_of(lane ^ 3)], sems.at[4]),
        pltpu.make_async_copy(opposite, rights.at[rows_of(lane ^ 2)], sems.at[5]),
    ]
    for copy in copies:
        copy.start()

    square = jnp.zeros((1, 1), jnp.float32)
    for i, source in enumerate(LANE_ORDER):
        even, odd = [None] * COLUMNS, [None] * COLUMNS
        for j, y in enumerate(COLUMN_ORDER):
            even[y], odd[y] = paired(
                pieces[i, j * CORES].astype(jnp.float32),
                pieces[i, j * CORES + 1].astype(jnp.float32),
            )
        value = jnp.stack([jnp.stack(even, axis=1), jnp.stack(odd, axis=1)], axis=1)
        value = value.reshape(width // 8, 8, quarter)
        sums = jnp.sum(value * value, axis=0)
        square += jnp.sum(sums, axis=(0, 1), keepdims=True)
        flat = value.reshape(width, quarter).astype(jnp.bfloat16)
        grads_ref[:, source * quarter : (source + 1) * quarter] = flat
    for copy in copies:
        copy.wait()
    half = jnp.dot(lefts[...], grads_ref[...], preferred_element_type=jnp.float32)
    product = jnp.dot(
        half.astype(jnp.bfloat16), rights[...], preferred_element_type=jnp.float32
    )
    prod_sq = jnp.sum(jnp.sum(product * product, axis=0, keepdims=True), axis=1, keepdims=True)
    rows = lax.broadcasted_iota(jnp.int32, (8, quarter), 0)
    tail = jnp.zeros((8, quarter), jnp.float32)
    for r, value in enumerate((*two_terms(prod_sq), *two_terms(square))):
        tail = jnp.where(rows == r, value, tail)
    tail = tail.astype(out_ref.dtype)
    pairs = out_ref.shape[1] - 1
    for i, target in enumerate(LANE_ORDER):
        block = product[:, target * quarter : (target + 1) * quarter]
        block = block.reshape(pairs, 2, COLUMNS, 8, quarter)
        for j, y in enumerate(COLUMN_ORDER):
            for core, value in enumerate(paired(block[:, 0, y], block[:, 1, y])):
                seat = i * SEATS + j * CORES + core
                out_ref[seat, pl.ds(0, pairs)] = value.astype(out_ref.dtype)
                out_ref[seat, pairs] = tail


def graft(x_ref, out_ref):
    quarter = out_ref.shape[3]
    pairs = x_ref.shape[1] - 1
    cells = float((LANES * quarter) ** 2)
    for j, seat in enumerate(SEAT_ORDER):
        ratios = []
        for slot in range(2):
            upper, lower = [
                x_ref[LANE_ORDER.index(2 * half + slot) * SEATS + j, pairs].astype(jnp.float32)
                for half in range(2)
            ]
            total = upper + lower
            prod_sq = total[0:1] + total[1:2]
            grad_sq = upper[2:3] + upper[3:4]
            ratios.append(jnp.sqrt(grad_sq / cells) / jnp.sqrt(prod_sq / cells + epsilon))
        for half in range(2):
            scaled = []
            for slot in range(2):
                member = LANE_ORDER.index(2 * half + slot) * SEATS + j
                value = x_ref[member, pl.ds(0, pairs)].astype(jnp.float32)
                scaled.append(value * ratios[slot])
            for odd, value in enumerate(paired(*scaled)):
                for p in range(pairs):
                    plane = half * (PLANES // 2) + 2 * p + odd
                    place = (plane - FIRST_PLANE) % PLANES
                    out_ref[place, seat] = value[p].astype(out_ref.dtype)


def gram_rows(block, side, near):
    rows = block[near, :] if side == 0 else block[:, near]
    dims = ((1 - side,), (1 - side,))
    return lax.dot_general(rows, block[...], (dims, ((), ())), preferred_element_type=jnp.float32)


def own_statistics(
    info_ref, block, left_hbm, right_hbm, new_left_hbm, new_right_hbm, sent_ref, old, new, sems
):
    lane, used = info_ref[0], info_ref[1]
    slot = lax.rem(lane, 2)
    width = block.shape[0]
    quarter = old.shape[1]
    loads = [
        pltpu.make_async_copy(src.at[slot], old.at[i], sems.at[i])
        for i, src in enumerate((left_hbm, right_hbm))
    ]
    stores = [
        pltpu.make_async_copy(new.at[i], target.at[slot], sems.at[2 + i])
        for i, target in enumerate((new_left_hbm, new_right_hbm))
    ]
    for copy in loads:
        copy.start()
    mine = pl.ds(pl.multiple_of(lane * quarter, quarter), quarter)
    theirs = pl.ds(pl.multiple_of((lane ^ 1) * quarter, quarter), quarter)
    for i in range(2):
        gram = gram_rows(block, i, mine)
        loads[i].wait()
        was = old[i]
        new[i] = jnp.where(slot < used, decay_rate * was + gram / width, was)
        stores[i].start()
    for i in range(2):
        sent_ref[i] = gram_rows(block, i, theirs).astype(sent_ref.dtype)
    for copy in stores:
        copy.wait()


def other_statistics(
    info_ref, grams_ref, left_hbm, right_hbm, _, __, new_left_hbm, new_right_hbm, old, new, sems
):
    lane, used = info_ref[0], info_ref[1]
    slot = 1 - lax.rem(lane, 2)
    width = old.shape[2]
    loads = [
        pltpu.make_async_copy(src.at[slot], old.at[i], sems.at[i])
        for i, src in enumerate((left_hbm, right_hbm))
    ]
    stores = [
        pltpu.make_async_copy(new.at[i], target.at[slot], sems.at[2 + i])
        for i, target in enumerate((new_left_hbm, new_right_hbm))
    ]
    for copy in loads:
        copy.start()
    for i in range(2):
        loads[i].wait()
        was = old[i]
        gram = grams_ref[i].astype(jnp.float32)
        new[i] = jnp.where(slot < used, decay_rate * was + gram / width, was)
        stores[i].start()
    for copy in stores:
        copy.wait()


def lane_swap(x, mask):
    return lax.ppermute(x, "dp", [(i, i ^ mask) for i in range(LANES)])


def exchange(x, axes, groups):
    return lax.all_to_all(
        x, axes, split_axis=0, concat_axis=0, tiled=True, axis_index_groups=groups
    )


def body(partial_grads, owner_list, left_stat, right_stat, left_root, right_root):
    owners = PLANES * SEATS
    capacity, quarter, width = left_stat.shape
    blocks = owner_list.shape[0]
    rows = width // owners
    block_ids = jnp.arange(blocks, dtype=jnp.int32)
    lane = lax.axis_index("dp")
    lane_groups = [list(LANE_ORDER)]
    plane_groups = [[z * SEATS + seat for z in PLANE_ORDER] for seat in range(SEATS)]
    flat_groups = [
        [x * owners + z * SEATS + seat for x in LANE_ORDER for seat in SEAT_ORDER]
        for z in range(PLANES)
    ]

    terms = pl.pallas_call(
        split_columns,
        out_shape=jax.ShapeDtypeStruct((LANES, blocks, rows, quarter), jnp.bfloat16),
        in_specs=[VMEM],
        out_specs=VMEM,
        compiler_params=PARAMS,
        name="split_columns",
    )(partial_grads[0])
    terms = exchange(terms, "dp", lane_groups)

    same = (owner_list[:, None] == owner_list[None, :]) & (block_ids[None, :] < block_ids[:, None])
    slot_index = jnp.sum(same.astype(jnp.int32), axis=1)
    turned = lax.rem(owner_list + (PLANES - FIRST_PLANE) * SEATS, owners)
    place = turned * capacity + slot_index

    outgoing = pl.pallas_call(
        sum_and_place,
        out_shape=jax.ShapeDtypeStruct((owners * capacity, rows, quarter), jnp.bfloat16),
        in_specs=[SMEM, VMEM],
        out_specs=VMEM,
        compiler_params=PARAMS,
        name="sum_and_place",
    )(place, terms)
    outgoing = outgoing.reshape(PLANES, SEATS * capacity * rows, quarter)
    parity = lane % 2
    theirs = jnp.stack([right_root, left_root])
    theirs = lax.dynamic_index_in_dim(theirs, 1 - parity, 1, keepdims=False)
    mine = lax.dynamic_index_in_dim(right_root, parity, 0, keepdims=False)
    theirs, mine, outgoing = lax.optimization_barrier((theirs, mine, outgoing))
    arrived = exchange(outgoing, "own", plane_groups)
    opposite, beside, across = lane_swap(mine, 2), lane_swap(theirs, 1), lane_swap(theirs[0], 3)
    opposite, beside, arrived = lax.optimization_barrier((opposite, beside, arrived))

    tile = capacity * rows
    copies = pl.pallas_call(
        fan_out,
        out_shape=jax.ShapeDtypeStruct((LANES, SEATS, PLANES, rows, quarter), jnp.bfloat16),
        in_specs=[VMEM],
        out_specs=HBM,
        scratch_shapes=[
            pltpu.VMEM((capacity, SEATS, PLANES, rows, quarter), jnp.bfloat16),
            pltpu.SemaphoreType.DMA((LANES,)),
        ],
        compiler_params=PARAMS,
        name="fan_out",
    )(arrived.reshape(PLANES, SEATS, capacity, rows, quarter))
    members = LANES * SEATS
    pieces = exchange(copies.reshape(members, PLANES * rows, quarter), ("dp", "own"), flat_groups)
    pieces = pieces.reshape(LANES, SEATS, PLANES // 2, 2 * rows, quarter)

    near = PLANES // 4 + 1
    grads, product = pl.pallas_call(
        precondition,
        out_shape=(
            jax.ShapeDtypeStruct((width, width), jnp.bfloat16),
            jax.ShapeDtypeStruct((members, near, tile, quarter), jnp.bfloat16),
        ),
        in_specs=[SMEM, VMEM] + [ANY] * 5,
        out_specs=(VMEM, VMEM),
        scratch_shapes=[
            pltpu.VMEM((width // 2, width), jnp.bfloat16),
            pltpu.VMEM((width, width), jnp.bfloat16),
            pltpu.SemaphoreType.DMA((6,)),
        ],
        compiler_params=PARAMS,
        name="precondition",
    )(lane.reshape(1), pieces, left_root, right_root, beside, across, opposite)
    product = exchange(product.reshape(members, near * tile, quarter), ("dp", "own"), flat_groups)

    used = jnp.sum((owner_list == lax.axis_index("own")).astype(jnp.int32))
    info = jnp.stack([lane, used])
    stat_shapes = (
        jax.ShapeDtypeStruct(left_stat.shape, jnp.float32),
        jax.ShapeDtypeStruct(right_stat.shape, jnp.float32),
    )
    stat_scratch = [
        pltpu.VMEM((2, quarter, width), jnp.float32),
        pltpu.VMEM((2, quarter, width), jnp.float32),
        pltpu.SemaphoreType.DMA((4,)),
    ]
    light = pl.CostEstimate(flops=1, bytes_accessed=1, transcendentals=0)
    new_left, new_right, grams = pl.pallas_call(
        own_statistics,
        out_shape=stat_shapes + (jax.ShapeDtypeStruct((2, quarter, width), jnp.bfloat16),),
        in_specs=[SMEM, VMEM, HBM, HBM],
        out_specs=(HBM, HBM, VMEM),
        scratch_shapes=stat_scratch,
        compiler_params=PARAMS,
        cost_estimate=light,
        name="own_statistics",
    )(info, grads, left_stat, right_stat)
    product, grams, new_left, new_right = lax.optimization_barrier(
        (product, grams, new_left, new_right)
    )
    scaled = pl.pallas_call(
        graft,
        out_shape=jax.ShapeDtypeStruct((PLANES, SEATS, tile, quarter), jnp.bfloat16),
        in_specs=[VMEM],
        out_specs=VMEM,
        compiler_params=PARAMS,
        name="graft",
    )(product.reshape(members, near, tile, quarter))
    grams, scaled = lax.optimization_barrier((grams, scaled))
    returned = exchange(scaled.reshape(PLANES, SEATS * tile, quarter), "own", plane_groups)

    new_left, new_right = pl.pallas_call(
        other_statistics,
        out_shape=stat_shapes,
        in_specs=[SMEM, VMEM, HBM, HBM, HBM, HBM],
        out_specs=(HBM, HBM),
        scratch_shapes=stat_scratch,
        input_output_aliases={4: 0, 5: 1},
        compiler_params=PARAMS,
        cost_estimate=light,
        name="other_statistics",
    )(info, lane_swap(grams, 1), left_stat, right_stat, new_left, new_right)

    update = pl.pallas_call(
        take_cells,
        out_shape=jax.ShapeDtypeStruct((blocks, rows, quarter), jnp.bfloat16),
        in_specs=[SMEM, VMEM],
        out_specs=VMEM,
        compiler_params=PARAMS,
        name="take_cells",
    )(place, returned.reshape(owners * capacity, rows, quarter))
    return (new_left, new_right, update)


def solution(mesh):
    in_specs = (
        P("dp", None, "own", None),
        P(),
        P("own", "dp", None),
        P("own", "dp", None),
        P("own", "dp", None),
        P("own", "dp", None),
    )
    out_specs = (P("own", "dp", None), P("own", "dp", None), P(None, "own", "dp"))
    return jax.shard_map(body, mesh=mesh, in_specs=in_specs, out_specs=out_specs, check_vma=False)
```

time: 143 us -> 111 us (0.78)
  blocking collectives: 42.8 us -> 0 us
  starting transfers between devices: 26.7 us -> 67.4 us
  waiting for transfers between devices: 52.7 us -> 26.1 us
  Pallas kernels: 0 us -> 12.2 us
  local copies, waits for them, and re-layouts: 11.3 us -> 1.83 us
  matrix products: 4.5 us -> 0 us
    all_to_all x5, waiting for transfers between devices: 52.7 us -> 8.7 us  [exchange(): lax.all_to_all(x, axes, split_axis=0, concat_axis=0, tiled=True, axis_ind...]
    all_to_all x1 -> x0, blocking collectives: 42.8 us -> none  [body(): lax.all_to_all(outgoing, 'own', split_axis=0, concat_axis=0, tiled=True)]
    all_to_all x5, starting transfers between devices: 26.7 us -> 55.7 us  [exchange(): lax.all_to_all(x, axes, split_axis=0, concat_axis=0, tiled=True, axis_ind...]
    ppermute x0 -> x4, waiting for transfers between devices: none -> 17.4 us  [lane_swap(): return lax.ppermute(x, 'dp', [(i, i ^ mask) for i in range(LANES)])]
    pallas_call x0 -> x8, Pallas kernels: none -> 12.2 us  [the longest x1 2.74 us: body(): pl.pallas_call(precondition, out_shape=(jax.ShapeDtypeStruct((width, widt...]
    ppermute x0 -> x4, starting transfers between devices: none -> 11.7 us  [lane_swap(): return lax.ppermute(x, 'dp', [(i, i ^ mask) for i in range(LANES)])]
    dot_general x3 -> x0, matrix products: 4.5 us -> none  [the longest x1 2.08 us: body(): jnp.einsum('cpn,cpq->cnq', left_full, half, preferred_element_type=jnp.fl...]
    transpose x4 -> x0, local copies, waits for them, and re-layouts: 3.07 us -> none  [the longest x1 1.15 us: body(): left_full = left_all.transpose(1, 0, 2, 3).reshape(capacity, width, width)]
  transfers between devices with their start and end apart: 5 -> 9, of which waited for: 5 -> 7; matrix products, arithmetic and copies ran while one was open for 4% -> 1% of each run, Pallas kernels for 0% -> 3%
where the time goes in v3:
time: 111 us; the launch traced here: 110 us
  starting transfers between devices  67.4 us (61%)
  waiting for transfers between devices  26.1 us (24%)
  Pallas kernels  12.2 us (11%)
  local copies, waits for them, and re-layouts  1.83 us (2%)
  other arithmetic  1.55 us (1%)
    all_to_all x5, starting transfers between devices, exchange(): lax.all_to_all(x, axes, split_axis=0, concat_axis=0, tiled=True, axis_ind...  55.7 us
    ppermute x4, waiting for transfers between devices, lane_swap(): return lax.ppermute(x, 'dp', [(i, i ^ mask) for i in range(LANES)])  17.4 us
    ppermute x4, starting transfers between devices, lane_swap(): return lax.ppermute(x, 'dp', [(i, i ^ mask) for i in range(LANES)])  11.7 us
    all_to_all x5, waiting for transfers between devices, exchange(): lax.all_to_all(x, axes, split_axis=0, concat_axis=0, tiled=True, axis_ind...  8.7 us
    pallas_call x1, Pallas kernels, body(): pl.pallas_call(precondition, out_shape=(jax.ShapeDtypeStruct((width, widt...  2.74 us
    pallas_call x1, Pallas kernels, body(): pl.pallas_call(own_statistics, out_shape=stat_shapes + (jax.ShapeDtypeStr...  2.25 us
  transfers between devices with their start and end apart: 9, of which 7 were waited for; matrix products, arithmetic and copies ran while one was open for 1% of the time, Pallas kernels for 3%

profile of v3, /device:TPU:1, one launch (start us, length us, event | category | flops | bytes accessed | tf_op | source)
XLA Modules:
  0.0 109.9 jit_solution(10273429199217599952)
XLA Ops:
  0.6 1.0 copy-done.4
  1.7 1.0 split_columns.1
  2.6 7.1 %all-to-all-start = ((bf16[4,128,4,128]{3,2,1,0:T(4,128)(2,1)}), bf16[4,128,4,128]{3,2,1,0:T(4,128)(2,1)S(1)}, u32[]{:S(2)}, u32[]{:S(2)}) async-start(bf16[4,128,4,128]{3,2,1,0:T(4,128)(2,1)} %split_columns.1), calls=%async_computation | async-start | bytes 1048576 | tf_op jit(solution)/shard_map/all_to_all | solution.py:238
  9.8 0.7 copy-done.5
  10.5 0.2 convert_reduce_fusion
  10.7 0.1 copy-done.3
  10.8 0.6 fusion.6
  11.4 2.6 %all-to-all-done.terms_ref = bf16[4,128,4,128]{3,2,1,0:T(4,128)(2,1)S(1)} async-done(((bf16[4,128,4,128]{3,2,1,0:T(4,128)(2,1)}), bf16[4,128,4,128]{3,2,1,0:T(4,128)(2,1)S(1)}, u32[]{:S(2)}, u32[]{:S(2)}) %all-to-all-start) | async-done | bytes 524320 | tf_op jit(solution)/shard_map/all_to_all | solution.py:238
  14.0 1.6 %sum_and_place.1 = bf16[256,4,128]{2,1,0:T(4,128)(2,1)} custom-call(s32[128]{0:T(128)S(1)} %get-tuple-element.41.place_ref, bf16[4,128,4,128]{3,2,1,0:T(4,128)(2,1)S(1)} %all-to-all-done.terms_ref), custom_call_target="tpu_custom_call" | custom-call | tf_op jit(solution)/shard_map/sum_and_place/pallas_call | solution.py:272
  15.6 18.5 %all-to-all-start.1 = ((bf16[16,64,128]{2,1,0:T(8,128)(2,1)}), bf16[16,64,128]{2,1,0:T(8,128)(2,1)S(1)}, u32[]{:S(2)}, u32[]{:S(2)}) async-start(bf16[16,64,128]{2,1,0:T(8,128)(2,1)} %bitcast.7), calls=%async_computation.1 | async-start | bytes 524288 | tf_op jit(solution)/shard_map/all_to_all | solution.py:238
  34.2 2.4 %collective-permute-start.1 = (bf16[2,128,512]{2,1,0:T(8,128)(2,1)S(1)}, bf16[2,128,512]{2,1,0:T(8,128)(2,1)S(1)}, u32[]{:S(2)}, u32[]{:S(2)}) collective-permute-start(bf16[2,128,512]{2,1,0:T(8,128)(2,1)S(1)} %fusion.1), channel_id=1, source_target_pairs={{0,128},{128,0},{256,384},{384,256},{1,129},{129,1},{257,385},{385... | collective-permute-start | bytes 786440 | tf_op jit(solution)/shard_map/ppermute | solution.py:234
  36.5 4.3 %collective-permute-start = (bf16[128,512]{1,0:T(8,128)(2,1)S(1)}, bf16[128,512]{1,0:T(8,128)(2,1)S(1)}, u32[]{:S(2)}, u32[]{:S(2)}) collective-permute-start(bf16[128,512]{1,0:T(8,128)(2,1)S(1)} %dynamic-slice_bitcast_fusion), channel_id=1, source_target_pairs={{0,256},{128,384},{256,0},{384,128},{1,257},{129,385},{257,1},{385... | collective-permute-start | bytes 393224 | tf_op jit(solution)/shard_map/ppermute | solution.py:234
  40.9 4.5 %collective-permute-done.opposite = bf16[128,512]{1,0:T(8,128)(2,1)S(1)} collective-permute-done((bf16[128,512]{1,0:T(8,128)(2,1)S(1)}, bf16[128,512]{1,0:T(8,128)(2,1)S(1)}, u32[]{:S(2)}, u32[]{:S(2)}) %collective-permute-start) | collective-permute-done | bytes 131104 | tf_op jit(solution)/shard_map/ppermute | solution.py:234
  45.3 0.0 collective-permute-done.1.beside
  45.4 1.4 %all-to-all-done.1 = bf16[16,64,128]{2,1,0:T(8,128)(2,1)S(1)} async-done(((bf16[16,64,128]{2,1,0:T(8,128)(2,1)}), bf16[16,64,128]{2,1,0:T(8,128)(2,1)S(1)}, u32[]{:S(2)}, u32[]{:S(2)}) %all-to-all-start.1) | async-done | bytes 262176 | tf_op jit(solution)/shard_map/all_to_all | solution.py:238
  46.7 0.9 fan_out.1
  47.6 11.1 %all-to-all-start.2 = ((bf16[32,64,128]{2,1,0:T(8,128)(2,1)}), bf16[32,64,128]{2,1,0:T(8,128)(2,1)S(1)}, u32[]{:S(2)}, u32[]{:S(2)}) async-start(bf16[32,64,128]{2,1,0:T(8,128)(2,1)} %bitcast.9), calls=%async_computation.2 | async-start | bytes 1048576 | tf_op jit(solution)/shard_map/all_to_all | solution.py:238
  58.8 2.1 %collective-permute-start.2 = (bf16[128,512]{1,0:T(8,128)(2,1)S(1)}, bf16[128,512]{1,0:T(8,128)(2,1)S(1)}, u32[]{:S(2)}, u32[]{:S(2)}) collective-permute-start(bf16[128,512]{1,0:T(8,128)(2,1)S(1)} %slice_bitcast_fusion), channel_id=1, source_target_pairs={{0,384},{128,256},{256,128},{384,0},{1,385},{129,257},{257,129},{3... | collective-permute-start | bytes 393224 | tf_op jit(solution)/shard_map/ppermute | solution.py:234
  60.9 7.5 %collective-permute-done.2.across = bf16[128,512]{1,0:T(8,128)(2,1)S(1)} collective-permute-done((bf16[128,512]{1,0:T(8,128)(2,1)S(1)}, bf16[128,512]{1,0:T(8,128)(2,1)S(1)}, u32[]{:S(2)}, u32[]{:S(2)}) %collective-permute-start.2) | collective-permute-done | bytes 131104 | tf_op jit(solution)/shard_map/ppermute | solution.py:234
  68.4 2.7 %precondition.1 = (bf16[512,512]{1,0:T(8,128)(2,1)S(1)}, bf16[32,5,8,128]{3,2,1,0:T(8,128)(2,1)}) custom-call(s32[1]{0:T(128)} %bitcast.lane_ref, bf16[4,8,8,8,128]{4,3,2,1,0:T(8,128)(2,1)S(1)} %bitcast.19, bf16[2,128,512]{2,1,0:T(8,128)(2,1)S(1)} %copy-done.3, bf16[2,128,512]{2,1,0:T(8,128)(2,1)S(1)} %copy-done.2, ...), custom_call_target="tpu_custom_call" | custom-call | tf_op jit(solution)/shard_map/precondition/pallas_call | solution.py:308
  71.2 0.0 copy-start
  71.2 8.3 %all-to-all-start.3 = ((bf16[32,40,128]{2,1,0:T(8,128)(2,1)}), bf16[32,40,128]{2,1,0:T(8,128)(2,1)S(1)}, u32[]{:S(2)}, u32[]{:S(2)}) async-start(bf16[32,40,128]{2,1,0:T(8,128)(2,1)} %bitcast.12), calls=%async_computation.3 | async-start | bytes 655360 | tf_op jit(solution)/shard_map/all_to_all | solution.py:238
  79.5 0.7 pad_add_fusion.info_ref
  80.3 2.3 %own_statistics.1 = (f32[2,128,512]{2,1,0:T(8,128)}, f32[2,128,512]{2,1,0:T(8,128)}, bf16[2,128,512]{2,1,0:T(8,128)(2,1)S(1)}) custom-call(s32[2]{0:T(128)S(1)} %pad_add_fusion.info_ref, bf16[512,512]{1,0:T(8,128)(2,1)S(1)} %get-tuple-element.29.block, f32[2,128,512]{2,1,0:T(8,128)S(1)} %copy-done, f32[2,128,512]{2,1,0:T(8,128)S(1)} %copy-done.1), custom_call_target="tpu_custom_call" | custom-call | flops 1 | bytes 1 | tf_op jit(solution)/shard_map/own_statistics/pallas_call | solution.py:338
  82.5 1.7 %all-to-all-done.3 = bf16[32,40,128]{2,1,0:T(8,128)(2,1)S(1)} async-done(((bf16[32,40,128]{2,1,0:T(8,128)(2,1)}), bf16[32,40,128]{2,1,0:T(8,128)(2,1)S(1)}, u32[]{:S(2)}, u32[]{:S(2)}) %all-to-all-start.3) | async-done | bytes 327712 | tf_op jit(solution)/shard_map/all_to_all | solution.py:238
  84.2 0.9 graft.1
  85.1 10.6 %all-to-all-start.4 = ((bf16[16,64,128]{2,1,0:T(8,128)(2,1)}), bf16[16,64,128]{2,1,0:T(8,128)(2,1)S(1)}, u32[]{:S(2)}, u32[]{:S(2)}) async-start(bf16[16,64,128]{2,1,0:T(8,128)(2,1)} %bitcast.14), calls=%async_computation.4 | async-start | bytes 524288 | tf_op jit(solution)/shard_map/all_to_all | solution.py:238
  95.7 2.9 %collective-permute-start.3 = (bf16[2,128,512]{2,1,0:T(8,128)(2,1)S(1)}, bf16[2,128,512]{2,1,0:T(8,128)(2,1)S(1)}, u32[]{:S(2)}, u32[]{:S(2)}) collective-permute-start(bf16[2,128,512]{2,1,0:T(8,128)(2,1)S(1)} %get-tuple-element.35), channel_id=1, source_target_pairs={{0,128},{128,0},{256,384},{384,256},{1,129},{129,1},{257,385},{385... | collective-permute-start | bytes 786440 | tf_op jit(solution)/shard_map/ppermute | solution.py:234
  98.6 5.4 %collective-permute-done.3.grams_ref = bf16[2,128,512]{2,1,0:T(8,128)(2,1)S(1)} collective-permute-done((bf16[2,128,512]{2,1,0:T(8,128)(2,1)S(1)}, bf16[2,128,512]{2,1,0:T(8,128)(2,1)S(1)}, u32[]{:S(2)}, u32[]{:S(2)}) %collective-permute-start.3) | collective-permute-done | bytes 262176 | tf_op jit(solution)/shard_map/ppermute | solution.py:234
  104.0 1.5 %other_statistics.1 = (f32[2,128,512]{2,1,0:T(8,128)}, f32[2,128,512]{2,1,0:T(8,128)}) custom-call(s32[2]{0:T(128)S(1)} %pad_add_fusion.info_ref, bf16[2,128,512]{2,1,0:T(8,128)(2,1)S(1)} %collective-permute-done.3.grams_ref, f32[2,128,512]{2,1,0:T(8,128)S(1)} %copy-done, ...), custom_call_target="tpu_custom_call", output_to_operand_aliasing={{0}: (4, {}), {1}: (5, {})} | custom-call | flops 1 | bytes 1 | tf_op jit(solution)/shard_map/other_statistics/pallas_call | solution.py:362
  105.5 3.0 %all-to-all-done.4 = bf16[16,64,128]{2,1,0:T(8,128)(2,1)S(1)} async-done(((bf16[16,64,128]{2,1,0:T(8,128)(2,1)}), bf16[16,64,128]{2,1,0:T(8,128)(2,1)S(1)}, u32[]{:S(2)}, u32[]{:S(2)}) %all-to-all-start.4) | async-done | bytes 262176 | tf_op jit(solution)/shard_map/all_to_all | solution.py:238
  108.5 1.4 %take_cells.1 = bf16[128,4,128]{2,1,0:T(4,128)(2,1)} custom-call(s32[128]{0:T(128)S(1)} %get-tuple-element.41.place_ref, bf16[256,4,128]{2,1,0:T(4,128)(2,1)S(1)} %bitcast.23), custom_call_target="tpu_custom_call" | custom-call | tf_op jit(solution)/shard_map/take_cells/pallas_call | solution.py:374
  (12 shorter events, 0.1 us)
Async XLA Ops:
  0.6 1.0 copy-start.4
  2.6 7.2 %copy-start.2 = (bf16[2,128,512]{2,1,0:T(8,128)(2,1)S(1)}, bf16[2,128,512]{2,1,0:T(8,128)(2,1)}, u32[]{:S(2)}) copy-start(bf16[2,128,512]{2,1,0:T(8,128)(2,1)} %right_hbm.3) | copy-start | bytes 786436
  2.6 11.4 %all-to-all-start = ((bf16[4,128,4,128]{3,2,1,0:T(4,128)(2,1)}), bf16[4,128,4,128]{3,2,1,0:T(4,128)(2,1)S(1)}, u32[]{:S(2)}, u32[]{:S(2)}) async-start(bf16[4,128,4,128]{3,2,1,0:T(4,128)(2,1)} %split_columns.1), calls=%async_computation | async-start | bytes 1048576 | tf_op jit(solution)/shard_map/all_to_all | solution.py:238
  9.8 1.0 copy-start.3
  9.8 0.7 copy-start.5
  15.6 31.1 %all-to-all-start.1 = ((bf16[16,64,128]{2,1,0:T(8,128)(2,1)}), bf16[16,64,128]{2,1,0:T(8,128)(2,1)S(1)}, u32[]{:S(2)}, u32[]{:S(2)}) async-start(bf16[16,64,128]{2,1,0:T(8,128)(2,1)} %bitcast.7), calls=%async_computation.1 | async-start | bytes 524288 | tf_op jit(solution)/shard_map/all_to_all | solution.py:238
  34.2 11.2 %collective-permute-start.1 = (bf16[2,128,512]{2,1,0:T(8,128)(2,1)S(1)}, bf16[2,128,512]{2,1,0:T(8,128)(2,1)S(1)}, u32[]{:S(2)}, u32[]{:S(2)}) collective-permute-start(bf16[2,128,512]{2,1,0:T(8,128)(2,1)S(1)} %fusion.1), channel_id=1, source_target_pairs={{0,128},{128,0},{256,384},{384,256},{1,129},{129,1},{257,385},{385... | collective-permute-start | bytes 786440 | tf_op jit(solution)/shard_map/ppermute | solution.py:234
  36.5 8.8 %collective-permute-start = (bf16[128,512]{1,0:T(8,128)(2,1)S(1)}, bf16[128,512]{1,0:T(8,128)(2,1)S(1)}, u32[]{:S(2)}, u32[]{:S(2)}) collective-permute-start(bf16[128,512]{1,0:T(8,128)(2,1)S(1)} %dynamic-slice_bitcast_fusion), channel_id=1, source_target_pairs={{0,256},{128,384},{256,0},{384,128},{1,257},{129,385},{257,1},{385... | collective-permute-start | bytes 393224 | tf_op jit(solution)/shard_map/ppermute | solution.py:234
  47.6 20.8 %all-to-all-start.2 = ((bf16[32,64,128]{2,1,0:T(8,128)(2,1)}), bf16[32,64,128]{2,1,0:T(8,128)(2,1)S(1)}, u32[]{:S(2)}, u32[]{:S(2)}) async-start(bf16[32,64,128]{2,1,0:T(8,128)(2,1)} %bitcast.9), calls=%async_computation.2 | async-start | bytes 1048576 | tf_op jit(solution)/shard_map/all_to_all | solution.py:238
  58.8 9.7 %collective-permute-start.2 = (bf16[128,512]{1,0:T(8,128)(2,1)S(1)}, bf16[128,512]{1,0:T(8,128)(2,1)S(1)}, u32[]{:S(2)}, u32[]{:S(2)}) collective-permute-start(bf16[128,512]{1,0:T(8,128)(2,1)S(1)} %slice_bitcast_fusion), channel_id=1, source_target_pairs={{0,384},{128,256},{256,128},{384,0},{1,385},{129,257},{257,129},{3... | collective-permute-start | bytes 393224 | tf_op jit(solution)/shard_map/ppermute | solution.py:234
  68.4 11.8 %copy-start.1 = (f32[2,128,512]{2,1,0:T(8,128)S(1)}, f32[2,128,512]{2,1,0:T(8,128)}, u32[]{:S(2)}) copy-start(f32[2,128,512]{2,1,0:T(8,128)} %right_hbm.5) | copy-start | bytes 1572868
  71.2 9.1 %copy-start = (f32[2,128,512]{2,1,0:T(8,128)S(1)}, f32[2,128,512]{2,1,0:T(8,128)}, u32[]{:S(2)}) copy-start(f32[2,128,512]{2,1,0:T(8,128)} %left_hbm.5) | copy-start | bytes 1572868
  71.2 13.0 %all-to-all-start.3 = ((bf16[32,40,128]{2,1,0:T(8,128)(2,1)}), bf16[32,40,128]{2,1,0:T(8,128)(2,1)S(1)}, u32[]{:S(2)}, u32[]{:S(2)}) async-start(bf16[32,40,128]{2,1,0:T(8,128)(2,1)} %bitcast.12), calls=%async_computation.3 | async-start | bytes 655360 | tf_op jit(solution)/shard_map/all_to_all | solution.py:238
  85.1 23.4 %all-to-all-start.4 = ((bf16[16,64,128]{2,1,0:T(8,128)(2,1)}), bf16[16,64,128]{2,1,0:T(8,128)(2,1)S(1)}, u32[]{:S(2)}, u32[]{:S(2)}) async-start(bf16[16,64,128]{2,1,0:T(8,128)(2,1)} %bitcast.14), calls=%async_computation.4 | async-start | bytes 524288 | tf_op jit(solution)/shard_map/all_to_all | solution.py:238
  95.7 8.3 %collective-permute-start.3 = (bf16[2,128,512]{2,1,0:T(8,128)(2,1)S(1)}, bf16[2,128,512]{2,1,0:T(8,128)(2,1)S(1)}, u32[]{:S(2)}, u32[]{:S(2)}) collective-permute-start(bf16[2,128,512]{2,1,0:T(8,128)(2,1)S(1)} %get-tuple-element.35), channel_id=1, source_target_pairs={{0,128},{128,0},{256,384},{384,256},{1,129},{129,1},{257,385},{385... | collective-permute-start | bytes 786440 | tf_op jit(solution)/shard_map/ppermute | solution.py:234

commit v4 on v3

--- a/solution.py
+++ b/solution.py
@@ -23,11 +23,26 @@
 SEAT_ORDER = tuple(y * CORES + c for y in COLUMN_ORDER for c in range(CORES))
 
 
-def split_columns(x_ref, out_ref):
-    quarter = out_ref.shape[3]
-    for place in range(out_ref.shape[0]):
-        lane = LANE_ORDER[place]
-        out_ref[place] = x_ref[:, :, lane * quarter : (lane + 1) * quarter]
+def split_columns(x_hbm, out_hbm, x, out, in_sems, out_sems):
+    quarter = out.shape[3]
+    parts = in_sems.shape[0]
+    size = x.shape[0] // parts
+    arriving, leaving = [], []
+    for part in range(parts):
+        blocks = pl.ds(part * size, size)
+        arriving.append(pltpu.make_async_copy(x_hbm.at[blocks], x.at[blocks], in_sems.at[part]))
+        leaving.append(
+            pltpu.make_async_copy(out.at[:, blocks], out_hbm.at[:, blocks], out_sems.at[part])
+        )
+        arriving[part].start()
+    for part in range(parts):
+        arriving[part].wait()
+        blocks = pl.ds(part * size, size)
+        for place, lane in enumerate(LANE_ORDER):
+            out[place, blocks] = x[blocks, :, lane * quarter : (lane + 1) * quarter]
+        leaving[part].start()
+    for copy in leaving:
+        copy.wait()
 
 
 def sum_and_place(place_ref, terms_ref, out_ref):
@@ -68,7 +83,7 @@
 
 def two_terms(value):
     high = value.astype(jnp.bfloat16).astype(jnp.float32)
-    return high, value - high
+    return high, jnp.where(high < jnp.inf, value - high, 0.0)
 
 
 def paired(first, second):
@@ -79,8 +94,32 @@
     )
 
 
+def gram_rows(block, side, near):
+    rows = block[near, :] if side == 0 else block[:, near]
+    dims = ((1 - side,), (1 - side,))
+    return lax.dot_general(rows, block[...], (dims, ((), ())), preferred_element_type=jnp.float32)
+
+
+def pick_blocks(lane_ref, left_ref, right_ref, beside_ref, across_ref, opposite_ref):
+    lane = lane_ref[0]
+    parity = lax.rem(lane, 2)
+    quarter = left_ref.shape[1]
+
+    def block(ref, slot, lane_of_columns):
+        columns = pl.ds(pl.multiple_of(lane_of_columns * quarter, quarter), quarter)
+        return ref[slot, :, columns]
+
+    for i, column in enumerate((lane, lane ^ 3, lane ^ 1)):
+        opposite_ref[i] = block(right_ref, parity, column)
+    for i, column in enumerate((lane, lane ^ 3, lane ^ 2)):
+        beside_ref[i] = block(left_ref, 1 - parity, column)
+    beside_ref[3] = block(right_ref, 1 - parity, lane)
+    beside_ref[4] = block(right_ref, 1 - parity, lane ^ 2)
+    across_ref[0] = block(right_ref, 1 - parity, lane)
+
+
 def precondition(
-    lane_ref, pieces, left_hbm, right_hbm, beside, across, opposite, grads_ref, out_ref,
+    lane_ref, pieces, left_hbm, right_hbm, beside, across, opposite, grads_ref, out_ref, grams_ref,
     lefts, rights, sems,
 ):
     lane = lane_ref[0]
@@ -93,11 +132,7 @@
 
     copies = [
         pltpu.make_async_copy(left_hbm.at[parity], lefts.at[rows_of(parity)], sems.at[0]),
-        pltpu.make_async_copy(beside.at[1], lefts.at[rows_of(1 - parity)], sems.at[1]),
-        pltpu.make_async_copy(right_hbm.at[parity], rights.at[rows_of(lane)], sems.at[2]),
-        pltpu.make_async_copy(beside.at[0], rights.at[rows_of(lane ^ 1)], sems.at[3]),
-        pltpu.make_async_copy(across, rights.at[rows_of(lane ^ 3)], sems.at[4]),
-        pltpu.make_async_copy(opposite, rights.at[rows_of(lane ^ 2)], sems.at[5]),
+        pltpu.make_async_copy(right_hbm.at[parity], rights.at[rows_of(lane)], sems.at[1]),
     ]
     for copy in copies:
         copy.start()
@@ -118,6 +153,25 @@
         grads_ref[:, source * quarter : (source + 1) * quarter] = flat
     for copy in copies:
         copy.wait()
+    side, far, last = lane ^ 1, lane ^ 3, lane ^ 2
+
+    def put(row, column, block):
+        rights[rows_of(row), rows_of(column)] = block
+        if row is not column:
+            rights[rows_of(column), rows_of(row)] = block.T
+
+    for other in (side, far, last):
+        rights[rows_of(other), rows_of(lane)] = rights[rows_of(lane), rows_of(other)].T
+    put(last, last, opposite[0])
+    put(last, side, opposite[1])
+    put(last, far, opposite[2])
+    put(side, side, beside[3])
+    put(side, far, beside[4])
+    put(far, far, across[0])
+    below = rows_of(1 - parity)
+    lefts[below, rows_of(lane)] = lefts[rows_of(parity), rows_of(side)].T
+    for i, column in enumerate((side, last, far)):
+        lefts[below, rows_of(column)] = beside[i]
     half = jnp.dot(lefts[...], grads_ref[...], preferred_element_type=jnp.float32)
     product = jnp.dot(
         half.astype(jnp.bfloat16), rights[...], preferred_element_type=jnp.float32
@@ -137,6 +191,8 @@
                 seat = i * SEATS + j * CORES + core
                 out_ref[seat, pl.ds(0, pairs)] = value.astype(out_ref.dtype)
                 out_ref[seat, pairs] = tail
+    for side in range(2):
+        grams_ref[side] = gram_rows(grads_ref, side, rows_of(lane ^ 1)).astype(grams_ref.dtype)
 
 
 def graft(x_ref, out_ref):
@@ -167,65 +223,32 @@
                     out_ref[place, seat] = value[p].astype(out_ref.dtype)
 
 
-def gram_rows(block, side, near):
-    rows = block[near, :] if side == 0 else block[:, near]
-    dims = ((1 - side,), (1 - side,))
-    return lax.dot_general(rows, block[...], (dims, ((), ())), preferred_element_type=jnp.float32)
-
-
-def own_statistics(
-    info_ref, block, left_hbm, right_hbm, new_left_hbm, new_right_hbm, sent_ref, old, new, sems
+def statistics(
+    info_ref, block, grams_ref, left_hbm, right_hbm, new_left_hbm, new_right_hbm, old, new, sems
 ):
     lane, used = info_ref[0], info_ref[1]
-    slot = lax.rem(lane, 2)
+    parity = lax.rem(lane, 2)
+    slots = (parity, 1 - parity)
     width = block.shape[0]
-    quarter = old.shape[1]
-    loads = [
-        pltpu.make_async_copy(src.at[slot], old.at[i], sems.at[i])
-        for i, src in enumerate((left_hbm, right_hbm))
-    ]
-    stores = [
-        pltpu.make_async_copy(new.at[i], target.at[slot], sems.at[2 + i])
-        for i, target in enumerate((new_left_hbm, new_right_hbm))
-    ]
+    quarter = old.shape[2]
+    loads, stores = [], []
+    for i, slot in enumerate(slots):
+        for side, (src, target) in enumerate(((left_hbm, new_left_hbm), (right_hbm, new_right_hbm))):
+            loads.append(pltpu.make_async_copy(src.at[slot], old.at[i, side], sems.at[0, i, side]))
+            stores.append(pltpu.make_async_copy(new.at[i, side], target.at[slot], sems.at[1, i, side]))
     for copy in loads:
         copy.start()
     mine = pl.ds(pl.multiple_of(lane * quarter, quarter), quarter)
-    theirs = pl.ds(pl.multiple_of((lane ^ 1) * quarter, quarter), quarter)
-    for i in range(2):
-        gram = gram_rows(block, i, mine)
-        loads[i].wait()
-        was = old[i]
-        new[i] = jnp.where(slot < used, decay_rate * was + gram / width, was)
-        stores[i].start()
-    for i in range(2):
-        sent_ref[i] = gram_rows(block, i, theirs).astype(sent_ref.dtype)
-    for copy in stores:
-        copy.wait()
-
-
-def other_statistics(
-    info_ref, grams_ref, left_hbm, right_hbm, _, __, new_left_hbm, new_right_hbm, old, new, sems
-):
-    lane, used = info_ref[0], info_ref[1]
-    slot = 1 - lax.rem(lane, 2)
-    width = old.shape[2]
-    loads = [
-        pltpu.make_async_copy(src.at[slot], old.at[i], sems.at[i])
-        for i, src in enumerate((left_hbm, right_hbm))
-    ]
-    stores = [
-        pltpu.make_async_copy(new.at[i], target.at[slot], sems.at[2 + i])
-        for i, target in enumerate((new_left_hbm, new_right_hbm))
-    ]
-    for copy in loads:
-        copy.start()
-    for i in range(2):
-        loads[i].wait()
-        was = old[i]
-        gram = grams_ref[i].astype(jnp.float32)
-        new[i] = jnp.where(slot < used, decay_rate * was + gram / width, was)
-        stores[i].start()
+    for i, slot in enumerate(slots):
+        for side in range(2):
+            if i == 0:
+                gram = gram_rows(block, side, mine)
+            else:
+                gram = grams_ref[side].astype(jnp.float32)
+            loads[2 * i + side].wait()
+            was = old[i, side]
+            new[i, side] = jnp.where(slot < used, decay_rate * was + gram / width, was)
+            stores[2 * i + side].start()
     for copy in stores:
         copy.wait()
 
@@ -257,12 +280,30 @@
     terms = pl.pallas_call(
         split_columns,
         out_shape=jax.ShapeDtypeStruct((LANES, blocks, rows, quarter), jnp.bfloat16),
-        in_specs=[VMEM],
-        out_specs=VMEM,
-        compiler_params=PARAMS,
+        in_specs=[HBM],
+        out_specs=HBM,
+        scratch_shapes=[
+            pltpu.VMEM((blocks, rows, width), jnp.bfloat16),
+            pltpu.VMEM((LANES, blocks, rows, quarter), jnp.bfloat16),
+            pltpu.SemaphoreType.DMA((4,)),
+            pltpu.SemaphoreType.DMA((4,)),
+        ],
         name="split_columns",
     )(partial_grads[0])
+    left, right, terms = lax.optimization_barrier((left_root, right_root, terms))
     terms = exchange(terms, "dp", lane_groups)
+    picked = pl.pallas_call(
+        pick_blocks,
+        out_shape=[jax.ShapeDtypeStruct((n, quarter, quarter), jnp.bfloat16) for n in (5, 1, 3)],
+        in_specs=[SMEM, VMEM, VMEM],
+        out_specs=[VMEM] * 3,
+        compiler_params=PARAMS,
+        cost_estimate=pl.CostEstimate(flops=1, bytes_accessed=4 * 1024 * 1024, transcendentals=0),
+        name="pick_blocks",
+    )(lane.reshape(1), left, right)
+
+    across = lane_swap(picked[1], 3)
+    across, terms = lax.optimization_barrier((across, terms))
 
     same = (owner_list[:, None] == owner_list[None, :]) & (block_ids[None, :] < block_ids[:, None])
     slot_index = jnp.sum(same.astype(jnp.int32), axis=1)
@@ -278,14 +319,10 @@
         name="sum_and_place",
     )(place, terms)
     outgoing = outgoing.reshape(PLANES, SEATS * capacity * rows, quarter)
-    parity = lane % 2
-    theirs = jnp.stack([right_root, left_root])
-    theirs = lax.dynamic_index_in_dim(theirs, 1 - parity, 1, keepdims=False)
-    mine = lax.dynamic_index_in_dim(right_root, parity, 0, keepdims=False)
-    theirs, mine, outgoing = lax.optimization_barrier((theirs, mine, outgoing))
+    picked, outgoing = lax.optimization_barrier((picked, outgoing))
     arrived = exchange(outgoing, "own", plane_groups)
-    opposite, beside, across = lane_swap(mine, 2), lane_swap(theirs, 1), lane_swap(theirs[0], 3)
-    opposite, beside, arrived = lax.optimization_barrier((opposite, beside, arrived))
+    beside, opposite = lane_swap(picked[0], 1), lane_swap(picked[2], 2)
+    beside, opposite, arrived = lax.optimization_barrier((beside, opposite, arrived))
 
     tile = capacity * rows
     copies = pl.pallas_call(
@@ -305,49 +342,25 @@
     pieces = pieces.reshape(LANES, SEATS, PLANES // 2, 2 * rows, quarter)
 
     near = PLANES // 4 + 1
-    grads, product = pl.pallas_call(
+    grads, product, grams = pl.pallas_call(
         precondition,
         out_shape=(
             jax.ShapeDtypeStruct((width, width), jnp.bfloat16),
             jax.ShapeDtypeStruct((members, near, tile, quarter), jnp.bfloat16),
+            jax.ShapeDtypeStruct((2, quarter, width), jnp.bfloat16),
         ),
-        in_specs=[SMEM, VMEM] + [ANY] * 5,
-        out_specs=(VMEM, VMEM),
+        in_specs=[SMEM, VMEM, ANY, ANY, VMEM, VMEM, VMEM],
+        out_specs=(VMEM, VMEM, VMEM),
         scratch_shapes=[
             pltpu.VMEM((width // 2, width), jnp.bfloat16),
             pltpu.VMEM((width, width), jnp.bfloat16),
-            pltpu.SemaphoreType.DMA((6,)),
+            pltpu.SemaphoreType.DMA((2,)),
         ],
         compiler_params=PARAMS,
         name="precondition",
     )(lane.reshape(1), pieces, left_root, right_root, beside, across, opposite)
     product = exchange(product.reshape(members, near * tile, quarter), ("dp", "own"), flat_groups)
 
-    used = jnp.sum((owner_list == lax.axis_index("own")).astype(jnp.int32))
-    info = jnp.stack([lane, used])
-    stat_shapes = (
-        jax.ShapeDtypeStruct(left_stat.shape, jnp.float32),
-        jax.ShapeDtypeStruct(right_stat.shape, jnp.float32),
-    )
-    stat_scratch = [
-        pltpu.VMEM((2, quarter, width), jnp.float32),
-        pltpu.VMEM((2, quarter, width), jnp.float32),
-        pltpu.SemaphoreType.DMA((4,)),
-    ]
-    light = pl.CostEstimate(flops=1, bytes_accessed=1, transcendentals=0)
-    new_left, new_right, grams = pl.pallas_call(
-        own_statistics,
-        out_shape=stat_shapes + (jax.ShapeDtypeStruct((2, quarter, width), jnp.bfloat16),),
-        in_specs=[SMEM, VMEM, HBM, HBM],
-        out_specs=(HBM, HBM, VMEM),
-        scratch_shapes=stat_scratch,
-        compiler_params=PARAMS,
-        cost_estimate=light,
-        name="own_statistics",
-    )(info, grads, left_stat, right_stat)
-    product, grams, new_left, new_right = lax.optimization_barrier(
-        (product, grams, new_left, new_right)
-    )
     scaled = pl.pallas_call(
         graft,
         out_shape=jax.ShapeDtypeStruct((PLANES, SEATS, tile, quarter), jnp.bfloat16),
@@ -356,20 +369,27 @@
         compiler_params=PARAMS,
         name="graft",
     )(product.reshape(members, near, tile, quarter))
-    grams, scaled = lax.optimization_barrier((grams, scaled))
+    grads, grams, scaled = lax.optimization_barrier((grads, grams, scaled))
     returned = exchange(scaled.reshape(PLANES, SEATS * tile, quarter), "own", plane_groups)
 
+    used = jnp.sum((owner_list == lax.axis_index("own")).astype(jnp.int32))
     new_left, new_right = pl.pallas_call(
-        other_statistics,
-        out_shape=stat_shapes,
-        in_specs=[SMEM, VMEM, HBM, HBM, HBM, HBM],
+        statistics,
+        out_shape=(
+            jax.ShapeDtypeStruct(left_stat.shape, jnp.float32),
+            jax.ShapeDtypeStruct(right_stat.shape, jnp.float32),
+        ),
+        in_specs=[SMEM, VMEM, VMEM, HBM, HBM],
         out_specs=(HBM, HBM),
-        scratch_shapes=stat_scratch,
-        input_output_aliases={4: 0, 5: 1},
-        compiler_params=PARAMS,
-        cost_estimate=light,
-        name="other_statistics",
-    )(info, lane_swap(grams, 1), left_stat, right_stat, new_left, new_right)
+        scratch_shapes=[
+            pltpu.VMEM((2, 2, quarter, width), jnp.float32),
+            pltpu.VMEM((2, 2, quarter, width), jnp.float32),
+            pltpu.SemaphoreType.DMA((2, 2, 2)),
+        ],
+        compiler_params=PARAMS,
+        cost_estimate=pl.CostEstimate(flops=1, bytes_accessed=1, transcendentals=0),
+        name="statistics",
+    )(jnp.stack([lane, used]), grads, lane_swap(grams, 1), left_stat, right_stat)
 
     update = pl.pallas_call(
         take_cells,

time: 111 us -> 107 us (0.964)
  blocking collectives: 0 us -> 29.5 us
  starting transfers between devices: 67.4 us -> 47 us
  waiting for transfers between devices: 26.1 us -> 15.9 us
  Pallas kernels: 12.2 us -> 10.2 us
  local copies, waits for them, and re-layouts: 1.83 us -> 0.67 us
    all_to_all x0 -> x2, blocking collectives: none -> 29.5 us  [exchange(): lax.all_to_all(x, axes, split_axis=0, concat_axis=0, tiled=True, axis_ind...]
    all_to_all x5 -> x3, starting transfers between devices: 55.7 us -> 35.5 us  [exchange(): lax.all_to_all(x, axes, split_axis=0, concat_axis=0, tiled=True, axis_ind...]
    ppermute x4, waiting for transfers between devices: 17.4 us -> 10.4 us  [lane_swap(): return lax.ppermute(x, 'dp', [(i, i ^ mask) for i in range(LANES)])]
    all_to_all x5 -> x3, waiting for transfers between devices: 8.7 us -> 5.47 us  [exchange(): lax.all_to_all(x, axes, split_axis=0, concat_axis=0, tiled=True, axis_ind...]
    pallas_call x2, Pallas kernels: 3.71 us -> 2.23 us  [the longest x1 2.18 us: body(): pl.pallas_call(statistics, out_shape=(jax.ShapeDtypeStruct(left_stat.shap...]
    pallas_call x1, Pallas kernels: 2.74 us -> 1.46 us  [body(): pl.pallas_call(precondition, out_shape=(jax.ShapeDtypeStruct((width, widt...]
    unnamed x12 -> x10, local copies, waits for them, and re-layouts: 1.81 us -> 0.67 us
  transfers between devices with their start and end apart: 9 -> 7, of which waited for: 7 -> 5; matrix products, arithmetic and copies ran while one was open for 1% -> 1% of each run, Pallas kernels for 3% -> 2%
where the time goes in v4:
time: 107 us; the launch traced here: 106 us
  starting transfers between devices  47 us (44%)
  blocking collectives  29.5 us (28%)
  waiting for transfers between devices  15.9 us (15%)
  Pallas kernels  10.2 us (10%)
  other arithmetic  1.53 us (1%)
    all_to_all x3, starting transfers between devices, exchange(): lax.all_to_all(x, axes, split_axis=0, concat_axis=0, tiled=True, axis_ind...  35.5 us
    all_to_all x2, blocking collectives, exchange(): lax.all_to_all(x, axes, split_axis=0, concat_axis=0, tiled=True, axis_ind...  29.5 us
    ppermute x4, starting transfers between devices, lane_swap(): return lax.ppermute(x, 'dp', [(i, i ^ mask) for i in range(LANES)])  11.5 us
    ppermute x4, waiting for transfers between devices, lane_swap(): return lax.ppermute(x, 'dp', [(i, i ^ mask) for i in range(LANES)])  10.4 us
    all_to_all x3, waiting for transfers between devices, exchange(): lax.all_to_all(x, axes, split_axis=0, concat_axis=0, tiled=True, axis_ind...  5.47 us
    pallas_call x1, Pallas kernels, body(): pl.pallas_call(statistics, out_shape=(jax.ShapeDtypeStruct(left_stat.shap...  2.18 us
  transfers between devices with their start and end apart: 7, of which 5 were waited for; matrix products, arithmetic and copies ran while one was open for 1% of the time, Pallas kernels for 2%

profile of v4, /device:TPU:1, one launch (start us, length us, event | category | flops | bytes accessed | tf_op | source)
XLA Modules:
  0.0 105.5 jit_solution(11873352141010131700)
XLA Ops:
  0.6 1.9 %split_columns.1 = bf16[4,128,4,128]{3,2,1,0:T(4,128)(2,1)} custom-call(bf16[128,4,512]{2,1,0:T(4,128)(2,1)} %bitcast.17), custom_call_target="tpu_custom_call" | custom-call | tf_op jit(solution)/shard_map/split_columns/pallas_call | solution.py:280
  2.5 0.0 copy-start
  2.5 0.0 copy-start.1
  2.5 7.2 %all-to-all-start = ((bf16[4,128,4,128]{3,2,1,0:T(4,128)(2,1)}), bf16[4,128,4,128]{3,2,1,0:T(4,128)(2,1)S(1)}, u32[]{:S(2)}, u32[]{:S(2)}) async-start(bf16[4,128,4,128]{3,2,1,0:T(4,128)(2,1)} %split_columns.1), calls=%async_computation | async-start | bytes 1048576 | tf_op jit(solution)/shard_map/all_to_all | solution.py:261
  9.7 0.0 copy-done
  9.7 2.2 %collective-permute-start = (bf16[1,128,128]{2,1,0:T(8,128)(2,1)S(1)}, bf16[1,128,128]{2,1,0:T(8,128)(2,1)S(1)}, u32[]{:S(2)}, u32[]{:S(2)}) collective-permute-start(bf16[1,128,128]{2,1,0:T(8,128)(2,1)S(1)} %get-tuple-element.28), channel_id=1, source_target_pairs={{0,384},{128,256},{256,128},{384,0},{1,385},{129,257},{257,129},{3... | collective-permute-start | bytes 98312 | tf_op jit(solution)/shard_map/ppermute | solution.py:257
  11.9 0.0 copy-start.4
  12.0 0.6 copy-done.4
  12.6 0.2 convert_reduce_fusion
  12.8 0.6 fusion.4
  13.4 2.2 %collective-permute-done.across = bf16[1,128,128]{2,1,0:T(8,128)(2,1)S(1)} collective-permute-done((bf16[1,128,128]{2,1,0:T(8,128)(2,1)S(1)}, bf16[1,128,128]{2,1,0:T(8,128)(2,1)S(1)}, u32[]{:S(2)}, u32[]{:S(2)}) %collective-permute-start) | collective-permute-done | bytes 32800 | tf_op jit(solution)/shard_map/ppermute | solution.py:257
  15.6 0.0 all-to-all-done.terms_ref
  15.6 1.6 %sum_and_place.1 = bf16[256,4,128]{2,1,0:T(4,128)(2,1)} custom-call(s32[128]{0:T(128)S(1)} %get-tuple-element.47.place_ref, bf16[4,128,4,128]{3,2,1,0:T(4,128)(2,1)S(1)} %all-to-all-done.terms_ref), custom_call_target="tpu_custom_call" | custom-call | tf_op jit(solution)/shard_map/sum_and_place/pallas_call | solution.py:313
  17.2 18.5 %all-to-all-start.1 = ((bf16[16,64,128]{2,1,0:T(8,128)(2,1)}), bf16[16,64,128]{2,1,0:T(8,128)(2,1)S(1)}, u32[]{:S(2)}, u32[]{:S(2)}) async-start(bf16[16,64,128]{2,1,0:T(8,128)(2,1)} %bitcast.3), calls=%async_computation.1 | async-start | bytes 524288 | tf_op jit(solution)/shard_map/all_to_all | solution.py:261
  35.7 1.9 %collective-permute-start.1 = (bf16[5,128,128]{2,1,0:T(8,128)(2,1)S(1)}, bf16[5,128,128]{2,1,0:T(8,128)(2,1)S(1)}, u32[]{:S(2)}, u32[]{:S(2)}) collective-permute-start(bf16[5,128,128]{2,1,0:T(8,128)(2,1)S(1)} %get-tuple-element.32), channel_id=1, source_target_pairs={{0,128},{128,0},{256,384},{384,256},{1,129},{129,1},{257,385},{385... | collective-permute-start | bytes 491528 | tf_op jit(solution)/shard_map/ppermute | solution.py:257
  37.6 4.5 %collective-permute-start.2 = (bf16[3,128,128]{2,1,0:T(8,128)(2,1)S(1)}, bf16[3,128,128]{2,1,0:T(8,128)(2,1)S(1)}, u32[]{:S(2)}, u32[]{:S(2)}) collective-permute-start(bf16[3,128,128]{2,1,0:T(8,128)(2,1)S(1)} %get-tuple-element.33), channel_id=1, source_target_pairs={{0,256},{128,384},{256,0},{384,128},{1,257},{129,385},{257,1},{385... | collective-permute-start | bytes 294920 | tf_op jit(solution)/shard_map/ppermute | solution.py:257
  42.1 3.5 %collective-permute-done.2.opposite = bf16[3,128,128]{2,1,0:T(8,128)(2,1)S(1)} collective-permute-done((bf16[3,128,128]{2,1,0:T(8,128)(2,1)S(1)}, bf16[3,128,128]{2,1,0:T(8,128)(2,1)S(1)}, u32[]{:S(2)}, u32[]{:S(2)}) %collective-permute-start.2) | collective-permute-done | bytes 98336 | tf_op jit(solution)/shard_map/ppermute | solution.py:257
  45.6 0.0 collective-permute-done.1.beside
  45.6 3.2 %all-to-all-done.1 = bf16[16,64,128]{2,1,0:T(8,128)(2,1)S(1)} async-done(((bf16[16,64,128]{2,1,0:T(8,128)(2,1)}), bf16[16,64,128]{2,1,0:T(8,128)(2,1)S(1)}, u32[]{:S(2)}, u32[]{:S(2)}) %all-to-all-start.1) | async-done | bytes 262176 | tf_op jit(solution)/shard_map/all_to_all | solution.py:261
  48.8 0.8 fan_out.1
  49.6 16.8 %all_to_all.25 = bf16[32,64,128]{2,1,0:T(8,128)(2,1)S(1)} all-to-all(bf16[32,64,128]{2,1,0:T(8,128)(2,1)S(1)} %bitcast.12), channel_id=1, replica_groups={{260,261,262,263,256,257,258,259,388,389,390,391,384,385,386,387,4,5,6,..., dimensions={0} | all-to-all | bytes 1048576 | tf_op jit(solution)/shard_map/all_to_all | solution.py:261
  66.5 1.5 %precondition.1 = (bf16[512,512]{1,0:T(8,128)(2,1)S(1)}, bf16[32,5,8,128]{3,2,1,0:T(8,128)(2,1)S(1)}, bf16[2,128,512]{2,1,0:T(8,128)(2,1)S(1)}) custom-call(s32[1]{0:T(128)} %bitcast.lane_ref, bf16[4,8,8,8,128]{4,3,2,1,0:T(8,128)(2,1)S(1)} %bitcast.11, bf16[2,128,512]{2,1,0:T(8,128)(2,1)S(1)} %copy-done, bf16[2,128,512]{2,1,0:T(8,128)(2,1)S(1)} %copy-done.1, ...), custom_call_target="tpu_custom_call" | custom-call | tf_op jit(solution)/shard_map/precondition/pallas_call | solution.py:345
  67.9 12.7 %all_to_all.26 = bf16[32,40,128]{2,1,0:T(8,128)(2,1)S(1)} all-to-all(bf16[32,40,128]{2,1,0:T(8,128)(2,1)S(1)} %bitcast.16), channel_id=1, replica_groups={{260,261,262,263,256,257,258,259,388,389,390,391,384,385,386,387,4,5,6,..., dimensions={0} | all-to-all | bytes 655360 | tf_op jit(solution)/shard_map/all_to_all | solution.py:261
  80.6 0.9 graft.1
  81.5 9.8 %all-to-all-start.4 = ((bf16[16,64,128]{2,1,0:T(8,128)(2,1)}), bf16[16,64,128]{2,1,0:T(8,128)(2,1)S(1)}, u32[]{:S(2)}, u32[]{:S(2)}) async-start(bf16[16,64,128]{2,1,0:T(8,128)(2,1)} %bitcast.9), calls=%async_computation.4 | async-start | bytes 524288 | tf_op jit(solution)/shard_map/all_to_all | solution.py:261
  91.3 2.9 %collective-permute-start.3 = (bf16[2,128,512]{2,1,0:T(8,128)(2,1)S(1)}, bf16[2,128,512]{2,1,0:T(8,128)(2,1)S(1)}, u32[]{:S(2)}, u32[]{:S(2)}) collective-permute-start(bf16[2,128,512]{2,1,0:T(8,128)(2,1)S(1)} %get-tuple-element.43), channel_id=1, source_target_pairs={{0,128},{128,0},{256,384},{384,256},{1,129},{129,1},{257,385},{385... | collective-permute-start | bytes 786440 | tf_op jit(solution)/shard_map/ppermute | solution.py:257
  94.3 0.7 pad_add_fusion.info_ref
  95.0 4.7 %collective-permute-done.3.grams_ref = bf16[2,128,512]{2,1,0:T(8,128)(2,1)S(1)} collective-permute-done((bf16[2,128,512]{2,1,0:T(8,128)(2,1)S(1)}, bf16[2,128,512]{2,1,0:T(8,128)(2,1)S(1)}, u32[]{:S(2)}, u32[]{:S(2)}) %collective-permute-start.3) | collective-permute-done | bytes 262176 | tf_op jit(solution)/shard_map/ppermute | solution.py:257
  99.6 0.0 copy-done.2
  99.6 2.2 %statistics.1 = (f32[2,128,512]{2,1,0:T(8,128)}, f32[2,128,512]{2,1,0:T(8,128)}) custom-call(s32[2]{0:T(128)S(1)} %pad_add_fusion.info_ref, bf16[512,512]{1,0:T(8,128)(2,1)S(1)} %get-tuple-element.42.block, bf16[2,128,512]{2,1,0:T(8,128)(2,1)S(1)} %collective-permute-done.3.grams_ref, f32[2,128,512]{2,1,0:T(8,128)S(1)} %copy-done.2, f32[2,128,512]{2,1,0:T(8,128)S(1)} %copy-done.3), custom_call_target="tpu_custom_call" | custom-call | flops 1 | bytes 1 | tf_op jit(solution)/shard_map/statistics/pallas_call | solution.py:376
  101.8 2.3 %all-to-all-done.4 = bf16[16,64,128]{2,1,0:T(8,128)(2,1)S(1)} async-done(((bf16[16,64,128]{2,1,0:T(8,128)(2,1)}), bf16[16,64,128]{2,1,0:T(8,128)(2,1)S(1)}, u32[]{:S(2)}, u32[]{:S(2)}) %all-to-all-start.4) | async-done | bytes 262176 | tf_op jit(solution)/shard_map/all_to_all | solution.py:261
  104.1 1.4 %take_cells.1 = bf16[128,4,128]{2,1,0:T(4,128)(2,1)} custom-call(s32[128]{0:T(128)S(1)} %get-tuple-element.47.place_ref, bf16[256,4,128]{2,1,0:T(4,128)(2,1)S(1)} %bitcast.15), custom_call_target="tpu_custom_call" | custom-call | tf_op jit(solution)/shard_map/take_cells/pallas_call | solution.py:394
  (5 shorter events, 0.1 us)
Async XLA Ops:
  2.5 7.2 %copy-start = (bf16[2,128,512]{2,1,0:T(8,128)(2,1)S(1)}, bf16[2,128,512]{2,1,0:T(8,128)(2,1)}, u32[]{:S(2)}) copy-start(bf16[2,128,512]{2,1,0:T(8,128)(2,1)} %left_hbm.2) | copy-start | bytes 786436
  2.5 7.2 %copy-start.1 = (bf16[2,128,512]{2,1,0:T(8,128)(2,1)S(1)}, bf16[2,128,512]{2,1,0:T(8,128)(2,1)}, u32[]{:S(2)}) copy-start(bf16[2,128,512]{2,1,0:T(8,128)(2,1)} %right_hbm.2) | copy-start | bytes 786436
  2.5 13.1 %all-to-all-start = ((bf16[4,128,4,128]{3,2,1,0:T(4,128)(2,1)}), bf16[4,128,4,128]{3,2,1,0:T(4,128)(2,1)S(1)}, u32[]{:S(2)}, u32[]{:S(2)}) async-start(bf16[4,128,4,128]{3,2,1,0:T(4,128)(2,1)} %split_columns.1), calls=%async_computation | async-start | bytes 1048576 | tf_op jit(solution)/shard_map/all_to_all | solution.py:261
  9.7 5.9 %collective-permute-start = (bf16[1,128,128]{2,1,0:T(8,128)(2,1)S(1)}, bf16[1,128,128]{2,1,0:T(8,128)(2,1)S(1)}, u32[]{:S(2)}, u32[]{:S(2)}) collective-permute-start(bf16[1,128,128]{2,1,0:T(8,128)(2,1)S(1)} %get-tuple-element.28), channel_id=1, source_target_pairs={{0,384},{128,256},{256,128},{384,0},{1,385},{129,257},{257,129},{3... | collective-permute-start | bytes 98312 | tf_op jit(solution)/shard_map/ppermute | solution.py:257
  11.9 0.7 copy-start.4
  17.2 31.6 %all-to-all-start.1 = ((bf16[16,64,128]{2,1,0:T(8,128)(2,1)}), bf16[16,64,128]{2,1,0:T(8,128)(2,1)S(1)}, u32[]{:S(2)}, u32[]{:S(2)}) async-start(bf16[16,64,128]{2,1,0:T(8,128)(2,1)} %bitcast.3), calls=%async_computation.1 | async-start | bytes 524288 | tf_op jit(solution)/shard_map/all_to_all | solution.py:261
  35.7 9.9 %collective-permute-start.1 = (bf16[5,128,128]{2,1,0:T(8,128)(2,1)S(1)}, bf16[5,128,128]{2,1,0:T(8,128)(2,1)S(1)}, u32[]{:S(2)}, u32[]{:S(2)}) collective-permute-start(bf16[5,128,128]{2,1,0:T(8,128)(2,1)S(1)} %get-tuple-element.32), channel_id=1, source_target_pairs={{0,128},{128,0},{256,384},{384,256},{1,129},{129,1},{257,385},{385... | collective-permute-start | bytes 491528 | tf_op jit(solution)/shard_map/ppermute | solution.py:257
  37.6 8.0 %collective-permute-start.2 = (bf16[3,128,128]{2,1,0:T(8,128)(2,1)S(1)}, bf16[3,128,128]{2,1,0:T(8,128)(2,1)S(1)}, u32[]{:S(2)}, u32[]{:S(2)}) collective-permute-start(bf16[3,128,128]{2,1,0:T(8,128)(2,1)S(1)} %get-tuple-element.33), channel_id=1, source_target_pairs={{0,256},{128,384},{256,0},{384,128},{1,257},{129,385},{257,1},{385... | collective-permute-start | bytes 294920 | tf_op jit(solution)/shard_map/ppermute | solution.py:257
  80.6 19.0 %copy-start.2 = (f32[2,128,512]{2,1,0:T(8,128)S(1)}, f32[2,128,512]{2,1,0:T(8,128)}, u32[]{:S(2)}) copy-start(f32[2,128,512]{2,1,0:T(8,128)} %left_hbm.3) | copy-start | bytes 1572868
  80.6 19.0 %copy-start.3 = (f32[2,128,512]{2,1,0:T(8,128)S(1)}, f32[2,128,512]{2,1,0:T(8,128)}, u32[]{:S(2)}) copy-start(f32[2,128,512]{2,1,0:T(8,128)} %right_hbm.3) | copy-start | bytes 1572868
  81.5 22.6 %all-to-all-start.4 = ((bf16[16,64,128]{2,1,0:T(8,128)(2,1)}), bf16[16,64,128]{2,1,0:T(8,128)(2,1)S(1)}, u32[]{:S(2)}, u32[]{:S(2)}) async-start(bf16[16,64,128]{2,1,0:T(8,128)(2,1)} %bitcast.9), calls=%async_computation.4 | async-start | bytes 524288 | tf_op jit(solution)/shard_map/all_to_all | solution.py:261
  91.3 8.3 %collective-permute-start.3 = (bf16[2,128,512]{2,1,0:T(8,128)(2,1)S(1)}, bf16[2,128,512]{2,1,0:T(8,128)(2,1)S(1)}, u32[]{:S(2)}, u32[]{:S(2)}) collective-permute-start(bf16[2,128,512]{2,1,0:T(8,128)(2,1)S(1)} %get-tuple-element.43), channel_id=1, source_target_pairs={{0,128},{128,0},{256,384},{384,256},{1,129},{129,1},{257,385},{385... | collective-permute-start | bytes 786440 | tf_op jit(solution)/shard_map/ppermute | solution.py:257

commit v5 on v4

--- a/solution.py
+++ b/solution.py
@@ -109,13 +109,12 @@
         columns = pl.ds(pl.multiple_of(lane_of_columns * quarter, quarter), quarter)
         return ref[slot, :, columns]
 
-    for i, column in enumerate((lane, lane ^ 3, lane ^ 1)):
-        opposite_ref[i] = block(right_ref, parity, column)
     for i, column in enumerate((lane, lane ^ 3, lane ^ 2)):
-        beside_ref[i] = block(left_ref, 1 - parity, column)
-    beside_ref[3] = block(right_ref, 1 - parity, lane)
-    beside_ref[4] = block(right_ref, 1 - parity, lane ^ 2)
+        beside_ref[i] = block(right_ref, 1 - parity, column)
+        beside_ref[3 + i] = block(left_ref, 1 - parity, column)
     across_ref[0] = block(right_ref, 1 - parity, lane)
+    across_ref[1] = block(right_ref, 1 - parity, lane ^ 1)
+    opposite_ref[0] = block(right_ref, parity, lane)
 
 
 def precondition(
@@ -162,16 +161,16 @@
 
     for other in (side, far, last):
         rights[rows_of(other), rows_of(lane)] = rights[rows_of(lane), rows_of(other)].T
+    put(side, side, beside[0])
+    put(side, last, beside[1])
+    put(side, far, beside[2])
+    put(far, far, across[0])
+    put(far, last, across[1])
     put(last, last, opposite[0])
-    put(last, side, opposite[1])
-    put(last, far, opposite[2])
-    put(side, side, beside[3])
-    put(side, far, beside[4])
-    put(far, far, across[0])
     below = rows_of(1 - parity)
     lefts[below, rows_of(lane)] = lefts[rows_of(parity), rows_of(side)].T
     for i, column in enumerate((side, last, far)):
-        lefts[below, rows_of(column)] = beside[i]
+        lefts[below, rows_of(column)] = beside[3 + i]
     half = jnp.dot(lefts[...], grads_ref[...], preferred_element_type=jnp.float32)
     product = jnp.dot(
         half.astype(jnp.bfloat16), rights[...], preferred_element_type=jnp.float32
@@ -294,7 +293,7 @@
     terms = exchange(terms, "dp", lane_groups)
     picked = pl.pallas_call(
         pick_blocks,
-        out_shape=[jax.ShapeDtypeStruct((n, quarter, quarter), jnp.bfloat16) for n in (5, 1, 3)],
+        out_shape=[jax.ShapeDtypeStruct((n, quarter, quarter), jnp.bfloat16) for n in (6, 2, 1)],
         in_specs=[SMEM, VMEM, VMEM],
         out_specs=[VMEM] * 3,
         compiler_params=PARAMS,
@@ -302,8 +301,7 @@
         name="pick_blocks",
     )(lane.reshape(1), left, right)
 
-    across = lane_swap(picked[1], 3)
-    across, terms = lax.optimization_barrier((across, terms))
+    opposite = lane_swap(picked[2], 2)
 
     same = (owner_list[:, None] == owner_list[None, :]) & (block_ids[None, :] < block_ids[:, None])
     slot_index = jnp.sum(same.astype(jnp.int32), axis=1)
@@ -319,10 +317,10 @@
         name="sum_and_place",
     )(place, terms)
     outgoing = outgoing.reshape(PLANES, SEATS * capacity * rows, quarter)
-    picked, outgoing = lax.optimization_barrier((picked, outgoing))
+    picked, opposite, outgoing = lax.optimization_barrier((picked, opposite, outgoing))
     arrived = exchange(outgoing, "own", plane_groups)
-    beside, opposite = lane_swap(picked[0], 1), lane_swap(picked[2], 2)
-    beside, opposite, arrived = lax.optimization_barrier((beside, opposite, arrived))
+    beside, across = lane_swap(picked[0], 1), lane_swap(picked[1], 3)
+    beside, across, arrived = lax.optimization_barrier((beside, across, arrived))
 
     tile = capacity * rows
     copies = pl.pallas_call(

time: 107 us -> 105 us (0.981)
  waiting for transfers between devices: 15.9 us -> 13.3 us
  blocking collectives: 29.5 us -> 31.1 us
    ppermute x4, waiting for transfers between devices: 10.4 us -> 7.61 us  [lane_swap(): return lax.ppermute(x, 'dp', [(i, i ^ mask) for i in range(LANES)])]
    all_to_all x2, blocking collectives: 29.5 us -> 31.1 us  [exchange(): lax.all_to_all(x, axes, split_axis=0, concat_axis=0, tiled=True, axis_ind...]
  transfers between devices with their start and end apart: 7 -> 7, of which waited for: 5 -> 6; matrix products, arithmetic and copies ran while one was open for 1% -> 1% of each run, Pallas kernels for 2% -> 4%
where the time goes in v5:
time: 105 us; the launch traced here: 104 us
  starting transfers between devices  46.5 us (44%)
  blocking collectives  31.1 us (30%)
  waiting for transfers between devices  13.3 us (13%)
  Pallas kernels  10.2 us (10%)
  other arithmetic  1.53 us (1%)
    all_to_all x3, starting transfers between devices, exchange(): lax.all_to_all(x, axes, split_axis=0, concat_axis=0, tiled=True, axis_ind...  34.9 us
    all_to_all x2, blocking collectives, exchange(): lax.all_to_all(x, axes, split_axis=0, concat_axis=0, tiled=True, axis_ind...  31.1 us
    ppermute x4, starting transfers between devices, lane_swap(): return lax.ppermute(x, 'dp', [(i, i ^ mask) for i in range(LANES)])  11.6 us
    ppermute x4, waiting for transfers between devices, lane_swap(): return lax.ppermute(x, 'dp', [(i, i ^ mask) for i in range(LANES)])  7.61 us
    all_to_all x3, waiting for transfers between devices, exchange(): lax.all_to_all(x, axes, split_axis=0, concat_axis=0, tiled=True, axis_ind...  5.67 us
    pallas_call x1, Pallas kernels, body(): pl.pallas_call(statistics, out_shape=(jax.ShapeDtypeStruct(left_stat.shap...  2.18 us
  transfers between devices with their start and end apart: 7, of which 6 were waited for; matrix products, arithmetic and copies ran while one was open for 1% of the time, Pallas kernels for 4%

profile of v5, /device:TPU:1, one launch (start us, length us, event | category | flops | bytes accessed | tf_op | source)
XLA Modules:
  0.0 104.0 jit_solution(1717257708071566685)
XLA Ops:
  0.6 1.9 %split_columns.1 = bf16[4,128,4,128]{3,2,1,0:T(4,128)(2,1)} custom-call(bf16[128,4,512]{2,1,0:T(4,128)(2,1)} %bitcast.17), custom_call_target="tpu_custom_call" | custom-call | tf_op jit(solution)/shard_map/split_columns/pallas_call | solution.py:279
  2.5 0.0 copy-start
  2.5 0.0 copy-start.1
  2.5 7.2 %all-to-all-start = ((bf16[4,128,4,128]{3,2,1,0:T(4,128)(2,1)}), bf16[4,128,4,128]{3,2,1,0:T(4,128)(2,1)S(1)}, u32[]{:S(2)}, u32[]{:S(2)}) async-start(bf16[4,128,4,128]{3,2,1,0:T(4,128)(2,1)} %split_columns.1), calls=%async_computation | async-start | bytes 1048576 | tf_op jit(solution)/shard_map/all_to_all | solution.py:260
  9.7 0.0 copy-done
  9.7 0.0 copy-done.1
  9.7 2.0 %collective-permute-start = (bf16[1,128,128]{2,1,0:T(8,128)(2,1)S(1)}, bf16[1,128,128]{2,1,0:T(8,128)(2,1)S(1)}, u32[]{:S(2)}, u32[]{:S(2)}) collective-permute-start(bf16[1,128,128]{2,1,0:T(8,128)(2,1)S(1)} %get-tuple-element.28), channel_id=1, source_target_pairs={{0,256},{128,384},{256,0},{384,128},{1,257},{129,385},{257,1},{385... | collective-permute-start | bytes 98312 | tf_op jit(solution)/shard_map/ppermute | solution.py:256
  11.7 0.0 copy-start.4
  11.7 0.6 copy-done.4
  12.4 0.2 convert_reduce_fusion
  12.6 0.6 fusion.4
  13.2 0.7 all-to-all-done.terms_ref
  13.9 1.6 %sum_and_place.1 = bf16[256,4,128]{2,1,0:T(4,128)(2,1)} custom-call(s32[128]{0:T(128)S(1)} %get-tuple-element.45.place_ref, bf16[4,128,4,128]{3,2,1,0:T(4,128)(2,1)S(1)} %all-to-all-done.terms_ref), custom_call_target="tpu_custom_call" | custom-call | tf_op jit(solution)/shard_map/sum_and_place/pallas_call | solution.py:311
  15.5 0.8 collective-permute-done.opposite
  16.3 17.8 %all-to-all-start.1 = ((bf16[16,64,128]{2,1,0:T(8,128)(2,1)}), bf16[16,64,128]{2,1,0:T(8,128)(2,1)S(1)}, u32[]{:S(2)}, u32[]{:S(2)}) async-start(bf16[16,64,128]{2,1,0:T(8,128)(2,1)} %bitcast.3), calls=%async_computation.1 | async-start | bytes 524288 | tf_op jit(solution)/shard_map/all_to_all | solution.py:260
  34.0 2.4 %collective-permute-start.1 = (bf16[6,128,128]{2,1,0:T(8,128)(2,1)S(1)}, bf16[6,128,128]{2,1,0:T(8,128)(2,1)S(1)}, u32[]{:S(2)}, u32[]{:S(2)}) collective-permute-start(bf16[6,128,128]{2,1,0:T(8,128)(2,1)S(1)} %get-tuple-element.30), channel_id=1, source_target_pairs={{0,128},{128,0},{256,384},{384,256},{1,129},{129,1},{257,385},{385... | collective-permute-start | bytes 589832 | tf_op jit(solution)/shard_map/ppermute | solution.py:256
  36.4 4.3 %collective-permute-start.2 = (bf16[2,128,128]{2,1,0:T(8,128)(2,1)S(1)}, bf16[2,128,128]{2,1,0:T(8,128)(2,1)S(1)}, u32[]{:S(2)}, u32[]{:S(2)}) collective-permute-start(bf16[2,128,128]{2,1,0:T(8,128)(2,1)S(1)} %get-tuple-element.31), channel_id=1, source_target_pairs={{0,384},{128,256},{256,128},{384,0},{1,385},{129,257},{257,129},{3... | collective-permute-start | bytes 196616 | tf_op jit(solution)/shard_map/ppermute | solution.py:256
  40.7 2.2 %collective-permute-done.2.across = bf16[2,128,128]{2,1,0:T(8,128)(2,1)S(1)} collective-permute-done((bf16[2,128,128]{2,1,0:T(8,128)(2,1)S(1)}, bf16[2,128,128]{2,1,0:T(8,128)(2,1)S(1)}, u32[]{:S(2)}, u32[]{:S(2)}) %collective-permute-start.2) | collective-permute-done | bytes 65568 | tf_op jit(solution)/shard_map/ppermute | solution.py:256
  42.9 0.0 collective-permute-done.1.beside
  43.0 2.7 %all-to-all-done.1 = bf16[16,64,128]{2,1,0:T(8,128)(2,1)S(1)} async-done(((bf16[16,64,128]{2,1,0:T(8,128)(2,1)}), bf16[16,64,128]{2,1,0:T(8,128)(2,1)S(1)}, u32[]{:S(2)}, u32[]{:S(2)}) %all-to-all-start.1) | async-done | bytes 262176 | tf_op jit(solution)/shard_map/all_to_all | solution.py:260
  45.6 0.8 fan_out.1
  46.4 18.4 %all_to_all.25 = bf16[32,64,128]{2,1,0:T(8,128)(2,1)S(1)} all-to-all(bf16[32,64,128]{2,1,0:T(8,128)(2,1)S(1)} %bitcast.12), channel_id=1, replica_groups={{260,261,262,263,256,257,258,259,388,389,390,391,384,385,386,387,4,5,6,..., dimensions={0} | all-to-all | bytes 1048576 | tf_op jit(solution)/shard_map/all_to_all | solution.py:260
  64.8 1.5 %precondition.1 = (bf16[512,512]{1,0:T(8,128)(2,1)S(1)}, bf16[32,5,8,128]{3,2,1,0:T(8,128)(2,1)S(1)}, bf16[2,128,512]{2,1,0:T(8,128)(2,1)S(1)}) custom-call(s32[1]{0:T(128)} %bitcast.lane_ref, bf16[4,8,8,8,128]{4,3,2,1,0:T(8,128)(2,1)S(1)} %bitcast.11, bf16[2,128,512]{2,1,0:T(8,128)(2,1)S(1)} %copy-done, bf16[2,128,512]{2,1,0:T(8,128)(2,1)S(1)} %copy-done.1, ...), custom_call_target="tpu_custom_call" | custom-call | tf_op jit(solution)/shard_map/precondition/pallas_call | solution.py:343
  66.3 12.7 %all_to_all.26 = bf16[32,40,128]{2,1,0:T(8,128)(2,1)S(1)} all-to-all(bf16[32,40,128]{2,1,0:T(8,128)(2,1)S(1)} %bitcast.16), channel_id=1, replica_groups={{260,261,262,263,256,257,258,259,388,389,390,391,384,385,386,387,4,5,6,..., dimensions={0} | all-to-all | bytes 655360 | tf_op jit(solution)/shard_map/all_to_all | solution.py:260
  79.0 0.9 graft.1
  79.9 9.9 %all-to-all-start.4 = ((bf16[16,64,128]{2,1,0:T(8,128)(2,1)}), bf16[16,64,128]{2,1,0:T(8,128)(2,1)S(1)}, u32[]{:S(2)}, u32[]{:S(2)}) async-start(bf16[16,64,128]{2,1,0:T(8,128)(2,1)} %bitcast.9), calls=%async_computation.4 | async-start | bytes 524288 | tf_op jit(solution)/shard_map/all_to_all | solution.py:260
  89.8 2.9 %collective-permute-start.3 = (bf16[2,128,512]{2,1,0:T(8,128)(2,1)S(1)}, bf16[2,128,512]{2,1,0:T(8,128)(2,1)S(1)}, u32[]{:S(2)}, u32[]{:S(2)}) collective-permute-start(bf16[2,128,512]{2,1,0:T(8,128)(2,1)S(1)} %get-tuple-element.41), channel_id=1, source_target_pairs={{0,128},{128,0},{256,384},{384,256},{1,129},{129,1},{257,385},{385... | collective-permute-start | bytes 786440 | tf_op jit(solution)/shard_map/ppermute | solution.py:256
  92.7 0.7 pad_add_fusion.info_ref
  93.5 4.7 %collective-permute-done.3.grams_ref = bf16[2,128,512]{2,1,0:T(8,128)(2,1)S(1)} collective-permute-done((bf16[2,128,512]{2,1,0:T(8,128)(2,1)S(1)}, bf16[2,128,512]{2,1,0:T(8,128)(2,1)S(1)}, u32[]{:S(2)}, u32[]{:S(2)}) %collective-permute-start.3) | collective-permute-done | bytes 262176 | tf_op jit(solution)/shard_map/ppermute | solution.py:256
  98.1 2.2 %statistics.1 = (f32[2,128,512]{2,1,0:T(8,128)}, f32[2,128,512]{2,1,0:T(8,128)}) custom-call(s32[2]{0:T(128)S(1)} %pad_add_fusion.info_ref, bf16[512,512]{1,0:T(8,128)(2,1)S(1)} %get-tuple-element.40.block, bf16[2,128,512]{2,1,0:T(8,128)(2,1)S(1)} %collective-permute-done.3.grams_ref, f32[2,128,512]{2,1,0:T(8,128)S(1)} %copy-done.2, f32[2,128,512]{2,1,0:T(8,128)S(1)} %copy-done.3), custom_call_target="tpu_custom_call" | custom-call | flops 1 | bytes 1 | tf_op jit(solution)/shard_map/statistics/pallas_call | solution.py:374
  100.3 2.3 %all-to-all-done.4 = bf16[16,64,128]{2,1,0:T(8,128)(2,1)S(1)} async-done(((bf16[16,64,128]{2,1,0:T(8,128)(2,1)}), bf16[16,64,128]{2,1,0:T(8,128)(2,1)S(1)}, u32[]{:S(2)}, u32[]{:S(2)}) %all-to-all-start.4) | async-done | bytes 262176 | tf_op jit(solution)/shard_map/all_to_all | solution.py:260
  102.6 1.4 %take_cells.1 = bf16[128,4,128]{2,1,0:T(4,128)(2,1)} custom-call(s32[128]{0:T(128)S(1)} %get-tuple-element.45.place_ref, bf16[256,4,128]{2,1,0:T(4,128)(2,1)S(1)} %bitcast.15), custom_call_target="tpu_custom_call" | custom-call | tf_op jit(solution)/shard_map/take_cells/pallas_call | solution.py:392
  (5 shorter events, 0.1 us)
Async XLA Ops:
  2.5 7.2 %copy-start = (bf16[2,128,512]{2,1,0:T(8,128)(2,1)S(1)}, bf16[2,128,512]{2,1,0:T(8,128)(2,1)}, u32[]{:S(2)}) copy-start(bf16[2,128,512]{2,1,0:T(8,128)(2,1)} %left_hbm.2) | copy-start | bytes 786436
  2.5 7.2 %copy-start.1 = (bf16[2,128,512]{2,1,0:T(8,128)(2,1)S(1)}, bf16[2,128,512]{2,1,0:T(8,128)(2,1)}, u32[]{:S(2)}) copy-start(bf16[2,128,512]{2,1,0:T(8,128)(2,1)} %right_hbm.2) | copy-start | bytes 786436
  2.5 11.4 %all-to-all-start = ((bf16[4,128,4,128]{3,2,1,0:T(4,128)(2,1)}), bf16[4,128,4,128]{3,2,1,0:T(4,128)(2,1)S(1)}, u32[]{:S(2)}, u32[]{:S(2)}) async-start(bf16[4,128,4,128]{3,2,1,0:T(4,128)(2,1)} %split_columns.1), calls=%async_computation | async-start | bytes 1048576 | tf_op jit(solution)/shard_map/all_to_all | solution.py:260
  9.7 6.5 %collective-permute-start = (bf16[1,128,128]{2,1,0:T(8,128)(2,1)S(1)}, bf16[1,128,128]{2,1,0:T(8,128)(2,1)S(1)}, u32[]{:S(2)}, u32[]{:S(2)}) collective-permute-start(bf16[1,128,128]{2,1,0:T(8,128)(2,1)S(1)} %get-tuple-element.28), channel_id=1, source_target_pairs={{0,256},{128,384},{256,0},{384,128},{1,257},{129,385},{257,1},{385... | collective-permute-start | bytes 98312 | tf_op jit(solution)/shard_map/ppermute | solution.py:256
  11.7 0.7 copy-start.4
  16.3 29.4 %all-to-all-start.1 = ((bf16[16,64,128]{2,1,0:T(8,128)(2,1)}), bf16[16,64,128]{2,1,0:T(8,128)(2,1)S(1)}, u32[]{:S(2)}, u32[]{:S(2)}) async-start(bf16[16,64,128]{2,1,0:T(8,128)(2,1)} %bitcast.3), calls=%async_computation.1 | async-start | bytes 524288 | tf_op jit(solution)/shard_map/all_to_all | solution.py:260
  34.0 8.9 %collective-permute-start.1 = (bf16[6,128,128]{2,1,0:T(8,128)(2,1)S(1)}, bf16[6,128,128]{2,1,0:T(8,128)(2,1)S(1)}, u32[]{:S(2)}, u32[]{:S(2)}) collective-permute-start(bf16[6,128,128]{2,1,0:T(8,128)(2,1)S(1)} %get-tuple-element.30), channel_id=1, source_target_pairs={{0,128},{128,0},{256,384},{384,256},{1,129},{129,1},{257,385},{385... | collective-permute-start | bytes 589832 | tf_op jit(solution)/shard_map/ppermute | solution.py:256
  36.4 6.5 %collective-permute-start.2 = (bf16[2,128,128]{2,1,0:T(8,128)(2,1)S(1)}, bf16[2,128,128]{2,1,0:T(8,128)(2,1)S(1)}, u32[]{:S(2)}, u32[]{:S(2)}) collective-permute-start(bf16[2,128,128]{2,1,0:T(8,128)(2,1)S(1)} %get-tuple-element.31), channel_id=1, source_target_pairs={{0,384},{128,256},{256,128},{384,0},{1,385},{129,257},{257,129},{3... | collective-permute-start | bytes 196616 | tf_op jit(solution)/shard_map/ppermute | solution.py:256
  79.0 19.1 %copy-start.2 = (f32[2,128,512]{2,1,0:T(8,128)S(1)}, f32[2,128,512]{2,1,0:T(8,128)}, u32[]{:S(2)}) copy-start(f32[2,128,512]{2,1,0:T(8,128)} %left_hbm.3) | copy-start | bytes 1572868
  79.0 19.1 %copy-start.3 = (f32[2,128,512]{2,1,0:T(8,128)S(1)}, f32[2,128,512]{2,1,0:T(8,128)}, u32[]{:S(2)}) copy-start(f32[2,128,512]{2,1,0:T(8,128)} %right_hbm.3) | copy-start | bytes 1572868
  79.9 22.7 %all-to-all-start.4 = ((bf16[16,64,128]{2,1,0:T(8,128)(2,1)}), bf16[16,64,128]{2,1,0:T(8,128)(2,1)S(1)}, u32[]{:S(2)}, u32[]{:S(2)}) async-start(bf16[16,64,128]{2,1,0:T(8,128)(2,1)} %bitcast.9), calls=%async_computation.4 | async-start | bytes 524288 | tf_op jit(solution)/shard_map/all_to_all | solution.py:260
  89.8 8.3 %collective-permute-start.3 = (bf16[2,128,512]{2,1,0:T(8,128)(2,1)S(1)}, bf16[2,128,512]{2,1,0:T(8,128)(2,1)S(1)}, u32[]{:S(2)}, u32[]{:S(2)}) collective-permute-start(bf16[2,128,512]{2,1,0:T(8,128)(2,1)S(1)} %get-tuple-element.41), channel_id=1, source_target_pairs={{0,128},{128,0},{256,384},{384,256},{1,129},{129,1},{257,385},{385... | collective-permute-start | bytes 786440 | tf_op jit(solution)/shard_map/ppermute | solution.py:256

commit v6 on v5

--- a/solution.py
+++ b/solution.py
@@ -81,11 +81,6 @@
         copy.wait()
 
 
-def two_terms(value):
-    high = value.astype(jnp.bfloat16).astype(jnp.float32)
-    return high, jnp.where(high < jnp.inf, value - high, 0.0)
-
-
 def paired(first, second):
     upper = lax.broadcasted_iota(jnp.int32, first.shape, first.ndim - 2) < 4
     return (
@@ -109,17 +104,17 @@
         columns = pl.ds(pl.multiple_of(lane_of_columns * quarter, quarter), quarter)
         return ref[slot, :, columns]
 
-    for i, column in enumerate((lane, lane ^ 3, lane ^ 2)):
-        beside_ref[i] = block(right_ref, 1 - parity, column)
-        beside_ref[3 + i] = block(left_ref, 1 - parity, column)
-    across_ref[0] = block(right_ref, 1 - parity, lane)
-    across_ref[1] = block(right_ref, 1 - parity, lane ^ 1)
-    opposite_ref[0] = block(right_ref, parity, lane)
+    for side, ref in enumerate((left_ref, right_ref)):
+        for i, column in enumerate((lane, lane ^ 3, lane ^ 2)):
+            beside_ref[3 * side + i] = block(ref, 1 - parity, column)
+        for i, column in enumerate((lane, lane ^ 1)):
+            across_ref[2 * side + i] = block(ref, 1 - parity, column)
+        opposite_ref[side] = block(ref, parity, lane)
 
 
 def precondition(
     lane_ref, pieces, left_hbm, right_hbm, beside, across, opposite, grads_ref, out_ref, grams_ref,
-    lefts, rights, sems,
+    lefts, rights, own, sems,
 ):
     lane = lane_ref[0]
     parity = lax.rem(lane, 2)
@@ -130,8 +125,8 @@
         return pl.ds(pl.multiple_of(x * quarter, quarter), quarter)
 
     copies = [
-        pltpu.make_async_copy(left_hbm.at[parity], lefts.at[rows_of(parity)], sems.at[0]),
-        pltpu.make_async_copy(right_hbm.at[parity], rights.at[rows_of(lane)], sems.at[1]),
+        pltpu.make_async_copy(left_hbm.at[parity], own.at[0], sems.at[0]),
+        pltpu.make_async_copy(right_hbm.at[parity], own.at[1], sems.at[1]),
     ]
     for copy in copies:
         copy.start()
@@ -152,74 +147,50 @@
         grads_ref[:, source * quarter : (source + 1) * quarter] = flat
     for copy in copies:
         copy.wait()
-    side, far, last = lane ^ 1, lane ^ 3, lane ^ 2
-
-    def put(row, column, block):
-        rights[rows_of(row), rows_of(column)] = block
-        if row is not column:
-            rights[rows_of(column), rows_of(row)] = block.T
-
-    for other in (side, far, last):
-        rights[rows_of(other), rows_of(lane)] = rights[rows_of(lane), rows_of(other)].T
-    put(side, side, beside[0])
-    put(side, last, beside[1])
-    put(side, far, beside[2])
-    put(far, far, across[0])
-    put(far, last, across[1])
-    put(last, last, opposite[0])
-    below = rows_of(1 - parity)
-    lefts[below, rows_of(lane)] = lefts[rows_of(parity), rows_of(side)].T
-    for i, column in enumerate((side, last, far)):
-        lefts[below, rows_of(column)] = beside[3 + i]
+    beyond, far, last = lane ^ 1, lane ^ 3, lane ^ 2
+    turn = lane & 2
+
+    for side, (target, mask) in enumerate(((lefts, 0), (rights, turn))):
+
+        def put(row, column, block):
+            target[rows_of(row), rows_of(column ^ mask)] = block
+            if row is not column:
+                target[rows_of(column), rows_of(row ^ mask)] = block.T
+
+        put(lane, lane, own[side, :, rows_of(lane)])
+        for other in (beyond, far, last):
+            put(lane, other, own[side, :, rows_of(other)])
+        put(beyond, beyond, beside[3 * side])
+        put(beyond, last, beside[3 * side + 1])
+        put(beyond, far, beside[3 * side + 2])
+        put(far, far, across[2 * side])
+        put(far, last, across[2 * side + 1])
+        put(last, last, opposite[side])
     half = jnp.dot(lefts[...], grads_ref[...], preferred_element_type=jnp.float32)
     product = jnp.dot(
         half.astype(jnp.bfloat16), rights[...], preferred_element_type=jnp.float32
     )
     prod_sq = jnp.sum(jnp.sum(product * product, axis=0, keepdims=True), axis=1, keepdims=True)
-    rows = lax.broadcasted_iota(jnp.int32, (8, quarter), 0)
-    tail = jnp.zeros((8, quarter), jnp.float32)
-    for r, value in enumerate((*two_terms(prod_sq), *two_terms(square))):
-        tail = jnp.where(rows == r, value, tail)
-    tail = tail.astype(out_ref.dtype)
-    pairs = out_ref.shape[1] - 1
-    for i, target in enumerate(LANE_ORDER):
-        block = product[:, target * quarter : (target + 1) * quarter]
+    cells = float(width * width)
+    ratio = jnp.sqrt(square / cells) / jnp.sqrt(prod_sq / cells + epsilon)
+    pairs = out_ref.shape[1]
+    for i in range(2):
+        block = product[:, i * quarter : (i + 1) * quarter] * ratio
         block = block.reshape(pairs, 2, COLUMNS, 8, quarter)
         for j, y in enumerate(COLUMN_ORDER):
             for core, value in enumerate(paired(block[:, 0, y], block[:, 1, y])):
-                seat = i * SEATS + j * CORES + core
-                out_ref[seat, pl.ds(0, pairs)] = value.astype(out_ref.dtype)
-                out_ref[seat, pairs] = tail
+                out_ref[i * SEATS + j * CORES + core] = value.astype(out_ref.dtype)
     for side in range(2):
         grams_ref[side] = gram_rows(grads_ref, side, rows_of(lane ^ 1)).astype(grams_ref.dtype)
 
 
-def graft(x_ref, out_ref):
-    quarter = out_ref.shape[3]
-    pairs = x_ref.shape[1] - 1
-    cells = float((LANES * quarter) ** 2)
+def regroup(x_ref, out_ref):
     for j, seat in enumerate(SEAT_ORDER):
-        ratios = []
-        for slot in range(2):
-            upper, lower = [
-                x_ref[LANE_ORDER.index(2 * half + slot) * SEATS + j, pairs].astype(jnp.float32)
-                for half in range(2)
-            ]
-            total = upper + lower
-            prod_sq = total[0:1] + total[1:2]
-            grad_sq = upper[2:3] + upper[3:4]
-            ratios.append(jnp.sqrt(grad_sq / cells) / jnp.sqrt(prod_sq / cells + epsilon))
-        for half in range(2):
-            scaled = []
-            for slot in range(2):
-                member = LANE_ORDER.index(2 * half + slot) * SEATS + j
-                value = x_ref[member, pl.ds(0, pairs)].astype(jnp.float32)
-                scaled.append(value * ratios[slot])
-            for odd, value in enumerate(paired(*scaled)):
-                for p in range(pairs):
-                    plane = half * (PLANES // 2) + 2 * p + odd
-                    place = (plane - FIRST_PLANE) % PLANES
-                    out_ref[place, seat] = value[p].astype(out_ref.dtype)
+        tiles = [x_ref[slot * SEATS + j].astype(jnp.float32) for slot in range(2)]
+        for odd, value in enumerate(paired(*tiles)):
+            for p in range(value.shape[0]):
+                place = (2 * p + odd - FIRST_PLANE) % PLANES
+                out_ref[place, seat] = value[p].astype(out_ref.dtype)
 
 
 def statistics(
@@ -276,6 +247,12 @@
         for z in range(PLANES)
     ]
 
+    half_groups = [
+        [x * owners + z * SEATS + seat for x in (half, half + 1) for seat in SEAT_ORDER]
+        for half in (0, 2)
+        for z in range(PLANES)
+    ]
+
     terms = pl.pallas_call(
         split_columns,
         out_shape=jax.ShapeDtypeStruct((LANES, blocks, rows, quarter), jnp.bfloat16),
@@ -293,7 +270,7 @@
     terms = exchange(terms, "dp", lane_groups)
     picked = pl.pallas_call(
         pick_blocks,
-        out_shape=[jax.ShapeDtypeStruct((n, quarter, quarter), jnp.bfloat16) for n in (6, 2, 1)],
+        out_shape=[jax.ShapeDtypeStruct((n, quarter, quarter), jnp.bfloat16) for n in (6, 4, 2)],
         in_specs=[SMEM, VMEM, VMEM],
         out_specs=[VMEM] * 3,
         compiler_params=PARAMS,
@@ -339,34 +316,36 @@
     pieces = exchange(copies.reshape(members, PLANES * rows, quarter), ("dp", "own"), flat_groups)
     pieces = pieces.reshape(LANES, SEATS, PLANES // 2, 2 * rows, quarter)
 
-    near = PLANES // 4 + 1
     grads, product, grams = pl.pallas_call(
         precondition,
         out_shape=(
             jax.ShapeDtypeStruct((width, width), jnp.bfloat16),
-            jax.ShapeDtypeStruct((members, near, tile, quarter), jnp.bfloat16),
+            jax.ShapeDtypeStruct((members // 2, PLANES // 2, tile, quarter), jnp.bfloat16),
             jax.ShapeDtypeStruct((2, quarter, width), jnp.bfloat16),
         ),
         in_specs=[SMEM, VMEM, ANY, ANY, VMEM, VMEM, VMEM],
         out_specs=(VMEM, VMEM, VMEM),
         scratch_shapes=[
-            pltpu.VMEM((width // 2, width), jnp.bfloat16),
             pltpu.VMEM((width, width), jnp.bfloat16),
+            pltpu.VMEM((width, width), jnp.bfloat16),
+            pltpu.VMEM((2, quarter, width), jnp.bfloat16),
             pltpu.SemaphoreType.DMA((2,)),
         ],
         compiler_params=PARAMS,
         name="precondition",
     )(lane.reshape(1), pieces, left_root, right_root, beside, across, opposite)
-    product = exchange(product.reshape(members, near * tile, quarter), ("dp", "own"), flat_groups)
+    product = exchange(
+        product.reshape(members // 2, PLANES // 2 * tile, quarter), ("dp", "own"), half_groups
+    )
 
     scaled = pl.pallas_call(
-        graft,
+        regroup,
         out_shape=jax.ShapeDtypeStruct((PLANES, SEATS, tile, quarter), jnp.bfloat16),
         in_specs=[VMEM],
         out_specs=VMEM,
         compiler_params=PARAMS,
-        name="graft",
-    )(product.reshape(members, near, tile, quarter))
+        name="regroup",
+    )(product.reshape(members // 2, PLANES // 2, tile, quarter))
     grads, grams, scaled = lax.optimization_barrier((grads, grams, scaled))
     returned = exchange(scaled.reshape(PLANES, SEATS * tile, quarter), "own", plane_groups)
 

time: 105 us -> 105 us (level)
  waiting for transfers between devices: 13.3 us -> 15 us
  blocking collectives: 31.1 us -> 29.9 us
    ppermute x4, waiting for transfers between devices: 7.61 us -> 10.5 us  [lane_swap(): return lax.ppermute(x, 'dp', [(i, i ^ mask) for i in range(LANES)])]
    all_to_all x3, waiting for transfers between devices: 5.67 us -> 4.45 us  [exchange(): lax.all_to_all(x, axes, split_axis=0, concat_axis=0, tiled=True, axis_ind...]
    all_to_all x2, blocking collectives: 31.1 us -> 29.9 us  [exchange(): lax.all_to_all(x, axes, split_axis=0, concat_axis=0, tiled=True, axis_ind...]
where the time goes in v6:
time: 105 us; the launch traced here: 104 us
  starting transfers between devices  45.7 us (44%)
  blocking collectives  29.9 us (28%)
  waiting for transfers between devices  15 us (14%)
  Pallas kernels  10.4 us (10%)
  other arithmetic  1.53 us (1%)
    all_to_all x3, starting transfers between devices, exchange(): lax.all_to_all(x, axes, split_axis=0, concat_axis=0, tiled=True, axis_ind...  34.8 us
    all_to_all x2, blocking collectives, exchange(): lax.all_to_all(x, axes, split_axis=0, concat_axis=0, tiled=True, axis_ind...  29.9 us
    ppermute x4, starting transfers between devices, lane_swap(): return lax.ppermute(x, 'dp', [(i, i ^ mask) for i in range(LANES)])  11 us
    ppermute x4, waiting for transfers between devices, lane_swap(): return lax.ppermute(x, 'dp', [(i, i ^ mask) for i in range(LANES)])  10.5 us
    all_to_all x3, waiting for transfers between devices, exchange(): lax.all_to_all(x, axes, split_axis=0, concat_axis=0, tiled=True, axis_ind...  4.45 us
    pallas_call x1, Pallas kernels, body(): pl.pallas_call(statistics, out_shape=(jax.ShapeDtypeStruct(left_stat.shap...  2.18 us
  transfers between devices with their start and end apart: 7, of which 6 were waited for; matrix products, arithmetic and copies ran while one was open for 1% of the time, Pallas kernels for 4%

profile of v6, /device:TPU:1, one launch (start us, length us, event | category | flops | bytes accessed | tf_op | source)
XLA Modules:
  0.0 104.0 jit_solution(7090222845036467170)
XLA Ops:
  0.6 1.9 %split_columns.1 = bf16[4,128,4,128]{3,2,1,0:T(4,128)(2,1)} custom-call(bf16[128,4,512]{2,1,0:T(4,128)(2,1)} %bitcast.17), custom_call_target="tpu_custom_call" | custom-call | tf_op jit(solution)/shard_map/split_columns/pallas_call | solution.py:256
  2.5 0.0 copy-start
  2.5 0.0 copy-start.1
  2.5 7.2 %all-to-all-start = ((bf16[4,128,4,128]{3,2,1,0:T(4,128)(2,1)}), bf16[4,128,4,128]{3,2,1,0:T(4,128)(2,1)S(1)}, u32[]{:S(2)}, u32[]{:S(2)}) async-start(bf16[4,128,4,128]{3,2,1,0:T(4,128)(2,1)} %split_columns.1), calls=%async_computation | async-start | bytes 1048576 | tf_op jit(solution)/shard_map/all_to_all | solution.py:231
  9.7 0.0 copy-done
  9.7 0.1 pick_blocks.1
  9.8 2.0 %collective-permute-start = (bf16[2,128,128]{2,1,0:T(8,128)(2,1)S(1)}, bf16[2,128,128]{2,1,0:T(8,128)(2,1)S(1)}, u32[]{:S(2)}, u32[]{:S(2)}) collective-permute-start(bf16[2,128,128]{2,1,0:T(8,128)(2,1)S(1)} %get-tuple-element.28), channel_id=1, source_target_pairs={{0,256},{128,384},{256,0},{384,128},{1,257},{129,385},{257,1},{385... | collective-permute-start | bytes 196616 | tf_op jit(solution)/shard_map/ppermute | solution.py:227
  11.7 0.0 copy-start.4
  11.8 0.6 copy-done.4
  12.4 0.2 convert_reduce_fusion
  12.6 0.6 fusion.4
  13.2 0.8 all-to-all-done.terms_ref
  14.1 1.6 %sum_and_place.1 = bf16[256,4,128]{2,1,0:T(4,128)(2,1)} custom-call(s32[128]{0:T(128)S(1)} %get-tuple-element.45.place_ref, bf16[4,128,4,128]{3,2,1,0:T(4,128)(2,1)S(1)} %all-to-all-done.terms_ref), custom_call_target="tpu_custom_call" | custom-call | tf_op jit(solution)/shard_map/sum_and_place/pallas_call | solution.py:288
  15.6 1.3 %collective-permute-done.opposite = bf16[2,128,128]{2,1,0:T(8,128)(2,1)S(1)} collective-permute-done((bf16[2,128,128]{2,1,0:T(8,128)(2,1)S(1)}, bf16[2,128,128]{2,1,0:T(8,128)(2,1)S(1)}, u32[]{:S(2)}, u32[]{:S(2)}) %collective-permute-start) | collective-permute-done | bytes 65568 | tf_op jit(solution)/shard_map/ppermute | solution.py:227
  17.0 17.1 %all-to-all-start.1 = ((bf16[16,64,128]{2,1,0:T(8,128)(2,1)}), bf16[16,64,128]{2,1,0:T(8,128)(2,1)S(1)}, u32[]{:S(2)}, u32[]{:S(2)}) async-start(bf16[16,64,128]{2,1,0:T(8,128)(2,1)} %bitcast.3), calls=%async_computation.1 | async-start | bytes 524288 | tf_op jit(solution)/shard_map/all_to_all | solution.py:231
  34.0 2.4 %collective-permute-start.1 = (bf16[6,128,128]{2,1,0:T(8,128)(2,1)S(1)}, bf16[6,128,128]{2,1,0:T(8,128)(2,1)S(1)}, u32[]{:S(2)}, u32[]{:S(2)}) collective-permute-start(bf16[6,128,128]{2,1,0:T(8,128)(2,1)S(1)} %get-tuple-element.30), channel_id=1, source_target_pairs={{0,128},{128,0},{256,384},{384,256},{1,129},{129,1},{257,385},{385... | collective-permute-start | bytes 589832 | tf_op jit(solution)/shard_map/ppermute | solution.py:227
  36.4 4.3 %collective-permute-start.2 = (bf16[4,128,128]{2,1,0:T(8,128)(2,1)S(1)}, bf16[4,128,128]{2,1,0:T(8,128)(2,1)S(1)}, u32[]{:S(2)}, u32[]{:S(2)}) collective-permute-start(bf16[4,128,128]{2,1,0:T(8,128)(2,1)S(1)} %get-tuple-element.31), channel_id=1, source_target_pairs={{0,384},{128,256},{256,128},{384,0},{1,385},{129,257},{257,129},{3... | collective-permute-start | bytes 393224 | tf_op jit(solution)/shard_map/ppermute | solution.py:227
  40.7 2.9 %collective-permute-done.2.across = bf16[4,128,128]{2,1,0:T(8,128)(2,1)S(1)} collective-permute-done((bf16[4,128,128]{2,1,0:T(8,128)(2,1)S(1)}, bf16[4,128,128]{2,1,0:T(8,128)(2,1)S(1)}, u32[]{:S(2)}, u32[]{:S(2)}) %collective-permute-start.2) | collective-permute-done | bytes 131104 | tf_op jit(solution)/shard_map/ppermute | solution.py:227
  43.6 0.0 collective-permute-done.1.beside
  43.7 1.1 %all-to-all-done.1 = bf16[16,64,128]{2,1,0:T(8,128)(2,1)S(1)} async-done(((bf16[16,64,128]{2,1,0:T(8,128)(2,1)}), bf16[16,64,128]{2,1,0:T(8,128)(2,1)S(1)}, u32[]{:S(2)}, u32[]{:S(2)}) %all-to-all-start.1) | async-done | bytes 262176 | tf_op jit(solution)/shard_map/all_to_all | solution.py:231
  44.7 0.8 fan_out.1
  45.5 19.4 %all_to_all.25 = bf16[32,64,128]{2,1,0:T(8,128)(2,1)S(1)} all-to-all(bf16[32,64,128]{2,1,0:T(8,128)(2,1)S(1)} %bitcast.12), channel_id=1, replica_groups={{260,261,262,263,256,257,258,259,388,389,390,391,384,385,386,387,4,5,6,..., dimensions={0} | all-to-all | bytes 1048576 | tf_op jit(solution)/shard_map/all_to_all | solution.py:231
  64.9 1.7 %precondition.1 = (bf16[512,512]{1,0:T(8,128)(2,1)S(1)}, bf16[16,8,8,128]{3,2,1,0:T(8,128)(2,1)S(1)}, bf16[2,128,512]{2,1,0:T(8,128)(2,1)S(1)}) custom-call(s32[1]{0:T(128)} %bitcast.lane_ref, bf16[4,8,8,8,128]{4,3,2,1,0:T(8,128)(2,1)S(1)} %bitcast.11, bf16[2,128,512]{2,1,0:T(8,128)(2,1)S(1)} %copy-done, bf16[2,128,512]{2,1,0:T(8,128)(2,1)S(1)} %copy-done.1, ...), custom_call_target="tpu_custom_call" | custom-call | tf_op jit(solution)/shard_map/precondition/pallas_call | solution.py:319
  66.6 10.6 %all_to_all.26 = bf16[16,64,128]{2,1,0:T(8,128)(2,1)S(1)} all-to-all(bf16[16,64,128]{2,1,0:T(8,128)(2,1)S(1)} %bitcast.16), channel_id=1, replica_groups={{4,5,6,7,0,1,2,3,132,133,134,135,128,129,130,131},{12,13,14,15,8,9,10,1..., dimensions={0} | all-to-all | bytes 524288 | tf_op jit(solution)/shard_map/all_to_all | solution.py:231
  77.2 0.8 regroup.1
  78.0 10.6 %all-to-all-start.4 = ((bf16[16,64,128]{2,1,0:T(8,128)(2,1)}), bf16[16,64,128]{2,1,0:T(8,128)(2,1)S(1)}, u32[]{:S(2)}, u32[]{:S(2)}) async-start(bf16[16,64,128]{2,1,0:T(8,128)(2,1)} %bitcast.9), calls=%async_computation.4 | async-start | bytes 524288 | tf_op jit(solution)/shard_map/all_to_all | solution.py:231
  88.5 2.3 %collective-permute-start.3 = (bf16[2,128,512]{2,1,0:T(8,128)(2,1)S(1)}, bf16[2,128,512]{2,1,0:T(8,128)(2,1)S(1)}, u32[]{:S(2)}, u32[]{:S(2)}) collective-permute-start(bf16[2,128,512]{2,1,0:T(8,128)(2,1)S(1)} %get-tuple-element.41), channel_id=1, source_target_pairs={{0,128},{128,0},{256,384},{384,256},{1,129},{129,1},{257,385},{385... | collective-permute-start | bytes 786440 | tf_op jit(solution)/shard_map/ppermute | solution.py:227
  90.9 0.7 pad_add_fusion.info_ref
  91.6 6.3 %collective-permute-done.3.grams_ref = bf16[2,128,512]{2,1,0:T(8,128)(2,1)S(1)} collective-permute-done((bf16[2,128,512]{2,1,0:T(8,128)(2,1)S(1)}, bf16[2,128,512]{2,1,0:T(8,128)(2,1)S(1)}, u32[]{:S(2)}, u32[]{:S(2)}) %collective-permute-start.3) | collective-permute-done | bytes 262176 | tf_op jit(solution)/shard_map/ppermute | solution.py:227
  97.9 2.2 %statistics.1 = (f32[2,128,512]{2,1,0:T(8,128)}, f32[2,128,512]{2,1,0:T(8,128)}) custom-call(s32[2]{0:T(128)S(1)} %pad_add_fusion.info_ref, bf16[512,512]{1,0:T(8,128)(2,1)S(1)} %get-tuple-element.40.block, bf16[2,128,512]{2,1,0:T(8,128)(2,1)S(1)} %collective-permute-done.3.grams_ref, f32[2,128,512]{2,1,0:T(8,128)S(1)} %copy-done.2, f32[2,128,512]{2,1,0:T(8,128)S(1)} %copy-done.3), custom_call_target="tpu_custom_call" | custom-call | flops 1 | bytes 1 | tf_op jit(solution)/shard_map/statistics/pallas_call | solution.py:353
  100.1 2.6 %all-to-all-done.4 = bf16[16,64,128]{2,1,0:T(8,128)(2,1)S(1)} async-done(((bf16[16,64,128]{2,1,0:T(8,128)(2,1)}), bf16[16,64,128]{2,1,0:T(8,128)(2,1)S(1)}, u32[]{:S(2)}, u32[]{:S(2)}) %all-to-all-start.4) | async-done | bytes 262176 | tf_op jit(solution)/shard_map/all_to_all | solution.py:231
  102.6 1.4 %take_cells.1 = bf16[128,4,128]{2,1,0:T(4,128)(2,1)} custom-call(s32[128]{0:T(128)S(1)} %get-tuple-element.45.place_ref, bf16[256,4,128]{2,1,0:T(4,128)(2,1)S(1)} %bitcast.14), custom_call_target="tpu_custom_call" | custom-call | tf_op jit(solution)/shard_map/take_cells/pallas_call | solution.py:371
  (5 shorter events, 0.0 us)
Async XLA Ops:
  2.5 7.2 %copy-start = (bf16[2,128,512]{2,1,0:T(8,128)(2,1)S(1)}, bf16[2,128,512]{2,1,0:T(8,128)(2,1)}, u32[]{:S(2)}) copy-start(bf16[2,128,512]{2,1,0:T(8,128)(2,1)} %left_hbm.2) | copy-start | bytes 786436
  2.5 7.2 %copy-start.1 = (bf16[2,128,512]{2,1,0:T(8,128)(2,1)S(1)}, bf16[2,128,512]{2,1,0:T(8,128)(2,1)}, u32[]{:S(2)}) copy-start(bf16[2,128,512]{2,1,0:T(8,128)(2,1)} %right_hbm.2) | copy-start | bytes 786436
  2.5 11.5 %all-to-all-start = ((bf16[4,128,4,128]{3,2,1,0:T(4,128)(2,1)}), bf16[4,128,4,128]{3,2,1,0:T(4,128)(2,1)S(1)}, u32[]{:S(2)}, u32[]{:S(2)}) async-start(bf16[4,128,4,128]{3,2,1,0:T(4,128)(2,1)} %split_columns.1), calls=%async_computation | async-start | bytes 1048576 | tf_op jit(solution)/shard_map/all_to_all | solution.py:231
  9.8 7.2 %collective-permute-start = (bf16[2,128,128]{2,1,0:T(8,128)(2,1)S(1)}, bf16[2,128,128]{2,1,0:T(8,128)(2,1)S(1)}, u32[]{:S(2)}, u32[]{:S(2)}) collective-permute-start(bf16[2,128,128]{2,1,0:T(8,128)(2,1)S(1)} %get-tuple-element.28), channel_id=1, source_target_pairs={{0,256},{128,384},{256,0},{384,128},{1,257},{129,385},{257,1},{385... | collective-permute-start | bytes 196616 | tf_op jit(solution)/shard_map/ppermute | solution.py:227
  11.7 0.7 copy-start.4
  17.0 27.7 %all-to-all-start.1 = ((bf16[16,64,128]{2,1,0:T(8,128)(2,1)}), bf16[16,64,128]{2,1,0:T(8,128)(2,1)S(1)}, u32[]{:S(2)}, u32[]{:S(2)}) async-start(bf16[16,64,128]{2,1,0:T(8,128)(2,1)} %bitcast.3), calls=%async_computation.1 | async-start | bytes 524288 | tf_op jit(solution)/shard_map/all_to_all | solution.py:231
  34.0 9.6 %collective-permute-start.1 = (bf16[6,128,128]{2,1,0:T(8,128)(2,1)S(1)}, bf16[6,128,128]{2,1,0:T(8,128)(2,1)S(1)}, u32[]{:S(2)}, u32[]{:S(2)}) collective-permute-start(bf16[6,128,128]{2,1,0:T(8,128)(2,1)S(1)} %get-tuple-element.30), channel_id=1, source_target_pairs={{0,128},{128,0},{256,384},{384,256},{1,129},{129,1},{257,385},{385... | collective-permute-start | bytes 589832 | tf_op jit(solution)/shard_map/ppermute | solution.py:227
  36.4 7.2 %collective-permute-start.2 = (bf16[4,128,128]{2,1,0:T(8,128)(2,1)S(1)}, bf16[4,128,128]{2,1,0:T(8,128)(2,1)S(1)}, u32[]{:S(2)}, u32[]{:S(2)}) collective-permute-start(bf16[4,128,128]{2,1,0:T(8,128)(2,1)S(1)} %get-tuple-element.31), channel_id=1, source_target_pairs={{0,384},{128,256},{256,128},{384,0},{1,385},{129,257},{257,129},{3... | collective-permute-start | bytes 393224 | tf_op jit(solution)/shard_map/ppermute | solution.py:227
  77.2 20.7 %copy-start.2 = (f32[2,128,512]{2,1,0:T(8,128)S(1)}, f32[2,128,512]{2,1,0:T(8,128)}, u32[]{:S(2)}) copy-start(f32[2,128,512]{2,1,0:T(8,128)} %left_hbm.3) | copy-start | bytes 1572868
  77.2 20.7 %copy-start.3 = (f32[2,128,512]{2,1,0:T(8,128)S(1)}, f32[2,128,512]{2,1,0:T(8,128)}, u32[]{:S(2)}) copy-start(f32[2,128,512]{2,1,0:T(8,128)} %right_hbm.3) | copy-start | bytes 1572868
  78.0 24.6 %all-to-all-start.4 = ((bf16[16,64,128]{2,1,0:T(8,128)(2,1)}), bf16[16,64,128]{2,1,0:T(8,128)(2,1)S(1)}, u32[]{:S(2)}, u32[]{:S(2)}) async-start(bf16[16,64,128]{2,1,0:T(8,128)(2,1)} %bitcast.9), calls=%async_computation.4 | async-start | bytes 524288 | tf_op jit(solution)/shard_map/all_to_all | solution.py:231
  88.5 9.3 %collective-permute-start.3 = (bf16[2,128,512]{2,1,0:T(8,128)(2,1)S(1)}, bf16[2,128,512]{2,1,0:T(8,128)(2,1)S(1)}, u32[]{:S(2)}, u32[]{:S(2)}) collective-permute-start(bf16[2,128,512]{2,1,0:T(8,128)(2,1)S(1)} %get-tuple-element.41), channel_id=1, source_target_pairs={{0,128},{128,0},{256,384},{384,256},{1,129},{129,1},{257,385},{385... | collective-permute-start | bytes 786440 | tf_op jit(solution)/shard_map/ppermute | solution.py:227

commit v7 on v6

--- a/solution.py
+++ b/solution.py
@@ -10,7 +10,6 @@
 
 VMEM = pl.BlockSpec(memory_space=pltpu.VMEM)
 SMEM = pl.BlockSpec(memory_space=pltpu.SMEM)
-ANY = pl.BlockSpec(memory_space=pl.ANY)
 HBM = pl.BlockSpec(memory_space=pltpu.HBM)
 PARAMS = pltpu.CompilerParams(vmem_limit_bytes=40 * 1024 * 1024)
 
@@ -45,17 +44,18 @@
         copy.wait()
 
 
-def sum_and_place(place_ref, terms_ref, out_ref):
+def sum_and_place(cell_ref, terms_ref, out_ref):
     out_ref[...] = jnp.zeros_like(out_ref)
 
-    def step(block, carry):
-        total = terms_ref[0, block].astype(jnp.float32)
+    def step(pair, carry):
+        total = terms_ref[0, pair].astype(jnp.float32)
         for term in range(1, terms_ref.shape[0]):
-            total += terms_ref[term, block].astype(jnp.float32)
-        out_ref[place_ref[block]] = total.astype(out_ref.dtype)
+            total += terms_ref[term, pair].astype(jnp.float32)
+        out_ref[cell_ref[2 * pair]] = total[:4].astype(out_ref.dtype)
+        out_ref[cell_ref[2 * pair + 1]] = total[4:].astype(out_ref.dtype)
         return carry
 
-    lax.fori_loop(0, terms_ref.shape[1], step, 0, unroll=8)
+    lax.fori_loop(0, terms_ref.shape[1], step, 0, unroll=32)
 
 
 def take_cells(place_ref, cells_ref, out_ref):
@@ -63,22 +63,17 @@
         out_ref[block] = cells_ref[place_ref[block]]
         return carry
 
-    lax.fori_loop(0, out_ref.shape[0], step, 0, unroll=8)
-
-
-def fan_out(x_ref, out_hbm, slots, sems):
-    for slot in range(2):
-        for i, seat in enumerate(SEAT_ORDER):
-            for k, plane in enumerate(PLANE_ORDER):
-                slots[slot, i, plane] = x_ref[k, seat, slot]
-    copies = [
-        pltpu.make_async_copy(slots.at[lane % 2], out_hbm.at[i], sems.at[i])
-        for i, lane in enumerate(LANE_ORDER)
-    ]
-    for copy in copies:
-        copy.start()
-    for copy in copies:
-        copy.wait()
+    lax.fori_loop(0, out_ref.shape[0], step, 0, unroll=32)
+
+
+def fan_out(x_ref, out_ref):
+    for i, seat in enumerate(SEAT_ORDER):
+        for k, plane in enumerate(PLANE_ORDER):
+            for slot in range(2):
+                value = x_ref[k, seat, slot]
+                for place, lane in enumerate(LANE_ORDER):
+                    if lane % 2 == slot:
+                        out_ref[place, i, plane] = value
 
 
 def paired(first, second):
@@ -112,24 +107,44 @@
         opposite_ref[side] = block(ref, parity, lane)
 
 
-def precondition(
-    lane_ref, pieces, left_hbm, right_hbm, beside, across, opposite, grads_ref, out_ref, grams_ref,
-    lefts, rights, own, sems,
-):
+def assemble(lane_ref, own_left_ref, own_right_ref, beside, across, opposite, lefts, rights):
     lane = lane_ref[0]
     parity = lax.rem(lane, 2)
-    width = grads_ref.shape[0]
-    quarter = left_hbm.shape[1]
+    quarter = own_left_ref.shape[1]
 
     def rows_of(x):
         return pl.ds(pl.multiple_of(x * quarter, quarter), quarter)
 
-    copies = [
-        pltpu.make_async_copy(left_hbm.at[parity], own.at[0], sems.at[0]),
-        pltpu.make_async_copy(right_hbm.at[parity], own.at[1], sems.at[1]),
-    ]
-    for copy in copies:
-        copy.start()
+    beyond, far, last = lane ^ 1, lane ^ 3, lane ^ 2
+    turn = lane & 2
+
+    for side, (own, target, mask) in enumerate(
+        ((own_left_ref, lefts, 0), (own_right_ref, rights, turn))
+    ):
+
+        def put(row, column, block):
+            target[rows_of(row), rows_of(column ^ mask)] = block
+            if row is not column:
+                target[rows_of(column), rows_of(row ^ mask)] = block.T
+
+        put(lane, lane, own[parity, :, rows_of(lane)])
+        for other in (beyond, far, last):
+            put(lane, other, own[parity, :, rows_of(other)])
+        put(beyond, beyond, beside[3 * side])
+        put(beyond, last, beside[3 * side + 1])
+        put(beyond, far, beside[3 * side + 2])
+        put(far, far, across[2 * side])
+        put(far, last, across[2 * side + 1])
+        put(last, last, opposite[side])
+
+
+def precondition(lane_ref, pieces, left_ref, right_ref, grads_ref, out_ref, grams_ref):
+    lane = lane_ref[0]
+    width = grads_ref.shape[0]
+    quarter = width // LANES
+
+    def rows_of(x):
+        return pl.ds(pl.multiple_of(x * quarter, quarter), quarter)
 
     square = jnp.zeros((1, 1), jnp.float32)
     for i, source in enumerate(LANE_ORDER):
@@ -145,30 +160,9 @@
         square += jnp.sum(sums, axis=(0, 1), keepdims=True)
         flat = value.reshape(width, quarter).astype(jnp.bfloat16)
         grads_ref[:, source * quarter : (source + 1) * quarter] = flat
-    for copy in copies:
-        copy.wait()
-    beyond, far, last = lane ^ 1, lane ^ 3, lane ^ 2
-    turn = lane & 2
-
-    for side, (target, mask) in enumerate(((lefts, 0), (rights, turn))):
-
-        def put(row, column, block):
-            target[rows_of(row), rows_of(column ^ mask)] = block
-            if row is not column:
-                target[rows_of(column), rows_of(row ^ mask)] = block.T
-
-        put(lane, lane, own[side, :, rows_of(lane)])
-        for other in (beyond, far, last):
-            put(lane, other, own[side, :, rows_of(other)])
-        put(beyond, beyond, beside[3 * side])
-        put(beyond, last, beside[3 * side + 1])
-        put(beyond, far, beside[3 * side + 2])
-        put(far, far, across[2 * side])
-        put(far, last, across[2 * side + 1])
-        put(last, last, opposite[side])
-    half = jnp.dot(lefts[...], grads_ref[...], preferred_element_type=jnp.float32)
+    half = jnp.dot(left_ref[...], grads_ref[...], preferred_element_type=jnp.float32)
     product = jnp.dot(
-        half.astype(jnp.bfloat16), rights[...], preferred_element_type=jnp.float32
+        half.astype(jnp.bfloat16), right_ref[...], preferred_element_type=jnp.float32
     )
     prod_sq = jnp.sum(jnp.sum(product * product, axis=0, keepdims=True), axis=1, keepdims=True)
     cells = float(width * width)
@@ -292,23 +286,27 @@
         out_specs=VMEM,
         compiler_params=PARAMS,
         name="sum_and_place",
-    )(place, terms)
+    )(place, terms.reshape(LANES, blocks // 2, 2 * rows, quarter))
     outgoing = outgoing.reshape(PLANES, SEATS * capacity * rows, quarter)
     picked, opposite, outgoing = lax.optimization_barrier((picked, opposite, outgoing))
     arrived = exchange(outgoing, "own", plane_groups)
     beside, across = lane_swap(picked[0], 1), lane_swap(picked[1], 3)
-    beside, across, arrived = lax.optimization_barrier((beside, across, arrived))
+    lefts, rights = pl.pallas_call(
+        assemble,
+        out_shape=[jax.ShapeDtypeStruct((width, width), jnp.bfloat16)] * 2,
+        in_specs=[SMEM] + [VMEM] * 5,
+        out_specs=[VMEM] * 2,
+        compiler_params=PARAMS,
+        name="assemble",
+    )(lane.reshape(1), left, right, beside, across, opposite)
+    lefts, rights, arrived = lax.optimization_barrier((lefts, rights, arrived))
 
     tile = capacity * rows
     copies = pl.pallas_call(
         fan_out,
         out_shape=jax.ShapeDtypeStruct((LANES, SEATS, PLANES, rows, quarter), jnp.bfloat16),
         in_specs=[VMEM],
-        out_specs=HBM,
-        scratch_shapes=[
-            pltpu.VMEM((capacity, SEATS, PLANES, rows, quarter), jnp.bfloat16),
-            pltpu.SemaphoreType.DMA((LANES,)),
-        ],
+        out_specs=VMEM,
         compiler_params=PARAMS,
         name="fan_out",
     )(arrived.reshape(PLANES, SEATS, capacity, rows, quarter))
@@ -323,17 +321,11 @@
             jax.ShapeDtypeStruct((members // 2, PLANES // 2, tile, quarter), jnp.bfloat16),
             jax.ShapeDtypeStruct((2, quarter, width), jnp.bfloat16),
         ),
-        in_specs=[SMEM, VMEM, ANY, ANY, VMEM, VMEM, VMEM],
+        in_specs=[SMEM, VMEM, VMEM, VMEM],
         out_specs=(VMEM, VMEM, VMEM),
-        scratch_shapes=[
-            pltpu.VMEM((width, width), jnp.bfloat16),
-            pltpu.VMEM((width, width), jnp.bfloat16),
-            pltpu.VMEM((2, quarter, width), jnp.bfloat16),
-            pltpu.SemaphoreType.DMA((2,)),
-        ],
         compiler_params=PARAMS,
         name="precondition",
-    )(lane.reshape(1), pieces, left_root, right_root, beside, across, opposite)
+    )(lane.reshape(1), pieces, lefts, rights)
     product = exchange(
         product.reshape(members // 2, PLANES // 2 * tile, quarter), ("dp", "own"), half_groups
     )

time: 105 us -> 103 us (0.981)
  Pallas kernels: 10.4 us -> 9.13 us
where the time goes in v7:
time: 103 us
  starting transfers between devices  45.9 us (45%)
  blocking collectives  29.9 us (29%)
  waiting for transfers between devices  14.9 us (14%)
  Pallas kernels  9.13 us (9%)
  other arithmetic  1.53 us (1%)
    all_to_all x3, starting transfers between devices, exchange(): lax.all_to_all(x, axes, split_axis=0, concat_axis=0, tiled=True, axis_ind...  34.9 us
    all_to_all x2, blocking collectives, exchange(): lax.all_to_all(x, axes, split_axis=0, concat_axis=0, tiled=True, axis_ind...  29.9 us
    ppermute x4, starting transfers between devices, lane_swap(): return lax.ppermute(x, 'dp', [(i, i ^ mask) for i in range(LANES)])  11 us
    ppermute x4, waiting for transfers between devices, lane_swap(): return lax.ppermute(x, 'dp', [(i, i ^ mask) for i in range(LANES)])  10.7 us
    all_to_all x3, waiting for transfers between devices, exchange(): lax.all_to_all(x, axes, split_axis=0, concat_axis=0, tiled=True, axis_ind...  4.23 us
    pallas_call x1, Pallas kernels, body(): pl.pallas_call(statistics, out_shape=(jax.ShapeDtypeStruct(left_stat.shap...  2.18 us
  transfers between devices with their start and end apart: 7, of which 6 were waited for; matrix products, arithmetic and copies ran while one was open for 1% of the time, Pallas kernels for 4%

profile of v7, /device:TPU:1, one launch (start us, length us, event | category | flops | bytes accessed | tf_op | source)
XLA Modules:
  0.0 102.8 jit_solution(1233074334881931836)
XLA Ops:
  0.6 1.9 %split_columns.1 = bf16[4,128,4,128]{3,2,1,0:T(4,128)(2,1)} custom-call(bf16[128,4,512]{2,1,0:T(4,128)(2,1)} %bitcast.19), custom_call_target="tpu_custom_call" | custom-call | tf_op jit(solution)/shard_map/split_columns/pallas_call | solution.py:250
  2.5 0.0 copy-start
  2.5 0.0 copy-start.1
  2.5 7.2 %all-to-all-start = ((bf16[4,128,4,128]{3,2,1,0:T(4,128)(2,1)}), bf16[4,128,4,128]{3,2,1,0:T(4,128)(2,1)S(1)}, u32[]{:S(2)}, u32[]{:S(2)}) async-start(bf16[4,128,4,128]{3,2,1,0:T(4,128)(2,1)} %split_columns.1), calls=%async_computation | async-start | bytes 1048576 | tf_op jit(solution)/shard_map/all_to_all | solution.py:225
  9.7 0.1 pick_blocks.1
  9.8 2.0 %collective-permute-start = (bf16[2,128,128]{2,1,0:T(8,128)(2,1)S(1)}, bf16[2,128,128]{2,1,0:T(8,128)(2,1)S(1)}, u32[]{:S(2)}, u32[]{:S(2)}) collective-permute-start(bf16[2,128,128]{2,1,0:T(8,128)(2,1)S(1)} %get-tuple-element.30), channel_id=1, source_target_pairs={{0,256},{128,384},{256,0},{384,128},{1,257},{129,385},{257,1},{385... | collective-permute-start | bytes 196616 | tf_op jit(solution)/shard_map/ppermute | solution.py:221
  11.7 0.0 copy-start.4
  11.8 0.6 copy-done.4
  12.4 0.2 convert_reduce_fusion
  12.6 0.6 fusion.4
  13.2 0.8 all-to-all-done
  14.1 1.5 %sum_and_place.1 = bf16[256,4,128]{2,1,0:T(4,128)(2,1)} custom-call(s32[128]{0:T(128)S(1)} %get-tuple-element.49.cell_ref.place_ref, bf16[4,64,8,128]{3,2,1,0:T(8,128)(2,1)S(1)} %bitcast.12), custom_call_target="tpu_custom_call" | custom-call | tf_op jit(solution)/shard_map/sum_and_place/pallas_call | solution.py:282
  15.5 1.5 %collective-permute-done.opposite = bf16[2,128,128]{2,1,0:T(8,128)(2,1)S(1)} collective-permute-done((bf16[2,128,128]{2,1,0:T(8,128)(2,1)S(1)}, bf16[2,128,128]{2,1,0:T(8,128)(2,1)S(1)}, u32[]{:S(2)}, u32[]{:S(2)}) %collective-permute-start) | collective-permute-done | bytes 65568 | tf_op jit(solution)/shard_map/ppermute | solution.py:221
  17.0 17.0 %all-to-all-start.1 = ((bf16[16,64,128]{2,1,0:T(8,128)(2,1)}), bf16[16,64,128]{2,1,0:T(8,128)(2,1)S(1)}, u32[]{:S(2)}, u32[]{:S(2)}) async-start(bf16[16,64,128]{2,1,0:T(8,128)(2,1)} %bitcast.4), calls=%async_computation.1 | async-start | bytes 524288 | tf_op jit(solution)/shard_map/all_to_all | solution.py:225
  33.9 2.4 %collective-permute-start.1 = (bf16[6,128,128]{2,1,0:T(8,128)(2,1)S(1)}, bf16[6,128,128]{2,1,0:T(8,128)(2,1)S(1)}, u32[]{:S(2)}, u32[]{:S(2)}) collective-permute-start(bf16[6,128,128]{2,1,0:T(8,128)(2,1)S(1)} %get-tuple-element.32), channel_id=1, source_target_pairs={{0,128},{128,0},{256,384},{384,256},{1,129},{129,1},{257,385},{385... | collective-permute-start | bytes 589832 | tf_op jit(solution)/shard_map/ppermute | solution.py:221
  36.3 4.3 %collective-permute-start.2 = (bf16[4,128,128]{2,1,0:T(8,128)(2,1)S(1)}, bf16[4,128,128]{2,1,0:T(8,128)(2,1)S(1)}, u32[]{:S(2)}, u32[]{:S(2)}) collective-permute-start(bf16[4,128,128]{2,1,0:T(8,128)(2,1)S(1)} %get-tuple-element.33), channel_id=1, source_target_pairs={{0,384},{128,256},{256,128},{384,0},{1,385},{129,257},{257,129},{3... | collective-permute-start | bytes 393224 | tf_op jit(solution)/shard_map/ppermute | solution.py:221
  40.6 2.9 %collective-permute-done.2.across = bf16[4,128,128]{2,1,0:T(8,128)(2,1)S(1)} collective-permute-done((bf16[4,128,128]{2,1,0:T(8,128)(2,1)S(1)}, bf16[4,128,128]{2,1,0:T(8,128)(2,1)S(1)}, u32[]{:S(2)}, u32[]{:S(2)}) %collective-permute-start.2) | collective-permute-done | bytes 131104 | tf_op jit(solution)/shard_map/ppermute | solution.py:221
  43.5 0.0 collective-permute-done.1.beside
  43.5 0.2 assemble.1
  43.8 0.8 all-to-all-done.1
  44.6 0.1 fan_out.1
  44.7 19.4 %all_to_all.25 = bf16[32,64,128]{2,1,0:T(8,128)(2,1)S(1)} all-to-all(bf16[32,64,128]{2,1,0:T(8,128)(2,1)S(1)} %bitcast.14), channel_id=1, replica_groups={{260,261,262,263,256,257,258,259,388,389,390,391,384,385,386,387,4,5,6,..., dimensions={0} | all-to-all | bytes 1048576 | tf_op jit(solution)/shard_map/all_to_all | solution.py:225
  64.1 1.1 %precondition.1 = (bf16[512,512]{1,0:T(8,128)(2,1)S(1)}, bf16[16,8,8,128]{3,2,1,0:T(8,128)(2,1)S(1)}, bf16[2,128,512]{2,1,0:T(8,128)(2,1)S(1)}) custom-call(s32[1]{0:T(128)} %bitcast.lane_ref, bf16[4,8,8,8,128]{4,3,2,1,0:T(8,128)(2,1)S(1)} %bitcast.13, bf16[512,512]{1,0:T(8,128)(2,1)S(1)} %get-tuple-element.39.left_ref, ...), custom_call_target="tpu_custom_call" | custom-call | tf_op jit(solution)/shard_map/precondition/pallas_call | solution.py:317
  65.2 10.6 %all_to_all.26 = bf16[16,64,128]{2,1,0:T(8,128)(2,1)S(1)} all-to-all(bf16[16,64,128]{2,1,0:T(8,128)(2,1)S(1)} %bitcast.18), channel_id=1, replica_groups={{4,5,6,7,0,1,2,3,132,133,134,135,128,129,130,131},{12,13,14,15,8,9,10,1..., dimensions={0} | all-to-all | bytes 524288 | tf_op jit(solution)/shard_map/all_to_all | solution.py:225
  75.8 0.8 regroup.1
  76.6 10.8 %all-to-all-start.4 = ((bf16[16,64,128]{2,1,0:T(8,128)(2,1)}), bf16[16,64,128]{2,1,0:T(8,128)(2,1)S(1)}, u32[]{:S(2)}, u32[]{:S(2)}) async-start(bf16[16,64,128]{2,1,0:T(8,128)(2,1)} %bitcast.10), calls=%async_computation.4 | async-start | bytes 524288 | tf_op jit(solution)/shard_map/all_to_all | solution.py:225
  87.4 2.3 %collective-permute-start.3 = (bf16[2,128,512]{2,1,0:T(8,128)(2,1)S(1)}, bf16[2,128,512]{2,1,0:T(8,128)(2,1)S(1)}, u32[]{:S(2)}, u32[]{:S(2)}) collective-permute-start(bf16[2,128,512]{2,1,0:T(8,128)(2,1)S(1)} %get-tuple-element.45), channel_id=1, source_target_pairs={{0,128},{128,0},{256,384},{384,256},{1,129},{129,1},{257,385},{385... | collective-permute-start | bytes 786440 | tf_op jit(solution)/shard_map/ppermute | solution.py:221
  89.7 0.7 pad_add_fusion.info_ref
  90.4 6.3 %collective-permute-done.3.grams_ref = bf16[2,128,512]{2,1,0:T(8,128)(2,1)S(1)} collective-permute-done((bf16[2,128,512]{2,1,0:T(8,128)(2,1)S(1)}, bf16[2,128,512]{2,1,0:T(8,128)(2,1)S(1)}, u32[]{:S(2)}, u32[]{:S(2)}) %collective-permute-start.3) | collective-permute-done | bytes 262176 | tf_op jit(solution)/shard_map/ppermute | solution.py:221
  96.7 2.2 %statistics.1 = (f32[2,128,512]{2,1,0:T(8,128)}, f32[2,128,512]{2,1,0:T(8,128)}) custom-call(s32[2]{0:T(128)S(1)} %pad_add_fusion.info_ref, bf16[512,512]{1,0:T(8,128)(2,1)S(1)} %get-tuple-element.44.block, bf16[2,128,512]{2,1,0:T(8,128)(2,1)S(1)} %collective-permute-done.3.grams_ref, f32[2,128,512]{2,1,0:T(8,128)S(1)} %copy-done.2, f32[2,128,512]{2,1,0:T(8,128)S(1)} %copy-done.3), custom_call_target="tpu_custom_call" | custom-call | flops 1 | bytes 1 | tf_op jit(solution)/shard_map/statistics/pallas_call | solution.py:345
  98.9 2.6 %all-to-all-done.4 = bf16[16,64,128]{2,1,0:T(8,128)(2,1)S(1)} async-done(((bf16[16,64,128]{2,1,0:T(8,128)(2,1)}), bf16[16,64,128]{2,1,0:T(8,128)(2,1)S(1)}, u32[]{:S(2)}, u32[]{:S(2)}) %all-to-all-start.4) | async-done | bytes 262176 | tf_op jit(solution)/shard_map/all_to_all | solution.py:225
  101.4 1.3 %take_cells.1 = bf16[128,4,128]{2,1,0:T(4,128)(2,1)} custom-call(s32[128]{0:T(128)S(1)} %get-tuple-element.49.cell_ref.place_ref, bf16[256,4,128]{2,1,0:T(4,128)(2,1)S(1)} %bitcast.16), custom_call_target="tpu_custom_call" | custom-call | tf_op jit(solution)/shard_map/take_cells/pallas_call | solution.py:363
  (6 shorter events, 0.0 us)
Async XLA Ops:
  2.5 7.2 %copy-start = (bf16[2,128,512]{2,1,0:T(8,128)(2,1)S(1)}, bf16[2,128,512]{2,1,0:T(8,128)(2,1)}, u32[]{:S(2)}) copy-start(bf16[2,128,512]{2,1,0:T(8,128)(2,1)} %own_left_ref) | copy-start | bytes 786436
  2.5 7.2 %copy-start.1 = (bf16[2,128,512]{2,1,0:T(8,128)(2,1)S(1)}, bf16[2,128,512]{2,1,0:T(8,128)(2,1)}, u32[]{:S(2)}) copy-start(bf16[2,128,512]{2,1,0:T(8,128)(2,1)} %own_right_ref) | copy-start | bytes 786436
  2.5 11.5 %all-to-all-start = ((bf16[4,128,4,128]{3,2,1,0:T(4,128)(2,1)}), bf16[4,128,4,128]{3,2,1,0:T(4,128)(2,1)S(1)}, u32[]{:S(2)}, u32[]{:S(2)}) async-start(bf16[4,128,4,128]{3,2,1,0:T(4,128)(2,1)} %split_columns.1), calls=%async_computation | async-start | bytes 1048576 | tf_op jit(solution)/shard_map/all_to_all | solution.py:225
  9.8 7.2 %collective-permute-start = (bf16[2,128,128]{2,1,0:T(8,128)(2,1)S(1)}, bf16[2,128,128]{2,1,0:T(8,128)(2,1)S(1)}, u32[]{:S(2)}, u32[]{:S(2)}) collective-permute-start(bf16[2,128,128]{2,1,0:T(8,128)(2,1)S(1)} %get-tuple-element.30), channel_id=1, source_target_pairs={{0,256},{128,384},{256,0},{384,128},{1,257},{129,385},{257,1},{385... | collective-permute-start | bytes 196616 | tf_op jit(solution)/shard_map/ppermute | solution.py:221
  11.7 0.7 copy-start.4
  17.0 27.6 %all-to-all-start.1 = ((bf16[16,64,128]{2,1,0:T(8,128)(2,1)}), bf16[16,64,128]{2,1,0:T(8,128)(2,1)S(1)}, u32[]{:S(2)}, u32[]{:S(2)}) async-start(bf16[16,64,128]{2,1,0:T(8,128)(2,1)} %bitcast.4), calls=%async_computation.1 | async-start | bytes 524288 | tf_op jit(solution)/shard_map/all_to_all | solution.py:225
  33.9 9.6 %collective-permute-start.1 = (bf16[6,128,128]{2,1,0:T(8,128)(2,1)S(1)}, bf16[6,128,128]{2,1,0:T(8,128)(2,1)S(1)}, u32[]{:S(2)}, u32[]{:S(2)}) collective-permute-start(bf16[6,128,128]{2,1,0:T(8,128)(2,1)S(1)} %get-tuple-element.32), channel_id=1, source_target_pairs={{0,128},{128,0},{256,384},{384,256},{1,129},{129,1},{257,385},{385... | collective-permute-start | bytes 589832 | tf_op jit(solution)/shard_map/ppermute | solution.py:221
  36.3 7.2 %collective-permute-start.2 = (bf16[4,128,128]{2,1,0:T(8,128)(2,1)S(1)}, bf16[4,128,128]{2,1,0:T(8,128)(2,1)S(1)}, u32[]{:S(2)}, u32[]{:S(2)}) collective-permute-start(bf16[4,128,128]{2,1,0:T(8,128)(2,1)S(1)} %get-tuple-element.33), channel_id=1, source_target_pairs={{0,384},{128,256},{256,128},{384,0},{1,385},{129,257},{257,129},{3... | collective-permute-start | bytes 393224 | tf_op jit(solution)/shard_map/ppermute | solution.py:221
  75.8 20.9 %copy-start.2 = (f32[2,128,512]{2,1,0:T(8,128)S(1)}, f32[2,128,512]{2,1,0:T(8,128)}, u32[]{:S(2)}) copy-start(f32[2,128,512]{2,1,0:T(8,128)} %left_hbm.1) | copy-start | bytes 1572868
  75.8 20.9 %copy-start.3 = (f32[2,128,512]{2,1,0:T(8,128)S(1)}, f32[2,128,512]{2,1,0:T(8,128)}, u32[]{:S(2)}) copy-start(f32[2,128,512]{2,1,0:T(8,128)} %right_hbm.1) | copy-start | bytes 1572868
  76.6 24.9 %all-to-all-start.4 = ((bf16[16,64,128]{2,1,0:T(8,128)(2,1)}), bf16[16,64,128]{2,1,0:T(8,128)(2,1)S(1)}, u32[]{:S(2)}, u32[]{:S(2)}) async-start(bf16[16,64,128]{2,1,0:T(8,128)(2,1)} %bitcast.10), calls=%async_computation.4 | async-start | bytes 524288 | tf_op jit(solution)/shard_map/all_to_all | solution.py:225
  87.4 9.3 %collective-permute-start.3 = (bf16[2,128,512]{2,1,0:T(8,128)(2,1)S(1)}, bf16[2,128,512]{2,1,0:T(8,128)(2,1)S(1)}, u32[]{:S(2)}, u32[]{:S(2)}) collective-permute-start(bf16[2,128,512]{2,1,0:T(8,128)(2,1)S(1)} %get-tuple-element.45), channel_id=1, source_target_pairs={{0,128},{128,0},{256,384},{384,256},{1,129},{129,1},{257,385},{385... | collective-permute-start | bytes 786440 | tf_op jit(solution)/shard_map/ppermute | solution.py:221

commit v8 on v7

--- a/solution.py
+++ b/solution.py
@@ -16,7 +16,7 @@
 PLANES, COLUMNS, CORES, LANES = 16, 4, 2, 4
 LANE_ORDER = (2, 3, 0, 1)
 COLUMN_ORDER = (2, 3, 0, 1)
-FIRST_PLANE = 10
+FIRST_PLANE = 11
 PLANE_ORDER = tuple((FIRST_PLANE + i) % PLANES for i in range(PLANES))
 SEATS = COLUMNS * CORES
 SEAT_ORDER = tuple(y * CORES + c for y in COLUMN_ORDER for c in range(CORES))
@@ -58,12 +58,23 @@
     lax.fori_loop(0, terms_ref.shape[1], step, 0, unroll=32)
 
 
-def take_cells(place_ref, cells_ref, out_ref):
+def take_cells(cell_ref, cells_ref, out_hbm, out, sems):
+    parts = sems.shape[0]
+    size = out.shape[0] // parts
+
     def step(block, carry):
-        out_ref[block] = cells_ref[place_ref[block]]
+        out[block] = cells_ref[cell_ref[block]]
         return carry
 
-    lax.fori_loop(0, out_ref.shape[0], step, 0, unroll=32)
+    copies = []
+    for part in range(parts):
+        blocks = pl.ds(part * size, size)
+        lax.fori_loop(part * size, (part + 1) * size, step, 0, unroll=32)
+        copy = pltpu.make_async_copy(out.at[blocks], out_hbm.at[blocks], sems.at[part])
+        copy.start()
+        copies.append(copy)
+    for copy in copies:
+        copy.wait()
 
 
 def fan_out(x_ref, out_ref):
@@ -364,7 +375,11 @@
         take_cells,
         out_shape=jax.ShapeDtypeStruct((blocks, rows, quarter), jnp.bfloat16),
         in_specs=[SMEM, VMEM],
-        out_specs=VMEM,
+        out_specs=HBM,
+        scratch_shapes=[
+            pltpu.VMEM((blocks, rows, quarter), jnp.bfloat16),
+            pltpu.SemaphoreType.DMA((2,)),
+        ],
         compiler_params=PARAMS,
         name="take_cells",
     )(place, returned.reshape(owners * capacity, rows, quarter))

time: 103 us -> 103 us (level)
  starting transfers between devices: 45.9 us -> 44 us
  waiting for transfers between devices: 14.9 us -> 16.7 us
    all_to_all x3, starting transfers between devices: 34.9 us -> 33.1 us  [exchange(): lax.all_to_all(x, axes, split_axis=0, concat_axis=0, tiled=True, axis_ind...]
    all_to_all x3, waiting for transfers between devices: 4.23 us -> 6.02 us  [exchange(): lax.all_to_all(x, axes, split_axis=0, concat_axis=0, tiled=True, axis_ind...]
where the time goes in v8:
time: 103 us; the launch traced here: 102 us
  starting transfers between devices  44 us (43%)
  blocking collectives  29.7 us (29%)
  waiting for transfers between devices  16.7 us (16%)
  Pallas kernels  9.12 us (9%)
  other arithmetic  1.53 us (1%)
    all_to_all x3, starting transfers between devices, exchange(): lax.all_to_all(x, axes, split_axis=0, concat_axis=0, tiled=True, axis_ind...  33.1 us
    all_to_all x2, blocking collectives, exchange(): lax.all_to_all(x, axes, split_axis=0, concat_axis=0, tiled=True, axis_ind...  29.7 us
    ppermute x4, starting transfers between devices, lane_swap(): return lax.ppermute(x, 'dp', [(i, i ^ mask) for i in range(LANES)])  11 us
    ppermute x4, waiting for transfers between devices, lane_swap(): return lax.ppermute(x, 'dp', [(i, i ^ mask) for i in range(LANES)])  10.7 us
    all_to_all x3, waiting for transfers between devices, exchange(): lax.all_to_all(x, axes, split_axis=0, concat_axis=0, tiled=True, axis_ind...  6.02 us
    pallas_call x1, Pallas kernels, body(): pl.pallas_call(statistics, out_shape=(jax.ShapeDtypeStruct(left_stat.shap...  2.18 us
  transfers between devices with their start and end apart: 7, of which 6 were waited for; matrix products, arithmetic and copies ran while one was open for 1% of the time, Pallas kernels for 4%

profile of v8, /device:TPU:1, one launch (start us, length us, event | category | flops | bytes accessed | tf_op | source)
XLA Modules:
  0.0 102.5 jit_solution(9420467627125004370)
XLA Ops:
  0.6 1.9 %split_columns.1 = bf16[4,128,4,128]{3,2,1,0:T(4,128)(2,1)} custom-call(bf16[128,4,512]{2,1,0:T(4,128)(2,1)} %bitcast.19), custom_call_target="tpu_custom_call" | custom-call | tf_op jit(solution)/shard_map/split_columns/pallas_call | solution.py:261
  2.5 0.0 copy-start
  2.5 0.0 copy-start.1
  2.5 7.2 %all-to-all-start = ((bf16[4,128,4,128]{3,2,1,0:T(4,128)(2,1)}), bf16[4,128,4,128]{3,2,1,0:T(4,128)(2,1)S(1)}, u32[]{:S(2)}, u32[]{:S(2)}) async-start(bf16[4,128,4,128]{3,2,1,0:T(4,128)(2,1)} %split_columns.1), calls=%async_computation | async-start | bytes 1048576 | tf_op jit(solution)/shard_map/all_to_all | solution.py:236
  9.7 0.1 pick_blocks.1
  9.8 2.0 %collective-permute-start = (bf16[2,128,128]{2,1,0:T(8,128)(2,1)S(1)}, bf16[2,128,128]{2,1,0:T(8,128)(2,1)S(1)}, u32[]{:S(2)}, u32[]{:S(2)}) collective-permute-start(bf16[2,128,128]{2,1,0:T(8,128)(2,1)S(1)} %get-tuple-element.30), channel_id=1, source_target_pairs={{0,256},{128,384},{256,0},{384,128},{1,257},{129,385},{257,1},{385... | collective-permute-start | bytes 196616 | tf_op jit(solution)/shard_map/ppermute | solution.py:232
  11.7 0.0 copy-start.4
  11.8 0.6 copy-done.4
  12.4 0.2 convert_reduce_fusion
  12.6 0.6 fusion.4
  13.2 0.8 all-to-all-done
  14.1 1.5 %sum_and_place.1 = bf16[256,4,128]{2,1,0:T(4,128)(2,1)} custom-call(s32[128]{0:T(128)S(1)} %get-tuple-element.49.cell_ref, bf16[4,64,8,128]{3,2,1,0:T(8,128)(2,1)S(1)} %bitcast.12), custom_call_target="tpu_custom_call" | custom-call | tf_op jit(solution)/shard_map/sum_and_place/pallas_call | solution.py:293
  15.5 1.5 %collective-permute-done.opposite = bf16[2,128,128]{2,1,0:T(8,128)(2,1)S(1)} collective-permute-done((bf16[2,128,128]{2,1,0:T(8,128)(2,1)S(1)}, bf16[2,128,128]{2,1,0:T(8,128)(2,1)S(1)}, u32[]{:S(2)}, u32[]{:S(2)}) %collective-permute-start) | collective-permute-done | bytes 65568 | tf_op jit(solution)/shard_map/ppermute | solution.py:232
  17.0 16.1 %all-to-all-start.1 = ((bf16[16,64,128]{2,1,0:T(8,128)(2,1)}), bf16[16,64,128]{2,1,0:T(8,128)(2,1)S(1)}, u32[]{:S(2)}, u32[]{:S(2)}) async-start(bf16[16,64,128]{2,1,0:T(8,128)(2,1)} %bitcast.4), calls=%async_computation.1 | async-start | bytes 524288 | tf_op jit(solution)/shard_map/all_to_all | solution.py:236
  33.0 2.4 %collective-permute-start.1 = (bf16[6,128,128]{2,1,0:T(8,128)(2,1)S(1)}, bf16[6,128,128]{2,1,0:T(8,128)(2,1)S(1)}, u32[]{:S(2)}, u32[]{:S(2)}) collective-permute-start(bf16[6,128,128]{2,1,0:T(8,128)(2,1)S(1)} %get-tuple-element.32), channel_id=1, source_target_pairs={{0,128},{128,0},{256,384},{384,256},{1,129},{129,1},{257,385},{385... | collective-permute-start | bytes 589832 | tf_op jit(solution)/shard_map/ppermute | solution.py:232
  35.4 4.3 %collective-permute-start.2 = (bf16[4,128,128]{2,1,0:T(8,128)(2,1)S(1)}, bf16[4,128,128]{2,1,0:T(8,128)(2,1)S(1)}, u32[]{:S(2)}, u32[]{:S(2)}) collective-permute-start(bf16[4,128,128]{2,1,0:T(8,128)(2,1)S(1)} %get-tuple-element.33), channel_id=1, source_target_pairs={{0,384},{128,256},{256,128},{384,0},{1,385},{129,257},{257,129},{3... | collective-permute-start | bytes 393224 | tf_op jit(solution)/shard_map/ppermute | solution.py:232
  39.7 2.9 %collective-permute-done.2.across = bf16[4,128,128]{2,1,0:T(8,128)(2,1)S(1)} collective-permute-done((bf16[4,128,128]{2,1,0:T(8,128)(2,1)S(1)}, bf16[4,128,128]{2,1,0:T(8,128)(2,1)S(1)}, u32[]{:S(2)}, u32[]{:S(2)}) %collective-permute-start.2) | collective-permute-done | bytes 131104 | tf_op jit(solution)/shard_map/ppermute | solution.py:232
  42.6 0.0 collective-permute-done.1.beside
  42.6 0.2 assemble.1
  42.9 2.0 %all-to-all-done.1 = bf16[16,64,128]{2,1,0:T(8,128)(2,1)S(1)} async-done(((bf16[16,64,128]{2,1,0:T(8,128)(2,1)}), bf16[16,64,128]{2,1,0:T(8,128)(2,1)S(1)}, u32[]{:S(2)}, u32[]{:S(2)}) %all-to-all-start.1) | async-done | bytes 262176 | tf_op jit(solution)/shard_map/all_to_all | solution.py:236
  44.9 0.1 fan_out.1
  45.0 19.0 %all_to_all.25 = bf16[32,64,128]{2,1,0:T(8,128)(2,1)S(1)} all-to-all(bf16[32,64,128]{2,1,0:T(8,128)(2,1)S(1)} %bitcast.14), channel_id=1, replica_groups={{260,261,262,263,256,257,258,259,388,389,390,391,384,385,386,387,4,5,6,..., dimensions={0} | all-to-all | bytes 1048576 | tf_op jit(solution)/shard_map/all_to_all | solution.py:236
  64.1 1.1 %precondition.1 = (bf16[512,512]{1,0:T(8,128)(2,1)S(1)}, bf16[16,8,8,128]{3,2,1,0:T(8,128)(2,1)S(1)}, bf16[2,128,512]{2,1,0:T(8,128)(2,1)S(1)}) custom-call(s32[1]{0:T(128)} %bitcast.lane_ref, bf16[4,8,8,8,128]{4,3,2,1,0:T(8,128)(2,1)S(1)} %bitcast.13, bf16[512,512]{1,0:T(8,128)(2,1)S(1)} %get-tuple-element.39.left_ref, ...), custom_call_target="tpu_custom_call" | custom-call | tf_op jit(solution)/shard_map/precondition/pallas_call | solution.py:328
  65.1 10.7 %all_to_all.26 = bf16[16,64,128]{2,1,0:T(8,128)(2,1)S(1)} all-to-all(bf16[16,64,128]{2,1,0:T(8,128)(2,1)S(1)} %bitcast.18), channel_id=1, replica_groups={{4,5,6,7,0,1,2,3,132,133,134,135,128,129,130,131},{12,13,14,15,8,9,10,1..., dimensions={0} | all-to-all | bytes 524288 | tf_op jit(solution)/shard_map/all_to_all | solution.py:236
  75.8 0.8 regroup.1
  76.6 9.8 %all-to-all-start.4 = ((bf16[16,64,128]{2,1,0:T(8,128)(2,1)}), bf16[16,64,128]{2,1,0:T(8,128)(2,1)S(1)}, u32[]{:S(2)}, u32[]{:S(2)}) async-start(bf16[16,64,128]{2,1,0:T(8,128)(2,1)} %bitcast.10), calls=%async_computation.4 | async-start | bytes 524288 | tf_op jit(solution)/shard_map/all_to_all | solution.py:236
  86.5 2.3 %collective-permute-start.3 = (bf16[2,128,512]{2,1,0:T(8,128)(2,1)S(1)}, bf16[2,128,512]{2,1,0:T(8,128)(2,1)S(1)}, u32[]{:S(2)}, u32[]{:S(2)}) collective-permute-start(bf16[2,128,512]{2,1,0:T(8,128)(2,1)S(1)} %get-tuple-element.45), channel_id=1, source_target_pairs={{0,128},{128,0},{256,384},{384,256},{1,129},{129,1},{257,385},{385... | collective-permute-start | bytes 786440 | tf_op jit(solution)/shard_map/ppermute | solution.py:232
  88.8 0.7 pad_add_fusion.info_ref
  89.5 6.3 %collective-permute-done.3.grams_ref = bf16[2,128,512]{2,1,0:T(8,128)(2,1)S(1)} collective-permute-done((bf16[2,128,512]{2,1,0:T(8,128)(2,1)S(1)}, bf16[2,128,512]{2,1,0:T(8,128)(2,1)S(1)}, u32[]{:S(2)}, u32[]{:S(2)}) %collective-permute-start.3) | collective-permute-done | bytes 262176 | tf_op jit(solution)/shard_map/ppermute | solution.py:232
  95.8 2.2 %statistics.1 = (f32[2,128,512]{2,1,0:T(8,128)}, f32[2,128,512]{2,1,0:T(8,128)}) custom-call(s32[2]{0:T(128)S(1)} %pad_add_fusion.info_ref, bf16[512,512]{1,0:T(8,128)(2,1)S(1)} %get-tuple-element.44.block, bf16[2,128,512]{2,1,0:T(8,128)(2,1)S(1)} %collective-permute-done.3.grams_ref, f32[2,128,512]{2,1,0:T(8,128)S(1)} %copy-done.2, f32[2,128,512]{2,1,0:T(8,128)S(1)} %copy-done.3), custom_call_target="tpu_custom_call" | custom-call | flops 1 | bytes 1 | tf_op jit(solution)/shard_map/statistics/pallas_call | solution.py:356
  98.0 3.2 %all-to-all-done.4 = bf16[16,64,128]{2,1,0:T(8,128)(2,1)S(1)} async-done(((bf16[16,64,128]{2,1,0:T(8,128)(2,1)}), bf16[16,64,128]{2,1,0:T(8,128)(2,1)S(1)}, u32[]{:S(2)}, u32[]{:S(2)}) %all-to-all-start.4) | async-done | bytes 262176 | tf_op jit(solution)/shard_map/all_to_all | solution.py:236
  101.1 1.3 %take_cells.1 = bf16[128,4,128]{2,1,0:T(4,128)(2,1)} custom-call(s32[128]{0:T(128)S(1)} %get-tuple-element.49.cell_ref, bf16[256,4,128]{2,1,0:T(4,128)(2,1)S(1)} %bitcast.16), custom_call_target="tpu_custom_call" | custom-call | tf_op jit(solution)/shard_map/take_cells/pallas_call | solution.py:374
  (6 shorter events, 0.0 us)
Async XLA Ops:
  2.5 7.2 %copy-start = (bf16[2,128,512]{2,1,0:T(8,128)(2,1)S(1)}, bf16[2,128,512]{2,1,0:T(8,128)(2,1)}, u32[]{:S(2)}) copy-start(bf16[2,128,512]{2,1,0:T(8,128)(2,1)} %own_left_ref) | copy-start | bytes 786436
  2.5 7.2 %copy-start.1 = (bf16[2,128,512]{2,1,0:T(8,128)(2,1)S(1)}, bf16[2,128,512]{2,1,0:T(8,128)(2,1)}, u32[]{:S(2)}) copy-start(bf16[2,128,512]{2,1,0:T(8,128)(2,1)} %own_right_ref) | copy-start | bytes 786436
  2.5 11.5 %all-to-all-start = ((bf16[4,128,4,128]{3,2,1,0:T(4,128)(2,1)}), bf16[4,128,4,128]{3,2,1,0:T(4,128)(2,1)S(1)}, u32[]{:S(2)}, u32[]{:S(2)}) async-start(bf16[4,128,4,128]{3,2,1,0:T(4,128)(2,1)} %split_columns.1), calls=%async_computation | async-start | bytes 1048576 | tf_op jit(solution)/shard_map/all_to_all | solution.py:236
  9.8 7.2 %collective-permute-start = (bf16[2,128,128]{2,1,0:T(8,128)(2,1)S(1)}, bf16[2,128,128]{2,1,0:T(8,128)(2,1)S(1)}, u32[]{:S(2)}, u32[]{:S(2)}) collective-permute-start(bf16[2,128,128]{2,1,0:T(8,128)(2,1)S(1)} %get-tuple-element.30), channel_id=1, source_target_pairs={{0,256},{128,384},{256,0},{384,128},{1,257},{129,385},{257,1},{385... | collective-permute-start | bytes 196616 | tf_op jit(solution)/shard_map/ppermute | solution.py:232
  11.7 0.7 copy-start.4
  17.0 27.9 %all-to-all-start.1 = ((bf16[16,64,128]{2,1,0:T(8,128)(2,1)}), bf16[16,64,128]{2,1,0:T(8,128)(2,1)S(1)}, u32[]{:S(2)}, u32[]{:S(2)}) async-start(bf16[16,64,128]{2,1,0:T(8,128)(2,1)} %bitcast.4), calls=%async_computation.1 | async-start | bytes 524288 | tf_op jit(solution)/shard_map/all_to_all | solution.py:236
  33.0 9.6 %collective-permute-start.1 = (bf16[6,128,128]{2,1,0:T(8,128)(2,1)S(1)}, bf16[6,128,128]{2,1,0:T(8,128)(2,1)S(1)}, u32[]{:S(2)}, u32[]{:S(2)}) collective-permute-start(bf16[6,128,128]{2,1,0:T(8,128)(2,1)S(1)} %get-tuple-element.32), channel_id=1, source_target_pairs={{0,128},{128,0},{256,384},{384,256},{1,129},{129,1},{257,385},{385... | collective-permute-start | bytes 589832 | tf_op jit(solution)/shard_map/ppermute | solution.py:232
  35.4 7.2 %collective-permute-start.2 = (bf16[4,128,128]{2,1,0:T(8,128)(2,1)S(1)}, bf16[4,128,128]{2,1,0:T(8,128)(2,1)S(1)}, u32[]{:S(2)}, u32[]{:S(2)}) collective-permute-start(bf16[4,128,128]{2,1,0:T(8,128)(2,1)S(1)} %get-tuple-element.33), channel_id=1, source_target_pairs={{0,384},{128,256},{256,128},{384,0},{1,385},{129,257},{257,129},{3... | collective-permute-start | bytes 393224 | tf_op jit(solution)/shard_map/ppermute | solution.py:232
  75.8 19.9 %copy-start.2 = (f32[2,128,512]{2,1,0:T(8,128)S(1)}, f32[2,128,512]{2,1,0:T(8,128)}, u32[]{:S(2)}) copy-start(f32[2,128,512]{2,1,0:T(8,128)} %left_hbm.1) | copy-start | bytes 1572868
  75.8 19.9 %copy-start.3 = (f32[2,128,512]{2,1,0:T(8,128)S(1)}, f32[2,128,512]{2,1,0:T(8,128)}, u32[]{:S(2)}) copy-start(f32[2,128,512]{2,1,0:T(8,128)} %right_hbm.1) | copy-start | bytes 1572868
  76.6 24.5 %all-to-all-start.4 = ((bf16[16,64,128]{2,1,0:T(8,128)(2,1)}), bf16[16,64,128]{2,1,0:T(8,128)(2,1)S(1)}, u32[]{:S(2)}, u32[]{:S(2)}) async-start(bf16[16,64,128]{2,1,0:T(8,128)(2,1)} %bitcast.10), calls=%async_computation.4 | async-start | bytes 524288 | tf_op jit(solution)/shard_map/all_to_all | solution.py:236
  86.5 9.3 %collective-permute-start.3 = (bf16[2,128,512]{2,1,0:T(8,128)(2,1)S(1)}, bf16[2,128,512]{2,1,0:T(8,128)(2,1)S(1)}, u32[]{:S(2)}, u32[]{:S(2)}) collective-permute-start(bf16[2,128,512]{2,1,0:T(8,128)(2,1)S(1)} %get-tuple-element.45), channel_id=1, source_target_pairs={{0,128},{128,0},{256,384},{384,256},{1,129},{129,1},{257,385},{385... | collective-permute-start | bytes 786440 | tf_op jit(solution)/shard_map/ppermute | solution.py:232

commit v9 on v8

--- a/solution.py
+++ b/solution.py
@@ -44,7 +44,7 @@
         copy.wait()
 
 
-def sum_and_place(cell_ref, terms_ref, out_ref):
+def sum_and_place(cell_ref, terms_ref, out_hbm, out_ref, sems):
     out_ref[...] = jnp.zeros_like(out_ref)
 
     def step(pair, carry):
@@ -55,7 +55,16 @@
         out_ref[cell_ref[2 * pair + 1]] = total[4:].astype(out_ref.dtype)
         return carry
 
-    lax.fori_loop(0, terms_ref.shape[1], step, 0, unroll=32)
+    lax.fori_loop(0, terms_ref.shape[1], step, 0, unroll=64)
+    parts = sems.shape[0]
+    size = out_ref.shape[0] // parts
+    copies = []
+    for part in range(parts):
+        cells = pl.ds(part * size, size)
+        copies.append(pltpu.make_async_copy(out_ref.at[cells], out_hbm.at[cells], sems.at[part]))
+        copies[part].start()
+    for copy in copies:
+        copy.wait()
 
 
 def take_cells(cell_ref, cells_ref, out_hbm, out, sems):
@@ -294,7 +303,11 @@
         sum_and_place,
         out_shape=jax.ShapeDtypeStruct((owners * capacity, rows, quarter), jnp.bfloat16),
         in_specs=[SMEM, VMEM],
-        out_specs=VMEM,
+        out_specs=HBM,
+        scratch_shapes=[
+            pltpu.VMEM((owners * capacity, rows, quarter), jnp.bfloat16),
+            pltpu.SemaphoreType.DMA((2,)),
+        ],
         compiler_params=PARAMS,
         name="sum_and_place",
     )(place, terms.reshape(LANES, blocks // 2, 2 * rows, quarter))

time: 103 us -> 103 us (level)
  no operation moved by 1% of the time
where the time goes in v9:
time: 103 us; the launch traced here: 102 us
  starting transfers between devices  44 us (43%)
  blocking collectives  29.7 us (29%)
  waiting for transfers between devices  16.7 us (16%)
  Pallas kernels  9.08 us (9%)
  other arithmetic  1.53 us (1%)
    all_to_all x3, starting transfers between devices, exchange(): lax.all_to_all(x, axes, split_axis=0, concat_axis=0, tiled=True, axis_ind...  33 us
    all_to_all x2, blocking collectives, exchange(): lax.all_to_all(x, axes, split_axis=0, concat_axis=0, tiled=True, axis_ind...  29.7 us
    ppermute x4, starting transfers between devices, lane_swap(): return lax.ppermute(x, 'dp', [(i, i ^ mask) for i in range(LANES)])  11 us
    ppermute x4, waiting for transfers between devices, lane_swap(): return lax.ppermute(x, 'dp', [(i, i ^ mask) for i in range(LANES)])  10.7 us
    all_to_all x3, waiting for transfers between devices, exchange(): lax.all_to_all(x, axes, split_axis=0, concat_axis=0, tiled=True, axis_ind...  6.02 us
    pallas_call x1, Pallas kernels, body(): pl.pallas_call(statistics, out_shape=(jax.ShapeDtypeStruct(left_stat.shap...  2.18 us
  transfers between devices with their start and end apart: 7, of which 6 were waited for; matrix products, arithmetic and copies ran while one was open for 1% of the time, Pallas kernels for 4%

profile of v9, /device:TPU:1, one launch (start us, length us, event | category | flops | bytes accessed | tf_op | source)
XLA Modules:
  0.0 102.5 jit_solution(4050283091601653028)
XLA Ops:
  0.6 1.9 %split_columns.1 = bf16[4,128,4,128]{3,2,1,0:T(4,128)(2,1)} custom-call(bf16[128,4,512]{2,1,0:T(4,128)(2,1)} %bitcast.19), custom_call_target="tpu_custom_call" | custom-call | tf_op jit(solution)/shard_map/split_columns/pallas_call | solution.py:270
  2.5 0.0 copy-start
  2.5 0.0 copy-start.1
  2.5 7.2 %all-to-all-start = ((bf16[4,128,4,128]{3,2,1,0:T(4,128)(2,1)}), bf16[4,128,4,128]{3,2,1,0:T(4,128)(2,1)S(1)}, u32[]{:S(2)}, u32[]{:S(2)}) async-start(bf16[4,128,4,128]{3,2,1,0:T(4,128)(2,1)} %split_columns.1), calls=%async_computation | async-start | bytes 1048576 | tf_op jit(solution)/shard_map/all_to_all | solution.py:245
  9.7 0.1 pick_blocks.1
  9.8 2.0 %collective-permute-start = (bf16[2,128,128]{2,1,0:T(8,128)(2,1)S(1)}, bf16[2,128,128]{2,1,0:T(8,128)(2,1)S(1)}, u32[]{:S(2)}, u32[]{:S(2)}) collective-permute-start(bf16[2,128,128]{2,1,0:T(8,128)(2,1)S(1)} %get-tuple-element.30), channel_id=1, source_target_pairs={{0,256},{128,384},{256,0},{384,128},{1,257},{129,385},{257,1},{385... | collective-permute-start | bytes 196616 | tf_op jit(solution)/shard_map/ppermute | solution.py:241
  11.7 0.0 copy-start.4
  11.8 0.6 copy-done.4
  12.4 0.2 convert_reduce_fusion
  12.6 0.6 fusion.4
  13.2 0.8 all-to-all-done
  14.1 1.4 %sum_and_place.1 = bf16[256,4,128]{2,1,0:T(4,128)(2,1)} custom-call(s32[128]{0:T(128)S(1)} %get-tuple-element.49.cell_ref, bf16[4,64,8,128]{3,2,1,0:T(8,128)(2,1)S(1)} %bitcast.12), custom_call_target="tpu_custom_call" | custom-call | tf_op jit(solution)/shard_map/sum_and_place/pallas_call | solution.py:302
  15.5 1.5 %collective-permute-done.opposite = bf16[2,128,128]{2,1,0:T(8,128)(2,1)S(1)} collective-permute-done((bf16[2,128,128]{2,1,0:T(8,128)(2,1)S(1)}, bf16[2,128,128]{2,1,0:T(8,128)(2,1)S(1)}, u32[]{:S(2)}, u32[]{:S(2)}) %collective-permute-start) | collective-permute-done | bytes 65568 | tf_op jit(solution)/shard_map/ppermute | solution.py:241
  17.0 16.0 %all-to-all-start.1 = ((bf16[16,64,128]{2,1,0:T(8,128)(2,1)}), bf16[16,64,128]{2,1,0:T(8,128)(2,1)S(1)}, u32[]{:S(2)}, u32[]{:S(2)}) async-start(bf16[16,64,128]{2,1,0:T(8,128)(2,1)} %bitcast.4), calls=%async_computation.1 | async-start | bytes 524288 | tf_op jit(solution)/shard_map/all_to_all | solution.py:245
  33.0 2.4 %collective-permute-start.1 = (bf16[6,128,128]{2,1,0:T(8,128)(2,1)S(1)}, bf16[6,128,128]{2,1,0:T(8,128)(2,1)S(1)}, u32[]{:S(2)}, u32[]{:S(2)}) collective-permute-start(bf16[6,128,128]{2,1,0:T(8,128)(2,1)S(1)} %get-tuple-element.32), channel_id=1, source_target_pairs={{0,128},{128,0},{256,384},{384,256},{1,129},{129,1},{257,385},{385... | collective-permute-start | bytes 589832 | tf_op jit(solution)/shard_map/ppermute | solution.py:241
  35.4 4.3 %collective-permute-start.2 = (bf16[4,128,128]{2,1,0:T(8,128)(2,1)S(1)}, bf16[4,128,128]{2,1,0:T(8,128)(2,1)S(1)}, u32[]{:S(2)}, u32[]{:S(2)}) collective-permute-start(bf16[4,128,128]{2,1,0:T(8,128)(2,1)S(1)} %get-tuple-element.33), channel_id=1, source_target_pairs={{0,384},{128,256},{256,128},{384,0},{1,385},{129,257},{257,129},{3... | collective-permute-start | bytes 393224 | tf_op jit(solution)/shard_map/ppermute | solution.py:241
  39.7 2.9 %collective-permute-done.2.across = bf16[4,128,128]{2,1,0:T(8,128)(2,1)S(1)} collective-permute-done((bf16[4,128,128]{2,1,0:T(8,128)(2,1)S(1)}, bf16[4,128,128]{2,1,0:T(8,128)(2,1)S(1)}, u32[]{:S(2)}, u32[]{:S(2)}) %collective-permute-start.2) | collective-permute-done | bytes 131104 | tf_op jit(solution)/shard_map/ppermute | solution.py:241
  42.6 0.0 collective-permute-done.1.beside
  42.6 0.2 assemble.1
  42.8 2.0 %all-to-all-done.1 = bf16[16,64,128]{2,1,0:T(8,128)(2,1)S(1)} async-done(((bf16[16,64,128]{2,1,0:T(8,128)(2,1)}), bf16[16,64,128]{2,1,0:T(8,128)(2,1)S(1)}, u32[]{:S(2)}, u32[]{:S(2)}) %all-to-all-start.1) | async-done | bytes 262176 | tf_op jit(solution)/shard_map/all_to_all | solution.py:245
  44.9 0.1 fan_out.1
  45.0 19.0 %all_to_all.25 = bf16[32,64,128]{2,1,0:T(8,128)(2,1)S(1)} all-to-all(bf16[32,64,128]{2,1,0:T(8,128)(2,1)S(1)} %bitcast.14), channel_id=1, replica_groups={{260,261,262,263,256,257,258,259,388,389,390,391,384,385,386,387,4,5,6,..., dimensions={0} | all-to-all | bytes 1048576 | tf_op jit(solution)/shard_map/all_to_all | solution.py:245
  64.0 1.1 %precondition.1 = (bf16[512,512]{1,0:T(8,128)(2,1)S(1)}, bf16[16,8,8,128]{3,2,1,0:T(8,128)(2,1)S(1)}, bf16[2,128,512]{2,1,0:T(8,128)(2,1)S(1)}) custom-call(s32[1]{0:T(128)} %bitcast.lane_ref, bf16[4,8,8,8,128]{4,3,2,1,0:T(8,128)(2,1)S(1)} %bitcast.13, bf16[512,512]{1,0:T(8,128)(2,1)S(1)} %get-tuple-element.39.left_ref, ...), custom_call_target="tpu_custom_call" | custom-call | tf_op jit(solution)/shard_map/precondition/pallas_call | solution.py:341
  65.1 10.7 %all_to_all.26 = bf16[16,64,128]{2,1,0:T(8,128)(2,1)S(1)} all-to-all(bf16[16,64,128]{2,1,0:T(8,128)(2,1)S(1)} %bitcast.18), channel_id=1, replica_groups={{4,5,6,7,0,1,2,3,132,133,134,135,128,129,130,131},{12,13,14,15,8,9,10,1..., dimensions={0} | all-to-all | bytes 524288 | tf_op jit(solution)/shard_map/all_to_all | solution.py:245
  75.8 0.8 regroup.1
  76.6 9.8 %all-to-all-start.4 = ((bf16[16,64,128]{2,1,0:T(8,128)(2,1)}), bf16[16,64,128]{2,1,0:T(8,128)(2,1)S(1)}, u32[]{:S(2)}, u32[]{:S(2)}) async-start(bf16[16,64,128]{2,1,0:T(8,128)(2,1)} %bitcast.10), calls=%async_computation.4 | async-start | bytes 524288 | tf_op jit(solution)/shard_map/all_to_all | solution.py:245
  86.4 2.3 %collective-permute-start.3 = (bf16[2,128,512]{2,1,0:T(8,128)(2,1)S(1)}, bf16[2,128,512]{2,1,0:T(8,128)(2,1)S(1)}, u32[]{:S(2)}, u32[]{:S(2)}) collective-permute-start(bf16[2,128,512]{2,1,0:T(8,128)(2,1)S(1)} %get-tuple-element.45), channel_id=1, source_target_pairs={{0,128},{128,0},{256,384},{384,256},{1,129},{129,1},{257,385},{385... | collective-permute-start | bytes 786440 | tf_op jit(solution)/shard_map/ppermute | solution.py:241
  88.7 0.7 pad_add_fusion.info_ref
  89.5 6.3 %collective-permute-done.3.grams_ref = bf16[2,128,512]{2,1,0:T(8,128)(2,1)S(1)} collective-permute-done((bf16[2,128,512]{2,1,0:T(8,128)(2,1)S(1)}, bf16[2,128,512]{2,1,0:T(8,128)(2,1)S(1)}, u32[]{:S(2)}, u32[]{:S(2)}) %collective-permute-start.3) | collective-permute-done | bytes 262176 | tf_op jit(solution)/shard_map/ppermute | solution.py:241
  95.8 2.2 %statistics.1 = (f32[2,128,512]{2,1,0:T(8,128)}, f32[2,128,512]{2,1,0:T(8,128)}) custom-call(s32[2]{0:T(128)S(1)} %pad_add_fusion.info_ref, bf16[512,512]{1,0:T(8,128)(2,1)S(1)} %get-tuple-element.44.block, bf16[2,128,512]{2,1,0:T(8,128)(2,1)S(1)} %collective-permute-done.3.grams_ref, f32[2,128,512]{2,1,0:T(8,128)S(1)} %copy-done.2, f32[2,128,512]{2,1,0:T(8,128)S(1)} %copy-done.3), custom_call_target="tpu_custom_call" | custom-call | flops 1 | bytes 1 | tf_op jit(solution)/shard_map/statistics/pallas_call | solution.py:369
  97.9 3.2 %all-to-all-done.4 = bf16[16,64,128]{2,1,0:T(8,128)(2,1)S(1)} async-done(((bf16[16,64,128]{2,1,0:T(8,128)(2,1)}), bf16[16,64,128]{2,1,0:T(8,128)(2,1)S(1)}, u32[]{:S(2)}, u32[]{:S(2)}) %all-to-all-start.4) | async-done | bytes 262176 | tf_op jit(solution)/shard_map/all_to_all | solution.py:245
  101.1 1.3 %take_cells.1 = bf16[128,4,128]{2,1,0:T(4,128)(2,1)} custom-call(s32[128]{0:T(128)S(1)} %get-tuple-element.49.cell_ref, bf16[256,4,128]{2,1,0:T(4,128)(2,1)S(1)} %bitcast.16), custom_call_target="tpu_custom_call" | custom-call | tf_op jit(solution)/shard_map/take_cells/pallas_call | solution.py:387
  (6 shorter events, 0.0 us)
Async XLA Ops:
  2.5 7.2 %copy-start = (bf16[2,128,512]{2,1,0:T(8,128)(2,1)S(1)}, bf16[2,128,512]{2,1,0:T(8,128)(2,1)}, u32[]{:S(2)}) copy-start(bf16[2,128,512]{2,1,0:T(8,128)(2,1)} %own_left_ref) | copy-start | bytes 786436
  2.5 7.2 %copy-start.1 = (bf16[2,128,512]{2,1,0:T(8,128)(2,1)S(1)}, bf16[2,128,512]{2,1,0:T(8,128)(2,1)}, u32[]{:S(2)}) copy-start(bf16[2,128,512]{2,1,0:T(8,128)(2,1)} %own_right_ref) | copy-start | bytes 786436
  2.5 11.5 %all-to-all-start = ((bf16[4,128,4,128]{3,2,1,0:T(4,128)(2,1)}), bf16[4,128,4,128]{3,2,1,0:T(4,128)(2,1)S(1)}, u32[]{:S(2)}, u32[]{:S(2)}) async-start(bf16[4,128,4,128]{3,2,1,0:T(4,128)(2,1)} %split_columns.1), calls=%async_computation | async-start | bytes 1048576 | tf_op jit(solution)/shard_map/all_to_all | solution.py:245
  9.8 7.2 %collective-permute-start = (bf16[2,128,128]{2,1,0:T(8,128)(2,1)S(1)}, bf16[2,128,128]{2,1,0:T(8,128)(2,1)S(1)}, u32[]{:S(2)}, u32[]{:S(2)}) collective-permute-start(bf16[2,128,128]{2,1,0:T(8,128)(2,1)S(1)} %get-tuple-element.30), channel_id=1, source_target_pairs={{0,256},{128,384},{256,0},{384,128},{1,257},{129,385},{257,1},{385... | collective-permute-start | bytes 196616 | tf_op jit(solution)/shard_map/ppermute | solution.py:241
  11.7 0.7 copy-start.4
  17.0 27.9 %all-to-all-start.1 = ((bf16[16,64,128]{2,1,0:T(8,128)(2,1)}), bf16[16,64,128]{2,1,0:T(8,128)(2,1)S(1)}, u32[]{:S(2)}, u32[]{:S(2)}) async-start(bf16[16,64,128]{2,1,0:T(8,128)(2,1)} %bitcast.4), calls=%async_computation.1 | async-start | bytes 524288 | tf_op jit(solution)/shard_map/all_to_all | solution.py:245
  33.0 9.6 %collective-permute-start.1 = (bf16[6,128,128]{2,1,0:T(8,128)(2,1)S(1)}, bf16[6,128,128]{2,1,0:T(8,128)(2,1)S(1)}, u32[]{:S(2)}, u32[]{:S(2)}) collective-permute-start(bf16[6,128,128]{2,1,0:T(8,128)(2,1)S(1)} %get-tuple-element.32), channel_id=1, source_target_pairs={{0,128},{128,0},{256,384},{384,256},{1,129},{129,1},{257,385},{385... | collective-permute-start | bytes 589832 | tf_op jit(solution)/shard_map/ppermute | solution.py:241
  35.4 7.2 %collective-permute-start.2 = (bf16[4,128,128]{2,1,0:T(8,128)(2,1)S(1)}, bf16[4,128,128]{2,1,0:T(8,128)(2,1)S(1)}, u32[]{:S(2)}, u32[]{:S(2)}) collective-permute-start(bf16[4,128,128]{2,1,0:T(8,128)(2,1)S(1)} %get-tuple-element.33), channel_id=1, source_target_pairs={{0,384},{128,256},{256,128},{384,0},{1,385},{129,257},{257,129},{3... | collective-permute-start | bytes 393224 | tf_op jit(solution)/shard_map/ppermute | solution.py:241
  75.8 20.0 %copy-start.2 = (f32[2,128,512]{2,1,0:T(8,128)S(1)}, f32[2,128,512]{2,1,0:T(8,128)}, u32[]{:S(2)}) copy-start(f32[2,128,512]{2,1,0:T(8,128)} %left_hbm.1) | copy-start | bytes 1572868
  75.8 20.0 %copy-start.3 = (f32[2,128,512]{2,1,0:T(8,128)S(1)}, f32[2,128,512]{2,1,0:T(8,128)}, u32[]{:S(2)}) copy-start(f32[2,128,512]{2,1,0:T(8,128)} %right_hbm.1) | copy-start | bytes 1572868
  76.6 24.5 %all-to-all-start.4 = ((bf16[16,64,128]{2,1,0:T(8,128)(2,1)}), bf16[16,64,128]{2,1,0:T(8,128)(2,1)S(1)}, u32[]{:S(2)}, u32[]{:S(2)}) async-start(bf16[16,64,128]{2,1,0:T(8,128)(2,1)} %bitcast.10), calls=%async_computation.4 | async-start | bytes 524288 | tf_op jit(solution)/shard_map/all_to_all | solution.py:245
  86.4 9.3 %collective-permute-start.3 = (bf16[2,128,512]{2,1,0:T(8,128)(2,1)S(1)}, bf16[2,128,512]{2,1,0:T(8,128)(2,1)S(1)}, u32[]{:S(2)}, u32[]{:S(2)}) collective-permute-start(bf16[2,128,512]{2,1,0:T(8,128)(2,1)S(1)} %get-tuple-element.45), channel_id=1, source_target_pairs={{0,128},{128,0},{256,384},{384,256},{1,129},{129,1},{257,385},{385... | collective-permute-start | bytes 786440 | tf_op jit(solution)/shard_map/ppermute | solution.py:241
